TPU v7x, 256 devices: a whole 4x4x8 slice. The times are simulated.
256 devices in a mesh: gx: 16 (over y_lo, z), gy: 16 (over x, y_hi, core).
Axes of the slice: x: 4, y: 4 (y_hi: 2, y_lo: 2; y = y_hi * 2 + y_lo), z: 8, core: 2. Of those that a mesh axis runs over, the one named last changes fastest.
Arguments:
- object_field: float32 [2, 4096, 4096], P(None, 'gy', 'gx'), may hold values from -5 to 5
- probe: float32 [3, 2, 256, 256], replicated, may hold values from -5 to 5
- amplitudes: float32 [16, 16, 4, 256, 256], P('gy', 'gx'), may hold values from 0 to 3
- positions: int32 [16, 16, 4, 2], P('gy', 'gx'), may hold values from 0 to 3840, as said below
- counts: int32 [16, 16], replicated, may hold values from 1 to 4, as said below
Outputs:
- new_object: float32 [2, 4096, 4096], P(None, 'gy', 'gx')
- new_probe: float32 [3, 2, 256, 256], replicated
Inputs may be any that keep to these rules, and one draw needn't show every extreme that they name: `positions`: every slot's patch lies inside the object, and its corner lies in the tile (rows a * 256 on, columns b * 256 on) of the slot's own (a, b); dead slots obey this too. Live slots are the first counts[a, b] of a tile; some tile has exactly 4.
All inputs are finite; a program needn't handle non-finite values.
Results may differ from a plain program's by a relative error of at most 0.0001.
Values sent between devices are 32-bit elements; how exact they have to be, the bound alone decides.
No kernel may reach another device: no remote copies, remote signals or barrier semaphores. Data moves between devices by JAX's collectives and lax.ppermute only.
A program may use at most 192 MiB of HBM per device.

v0:
```python
import math

import jax
import jax.numpy as jnp
from jax import lax
from jax.sharding import PartitionSpec as P


def shifted(value, axis, steps):
    count = lax.axis_size(axis)
    leading, last = (max(0, -steps), min(count, count - steps))
    return lax.ppermute(value, axis, [(source, source + steps) for source in range(leading, last)])


def tables(points):
    indices = jnp.arange(points, dtype=jnp.int32)
    phase_index = indices[:, None] * indices[None, :] % points
    angles = phase_index.astype(jnp.float32) * (-2.0 * math.pi / points)
    scale_factor = 1.0 / math.sqrt(points)
    return (jnp.cos(angles) * scale_factor, jnp.sin(angles) * scale_factor)


def apply_left(table_matrix, values):
    return jnp.einsum("jk,mkl->mjl", table_matrix, values, precision=lax.Precision.HIGHEST)


def apply_right(values, table_matrix):
    return jnp.einsum("mjk,kl->mjl", values, table_matrix, precision=lax.Precision.HIGHEST)


def transform(real_part, imag_part, cos_table, sin_table):
    mid_real = apply_left(cos_table, real_part) - apply_left(sin_table, imag_part)
    mid_imag = apply_left(cos_table, imag_part) + apply_left(sin_table, real_part)
    out_real = apply_right(mid_real, cos_table) - apply_right(mid_imag, sin_table)
    out_imag = apply_right(mid_real, sin_table) + apply_right(mid_imag, cos_table)
    return (out_real, out_imag)


def pattern_terms(patch_block, amplitude, probe, coverage, cos_table, sin_table):
    object_real = patch_block[0][None]
    object_imag = patch_block[1][None]
    probe_real = probe[:, 0]
    probe_imag = probe[:, 1]
    wave_real = probe_real * object_real - probe_imag * object_imag
    wave_imag = probe_real * object_imag + probe_imag * object_real
    far_real, far_imag = transform(wave_real, wave_imag, cos_table, sin_table)
    intensity = jnp.sum(far_real * far_real + far_imag * far_imag, axis=0)
    factor = (amplitude / jnp.maximum(jnp.sqrt(intensity), 0.5))[None]
    back_real, back_imag = transform(far_real * factor, far_imag * factor, cos_table, -sin_table)
    diff_real = wave_real - back_real
    diff_imag = wave_imag - back_imag
    grad_real = jnp.sum(probe_real * diff_real + probe_imag * diff_imag, axis=0)
    grad_imag = jnp.sum(probe_real * diff_imag - probe_imag * diff_real, axis=0)
    patch_piece = jnp.stack([grad_real, grad_imag, coverage], 0)
    probe_part = jnp.stack(
        [
            object_real * diff_real + object_imag * diff_imag,
            object_real * diff_imag - object_imag * diff_real,
        ],
        1,
    )
    density = patch_block[0] * patch_block[0] + patch_block[1] * patch_block[1]
    return (patch_piece, probe_part, density)


def shards(object_field, probe, amplitudes, positions, counts):
    tile_rows = object_field.shape[1]
    tile_cols = object_field.shape[2]
    patch_size = probe.shape[-1]
    row_id = lax.axis_index("gy")
    col_id = lax.axis_index("gx")
    cos_table, sin_table = tables(patch_size)
    coverage = jnp.sum(probe * probe, axis=(0, 1))
    zero_index = jnp.int32(0)
    right_strip = shifted(object_field, "gx", -1)
    lower_strip = shifted(object_field, "gy", -1)
    diagonal = shifted(lower_strip, "gx", -1)
    extended = jnp.concatenate(
        [
            jnp.concatenate([object_field, right_strip], 2),
            jnp.concatenate([lower_strip, diagonal], 2),
        ],
        1,
    )
    anchor = jnp.stack([row_id * tile_rows, col_id * tile_cols])
    local_corner = positions[0, 0] - anchor[None, :]
    own_count = counts[row_id, col_id]
    accumulated = jnp.zeros((3, tile_rows + patch_size, tile_cols + patch_size), jnp.float32)
    probe_sum = jnp.zeros_like(probe)
    density_sum = jnp.zeros((patch_size, patch_size), jnp.float32)

    def deposit(target, patch_piece, item):
        row_at = local_corner[item, 0]
        col_at = local_corner[item, 1]
        current = lax.dynamic_slice(
            target, (zero_index, row_at, col_at), (3, patch_size, patch_size)
        )
        return lax.dynamic_update_slice(target, current + patch_piece, (zero_index, row_at, col_at))

    def cut_patch(row_at, col_at):
        return lax.dynamic_slice(
            extended, (zero_index, row_at, col_at), (2, patch_size, patch_size)
        )

    def visit_own(item, carry):
        target, probe_sum, density_sum = carry
        patch_block = cut_patch(local_corner[item, 0], local_corner[item, 1])
        patch_piece, probe_part, density = pattern_terms(
            patch_block, amplitudes[0, 0, item], probe, coverage, cos_table, sin_table
        )
        return (deposit(target, patch_piece, item), probe_sum + probe_part, density_sum + density)

    accumulated, probe_sum, density_sum = lax.fori_loop(
        0, own_count, visit_own, (accumulated, probe_sum, density_sum)
    )
    from_left = shifted(accumulated[:, :tile_rows, tile_cols:], "gx", 1)
    from_above = shifted(accumulated[:, tile_rows:, :tile_cols], "gy", 1)
    diagonal_step = shifted(accumulated[:, tile_rows:, tile_cols:], "gx", 1)
    from_diagonal = shifted(diagonal_step, "gy", 1)
    core_sum = accumulated[:, :tile_rows, :tile_cols]
    core_sum = core_sum.at[:, :, :patch_size].add(from_left)
    core_sum = core_sum.at[:, :patch_size, :].add(from_above)
    core_sum = core_sum.at[:, :patch_size, :patch_size].add(from_diagonal)
    new_object = object_field - core_sum[:2] / (core_sum[2] + 1.0)[None]
    grad_total, density_total = lax.psum((probe_sum, density_sum), ("gx", "gy"))
    new_probe = probe - grad_total / (density_total + 1.0)[None, None]
    return (new_object, new_probe)


def solution(mesh):
    in_specs = (
        P(None, "gy", "gx"),
        P(),
        P("gy", "gx", None, None, None),
        P("gy", "gx", None, None),
        P(),
    )
    out_specs = (P(None, "gy", "gx"), P())
    return jax.shard_map(shards, mesh=mesh, in_specs=in_specs, out_specs=out_specs, check_vma=False)
```

profile of v0, /device:TPU:1, one launch (start us, length us, event | category | flops | bytes accessed | tf_op | source)
XLA Modules:
  0.0 603.3 jit_solution(305272916393551970)
XLA Ops:
  7.2 5.2 collective-permute-start.1
  13.7 6.9 %collective-permute-done.1 = f32[2,256,256]{2,1,0:T(8,128)} collective-permute-done((f32[2,256,256]{2,1,0:T(8,128)}, f32[2,256,256]{2,1,0:T(8,128)}, u32[]{:S(2)}, u32[]{:S(2)}) %collective-permute-start.1) | collective-permute-done | bytes 524320 | tf_op jit(solution)/shard_map/ppermute | solution.py:12
  25.2 3.3 collective-permute-done
  28.5 10.9 %collective-permute-done.2 = f32[2,256,256]{2,1,0:T(8,128)} collective-permute-done((f32[2,256,256]{2,1,0:T(8,128)}, f32[2,256,256]{2,1,0:T(8,128)}, u32[]{:S(2)}, u32[]{:S(2)}) %collective-permute-start.2) | collective-permute-done | bytes 524320 | tf_op jit(solution)/shard_map/ppermute | solution.py:12
  39.4 2.9 maximum_maximum_fusion
  45.7 180.5 %while.23 = (s32[]{:T(128)}, f32[3,512,512]{2,1,0:T(8,128)}, f32[3,2,256,256]{3,2,0,1:T(8,128)}, f32[256,256]{1,0:T(8,128)S(1)}, s32[]{:T(128)}, /*index=5*/s32[...) while((s32[]{:T(128)}, f32[3,512,512]{2,1,0:T(8,128)}, ...), condition=%wide.region_5.6_spmd.clone.clone, body=%wide.region_1.5_spmd.clone.clone.sunk | while | flops 9688711168 | bytes 54001972 | solution.py:113
  64.0 2.9 fusion.236
  88.6 2.9 add_bitcast_fusion.2
  95.9 8.8 %dynamic_update_slice.7 = f32[3,512,512]{2,1,0:T(8,128)} dynamic-update-slice(f32[3,512,512]{2,1,0:T(8,128)} %get-tuple-element.449, f32[3,256,256]{2,1,0:T(8,128)S(1)} %maximum_add_fusion.4, s32[]{:T(128)} %constant.142.clone.1..sunk, s32[]{:T(128)S(6)} %select_n.181, s32[]{:T(128)S(6)} %select_n.182) | dynamic-update-slice | bytes 1572868 | tf_op jit(solution)/shard_map/while/body/dynamic_update_slice | solution.py:98
  147.4 3.1 add_bitcast_fusion.2
  152.1 2.8 maximum_add_fusion.5
  154.9 9.1 %dynamic_update_slice.7 = f32[3,512,512]{2,1,0:T(8,128)} dynamic-update-slice(f32[3,512,512]{2,1,0:T(8,128)} %get-tuple-element.449, f32[3,256,256]{2,1,0:T(8,128)S(1)} %maximum_add_fusion.4, s32[]{:T(128)} %constant.142.clone.1..sunk, s32[]{:T(128)S(6)} %select_n.181, s32[]{:T(128)S(6)} %select_n.182) | dynamic-update-slice | bytes 1572868 | tf_op jit(solution)/shard_map/while/body/dynamic_update_slice | solution.py:98
  206.6 2.9 add_bitcast_fusion.2
  211.1 2.8 maximum_add_fusion.5
  213.9 8.9 %dynamic_update_slice.7 = f32[3,512,512]{2,1,0:T(8,128)} dynamic-update-slice(f32[3,512,512]{2,1,0:T(8,128)} %get-tuple-element.449, f32[3,256,256]{2,1,0:T(8,128)S(1)} %maximum_add_fusion.4, s32[]{:T(128)} %constant.142.clone.1..sunk, s32[]{:T(128)S(6)} %select_n.181, s32[]{:T(128)S(6)} %select_n.182) | dynamic-update-slice | bytes 1572868 | tf_op jit(solution)/shard_map/while/body/dynamic_update_slice | solution.py:98
  226.3 2.9 fusion.142
  229.2 61.1 %collective-permute-start.5 = (f32[3,256,256]{2,1,0:T(8,128)}, f32[3,256,256]{2,1,0:T(8,128)}, u32[]{:S(2)}, u32[]{:S(2)}) collective-permute-start(f32[3,256,256]{2,1,0:T(8,128)} %get-tuple-element.343), channel_id=1, source_target_pairs={{0,16},{16,32},{32,48},{48,64},{64,80},{80,96},{96,112},{112,128},... | collective-permute-start | bytes 2359304 | tf_op jit(solution)/shard_map/ppermute | solution.py:12
  290.3 2.8 copy.24
  293.1 3.3 collective-permute-start.3
  296.4 5.2 collective-permute-start.4
  301.6 4.2 collective-permute-done.5
  305.8 7.9 %collective-permute-start.6 = (f32[3,256,256]{2,1,0:T(8,128)}, f32[3,256,256]{2,1,0:T(8,128)}, u32[]{:S(2)}, u32[]{:S(2)}) collective-permute-start(f32[3,256,256]{2,1,0:T(8,128)} %collective-permute-done.5), channel_id=1, source_target_pairs={{0,1},{1,2},{2,3},{3,4},{4,5},{5,6},{6,7},{7,8},{8,9},{9,10},{10,1... | collective-permute-start | bytes 2359304 | tf_op jit(solution)/shard_map/ppermute | solution.py:12
  313.8 275.6 %all-reduce.3.cloned.1.call-done = (f32[3,2,256,256]{3,2,1,0:T(8,128)}, f32[256,256]{1,0:T(8,128)}) async-done(((f32[3,2,256,256]{3,2,1,0:T(8,128)}, f32[256,256]{1,0:T(8,128)}), (f32[3,2,256,256]{3,2,1,0:T(8,128)}, f32[256,256]{1,0:T(8,128)})) %all-reduce.3.cloned.1.call-update) | async-done | bytes 1835024 | tf_op jit(solution)/shard_map/psum | solution.py:125
  590.3 2.8 divide_subtract_fusion
  (91 shorter events, 131.3 us)
Async XLA Ops:
  7.2 582.2 %all-reduce.3.cloned.1.call-start = ((), (), s32[]{:S(2)}) async-start(), calls=%async_computation | async-start | bytes 3670016 | tf_op jit(solution)/shard_map/psum | solution.py:125
  7.2 13.4 %collective-permute-start.1 = (f32[2,256,256]{2,1,0:T(8,128)}, f32[2,256,256]{2,1,0:T(8,128)}, u32[]{:S(2)}, u32[]{:S(2)}) collective-permute-start(f32[2,256,256]{2,1,0:T(8,128)} %param.19), channel_id=1, source_target_pairs={{1,0},{2,1},{3,2},{4,3},{5,4},{6,5},{7,6},{8,7},{9,8},{10,9},{11,1... | collective-permute-start | bytes 1572872 | tf_op jit(solution)/shard_map/ppermute | solution.py:12
  12.4 16.2 %collective-permute-start = (f32[2,256,256]{2,1,0:T(8,128)}, f32[2,256,256]{2,1,0:T(8,128)}, u32[]{:S(2)}, u32[]{:S(2)}) collective-permute-start(f32[2,256,256]{2,1,0:T(8,128)} %param.19), channel_id=1, source_target_pairs={{16,0},{32,16},{48,32},{64,48},{80,64},{96,80},{112,96},{128,112},... | collective-permute-start | bytes 1572872 | tf_op jit(solution)/shard_map/ppermute | solution.py:12
  20.6 18.8 %collective-permute-start.2 = (f32[2,256,256]{2,1,0:T(8,128)}, f32[2,256,256]{2,1,0:T(8,128)}, u32[]{:S(2)}, u32[]{:S(2)}) collective-permute-start(f32[2,256,256]{2,1,0:T(8,128)} %collective-permute-done.1), channel_id=1, source_target_pairs={{16,0},{32,16},{48,32},{64,48},{80,64},{96,80},{112,96},{128,112},... | collective-permute-start | bytes 1572872 | tf_op jit(solution)/shard_map/ppermute | solution.py:12
  21.9 3.1 copy-start
  23.5 1.6 copy-start.5
  23.5 15.9 %copy-start.3 = (f32[2,256,256]{2,1,0:T(8,128)S(1)}, f32[2,256,256]{2,1,0:T(8,128)}, u32[]{:S(2)}) copy-start(f32[2,256,256]{2,1,0:T(8,128)} %param.19) | copy-start | bytes 1572868
  226.2 3.0 copy-start.2
  229.2 76.6 %collective-permute-start.5 = (f32[3,256,256]{2,1,0:T(8,128)}, f32[3,256,256]{2,1,0:T(8,128)}, u32[]{:S(2)}, u32[]{:S(2)}) collective-permute-start(f32[3,256,256]{2,1,0:T(8,128)} %get-tuple-element.343), channel_id=1, source_target_pairs={{0,16},{16,32},{32,48},{48,64},{64,80},{80,96},{96,112},{112,128},... | collective-permute-start | bytes 2359304 | tf_op jit(solution)/shard_map/ppermute | solution.py:12
  293.1 297.2 %copy-start.1 = (f32[3,2,256,256]{3,2,1,0:T(8,128)S(1)}, f32[3,2,256,256]{3,2,1,0:T(8,128)}, u32[]{:S(2)}) copy-start(f32[3,2,256,256]{3,2,1,0:T(8,128)} %param.20) | copy-start | bytes 4718596
  293.1 300.0 %collective-permute-start.3 = (f32[3,256,256]{2,1,0:T(8,128)S(1)}, f32[3,256,256]{2,1,0:T(8,128)}, u32[]{:S(2)}, u32[]{:S(2)}) collective-permute-start(f32[3,256,256]{2,1,0:T(8,128)S(1)} %get-tuple-element.342), channel_id=1, source_target_pairs={{0,16},{16,32},{32,48},{48,64},{64,80},{80,96},{96,112},{112,128},... | collective-permute-start | bytes 2359304 | tf_op jit(solution)/shard_map/ppermute | solution.py:12
  296.4 296.7 %collective-permute-start.4 = (f32[3,256,256]{2,1,0:T(8,128)S(1)}, f32[3,256,256]{2,1,0:T(8,128)}, u32[]{:S(2)}, u32[]{:S(2)}) collective-permute-start(f32[3,256,256]{2,1,0:T(8,128)S(1)} %get-tuple-element.344), channel_id=1, source_target_pairs={{0,1},{1,2},{2,3},{3,4},{4,5},{5,6},{6,7},{7,8},{8,9},{9,10},{10,1... | collective-permute-start | bytes 2359304 | tf_op jit(solution)/shard_map/ppermute | solution.py:12
  305.8 287.3 %collective-permute-start.6 = (f32[3,256,256]{2,1,0:T(8,128)}, f32[3,256,256]{2,1,0:T(8,128)}, u32[]{:S(2)}, u32[]{:S(2)}) collective-permute-start(f32[3,256,256]{2,1,0:T(8,128)} %collective-permute-done.5), channel_id=1, source_target_pairs={{0,1},{1,2},{2,3},{3,4},{4,5},{5,6},{6,7},{7,8},{8,9},{9,10},{10,1... | collective-permute-start | bytes 2359304 | tf_op jit(solution)/shard_map/ppermute | solution.py:12
  593.1 2.2 copy-start.4
Sparse Core Ops, SparseCore 0:
  293.3 296.0 all-reduce.2
where the time goes:
time: 608 us; the launch traced here: 603 us
  waiting for transfers between devices  301 us (50%)
  matrix products  113 us (19%)
  starting transfers between devices  85.3 us (14%)
  local copies, waits for them, and re-layouts  40.9 us (7%)
  other arithmetic  31 us (5%)
  loops' own time  18.2 us (3%)
  between operations  14.5 us (2%)
    psum x1, waiting for transfers between devices, shards(): grad_total, density_total = lax.psum((probe_sum, density_sum), ('gx', 'gy'))  276 us
    ppermute x7, starting transfers between devices, shifted(): lax.ppermute(value, axis, [(source, source + steps) for source in range(l...  85.2 us
    dot_general x24, matrix products, apply_right(): jnp.einsum('mjk,kl->mjl', values, table_matrix, precision=lax.Precision.H...  57.5 us
    dot_general x24, matrix products, apply_left(): jnp.einsum('jk,mkl->mjl', table_matrix, values, precision=lax.Precision.H...  55 us
    dynamic_update_slice x3, local copies, waits for them, and re-layouts, deposit(): lax.dynamic_update_slice(target, current + patch_piece, (zero_index, row_...  26.9 us
    ppermute x7, waiting for transfers between devices, shifted(): lax.ppermute(value, axis, [(source, source + steps) for source in range(l...  25.4 us
    another operation x1, loops' own time, shards(): lax.fori_loop(0, own_count, visit_own, (accumulated, probe_sum, density_s...  18.2 us
  transfers between devices with their start and end apart: 8, of which 5 were waited for; matrix products, arithmetic and copies ran while one was open for 2% of the time, Pallas kernels for 0%

commit v1 on v0

v1 whole, which is shorter than its diff:
```python
import math

import jax
import jax.numpy as jnp
import numpy as np
from jax import lax
from jax.experimental import pallas as pl
from jax.experimental.pallas import tpu as pltpu
from jax.sharding import PartitionSpec as P

SIDE = 256
HALF = 128
MODES = 3
SLOTS = 4
PLANES = 2 * MODES + 1
AXES = ("gx", "gy")
VMEM = pltpu.VMEM
SMEM = pltpu.SMEM
F32 = jnp.float32
BF16 = jnp.bfloat16


def flat_index(x, y, z, core):
    return ((y % 2) * 8 + z) * 16 + x * 4 + (y // 2) * 2 + core


def routes(move):
    pairs = []
    for x in range(4):
        for y in range(4):
            for z in range(8):
                for core in range(2):
                    tx, ty, tz, tc = move(x, y, z, core)
                    pairs.append((flat_index(x, y, z, core), flat_index(tx % 4, ty % 4, tz % 8, tc % 2)))
    return pairs


def first_ring(step):
    return routes(lambda x, y, z, c: (x + step, y, z, c) if c == 0 else (x, y + step, z, c))


def second_ring(step):
    return routes(lambda x, y, z, c: (x, y + step, z, c) if c == 0 else (x + step, y, z, c))


def depth_ring(step):
    return routes(lambda x, y, z, c: (x, y, z + step, c))


def depth_pair():
    return routes(lambda x, y, z, c: (x, y, z ^ 1, c))


def core_pair():
    return routes(lambda x, y, z, c: (x, y, z, 1 - c))


def send(value, pairs):
    return lax.ppermute(value, AXES, pairs)


def shifted(value, axis, steps):
    count = lax.axis_size(axis)
    leading, last = (max(0, -steps), min(count, count - steps))
    return lax.ppermute(value, axis, [(source, source + steps) for source in range(leading, last)])


def split_table(matrix):
    high = matrix.astype(np.float32).astype(jnp.bfloat16)
    low = (matrix - high.astype(np.float64)).astype(jnp.bfloat16)
    return high, low


def transform_tables():
    n = np.arange(HALF)[:, None].astype(np.int64)
    k = np.arange(HALF)[None, :].astype(np.int64)
    tables = []
    for odd in (0, 1):
        angle = (n * (2 * k + odd) % SIDE) * (-2.0 * math.pi / SIDE)
        cos, sin = np.cos(angle) / 16.0, np.sin(angle) / 16.0
        right = np.block([[cos, sin], [-sin, cos]])
        for matrix in (right, right.T):
            tables.extend(split_table(matrix))
    return np.stack(tables)


def order_table():
    table = np.zeros((SIDE, SIDE), np.float32)
    order = np.concatenate([np.arange(0, SIDE, 2), np.arange(1, SIDE, 2)])
    table[order, np.arange(SIDE)] = 1.0
    return table.astype(jnp.bfloat16)


def split(value):
    high = value.astype(BF16)
    low = (value - high.astype(F32)).astype(BF16)
    return high, low


def dot(left, right):
    return jnp.dot(left, right, preferred_element_type=F32)


def apply_right(value, table, which):
    high, low = split(value)
    return dot(low, table[which]) + dot(high, table[which + 1]) + dot(high, table[which])


def apply_left(table, which, value):
    high, low = split(value)
    return dot(table[which], low) + dot(table[which + 1], high) + dot(table[which], high)


def lanes(*parts):
    return jnp.concatenate(parts, axis=1)


def rows(*parts):
    return jnp.concatenate(parts, axis=0)


def prepare_kernel(place, counts, own, left, above, corner, probe, amplitude, order, amp_out, weight_out, doubled, measured, sems):
    loads = [
        pltpu.make_async_copy(
            amplitude.at[:, :, pl.ds(block * HALF, HALF)], measured.at[:, block], sems.at[block]
        )
        for block in range(2)
    ]
    for load in loads:
        load.start()
    for load in loads:
        load.wait()
    for item in range(SLOTS):
        sorted_rows = lanes(
            *[
                rows(*[measured[item, block, pl.ds(odd, HALF, stride=2), :] for odd in range(2)])
                for block in range(2)
            ]
        )
        high, rest = split(sorted_rows)
        rest32 = sorted_rows - high.astype(F32)
        middle, low = split(rest32)
        amp_out[item] = dot(high, order[...]) + (dot(middle, order[...]) + dot(low, order[...]))
    coverage = probe[0, 0] * probe[0, 0]
    for mode in range(MODES):
        for part in range(2):
            if mode or part:
                coverage = coverage + probe[mode, part] * probe[mode, part]
    for block in range(2):
        for start in (0, SIDE):
            doubled[block, pl.ds(start, SIDE), :] = coverage[:, block * HALF : (block + 1) * HALF]
    row_id = place[0]
    col_id = place[1]
    row_iota = lax.broadcasted_iota(jnp.int32, (SIDE, SIDE), 0)
    lane_iota = lax.broadcasted_iota(jnp.int32, (SIDE, SIDE), 1)
    weight_out[...] = jnp.ones((SIDE, SIDE), F32)
    for up, back, points in ((0, 0, own), (0, 1, left), (1, 0, above), (1, 1, corner)):
        tile_row = row_id - up
        tile_col = col_id - back
        inside = jnp.logical_and(tile_row >= 0, tile_col >= 0)
        count = jnp.where(inside, counts[jnp.maximum(tile_row, 0), jnp.maximum(tile_col, 0)], 0)

        def visit(item, carry, points=points, tile_row=tile_row, tile_col=tile_col, up=up, back=back):
            row_at = points[item, 0] - tile_row * SIDE
            col_at = points[item, 1] - tile_col * SIDE
            window = pl.ds(SIDE - row_at, SIDE)
            moved = pltpu.roll(lanes(doubled[0, window, :], doubled[1, window, :]), col_at, 1)
            row_ok = row_iota < row_at if up else row_iota >= row_at
            col_ok = lane_iota < col_at if back else lane_iota >= col_at
            weight_out[...] += jnp.where(jnp.logical_and(row_ok, col_ok), moved, 0.0)
            return carry

        lax.fori_loop(0, count, visit, 0)


def prepare(place, counts, own, left, above, corner, probe, amplitude, order):
    return pl.pallas_call(
        prepare_kernel,
        out_shape=(
            jax.ShapeDtypeStruct((SLOTS, SIDE, SIDE), F32),
            jax.ShapeDtypeStruct((SIDE, SIDE), F32),
        ),
        in_specs=[pl.BlockSpec(memory_space=SMEM)] * 6
        + [pl.BlockSpec(memory_space=VMEM), pl.BlockSpec(memory_space=pl.ANY), pl.BlockSpec(memory_space=VMEM)],
        out_specs=(pl.BlockSpec(memory_space=VMEM),) * 2,
        scratch_shapes=[
            VMEM((2, 2 * SIDE, HALF), F32),
            VMEM((SLOTS, 2, SIDE, HALF), F32),
            pltpu.SemaphoreType.DMA((2,)),
        ],
        compiler_params=pltpu.CompilerParams(vmem_limit_bytes=32 * 1024 * 1024),
        cost_estimate=pl.CostEstimate(flops=2_000_000_000, bytes_accessed=4_000_000, transcendentals=0),
        name="prepare",
    )(place, counts, own, left, above, corner, probe, amplitude, order)


def pattern_kernel(
    place, counts, points, own, right, lower, corner, probe, amplitude, table,
    core_out, right_out, lower_out, corner_out, send_out, keep_out,
    field, target, total, spectrum, sems,
):
    row_id = place[0]
    col_id = place[1]
    core = place[2]
    loads = []
    for piece, up, back in ((own, 0, 0), (right, 0, 1), (lower, 1, 0), (corner, 1, 1)):
        for block in range(2):
            loads.append(
                pltpu.make_async_copy(
                    piece.at[:, :, pl.ds(block * HALF, HALF)],
                    field.at[:, 2 * back + block, pl.ds(up * SIDE, SIDE), :],
                    sems.at[len(loads)],
                )
            )
    for load in loads:
        load.start()
    target[...] = jnp.zeros_like(target)
    total[...] = jnp.zeros_like(total)
    for load in loads:
        load.wait()
    lane_iota = lax.broadcasted_iota(jnp.int32, (SIDE, SIDE), 1)

    def visit(item, carry):
        row_at = points[item, 0] - row_id * SIDE
        col_at = points[item, 1] - col_id * SIDE
        in_left = lane_iota >= col_at
        rest = jnp.where(col_at == 0, 0, SIDE - col_at)

        def cut(part):
            window = pl.ds(row_at, SIDE)
            first = lanes(field[part, 0, window, :], field[part, 1, window, :])
            second = lanes(field[part, 2, window, :], field[part, 3, window, :])
            return pltpu.roll(jnp.where(in_left, first, second), rest, 1)

        object_real = cut(0)
        object_imag = cut(1)
        density = object_real * object_real + object_imag * object_imag
        total[:, PLANES - 1] += density.reshape(32, 8, SIDE)

        even_sum = jnp.zeros((HALF, SIDE), F32)
        odd_sum = jnp.zeros((HALF, SIDE), F32)
        for mode in range(MODES):
            probe_real = probe[mode, 0]
            probe_imag = probe[mode, 1]
            real = probe_real * object_real - probe_imag * object_imag
            imag = probe_real * object_imag + probe_imag * object_real
            even = apply_right(
                lanes(real[:, :HALF] + real[:, HALF:], imag[:, :HALF] + imag[:, HALF:]), table, 0
            )
            odd = apply_right(
                lanes(real[:, :HALF] - real[:, HALF:], imag[:, :HALF] - imag[:, HALF:]), table, 4
            )
            real = lanes(even[:, :HALF], odd[:, :HALF])
            imag = lanes(even[:, HALF:], odd[:, HALF:])
            even = apply_left(table, 2, rows(real[:HALF] + real[HALF:], imag[:HALF] + imag[HALF:]))
            odd = apply_left(table, 6, rows(real[:HALF] - real[HALF:], imag[:HALF] - imag[HALF:]))
            spectrum[mode, 0] = even
            spectrum[mode, 1] = odd
            even_sum += even[:HALF] * even[:HALF] + even[HALF:] * even[HALF:]
            odd_sum += odd[:HALF] * odd[:HALF] + odd[HALF:] * odd[HALF:]
        even_factor = amplitude[item, :HALF] / jnp.maximum(jnp.sqrt(even_sum), 0.5)
        odd_factor = amplitude[item, HALF:] / jnp.maximum(jnp.sqrt(odd_sum), 0.5)
        even_factor = rows(even_factor, even_factor)
        odd_factor = rows(odd_factor, odd_factor)
        grad_real = jnp.zeros((SIDE, SIDE), F32)
        grad_imag = jnp.zeros((SIDE, SIDE), F32)
        for mode in range(MODES):
            even = apply_left(table, 0, spectrum[mode, 0] * even_factor)
            odd = apply_left(table, 4, spectrum[mode, 1] * odd_factor)
            high = even + odd
            low = even - odd
            real = rows(high[:HALF], low[:HALF])
            imag = rows(high[HALF:], low[HALF:])
            even = apply_right(lanes(real[:, :HALF], imag[:, :HALF]), table, 2)
            odd = apply_right(lanes(real[:, HALF:], imag[:, HALF:]), table, 6)
            high = even + odd
            low = even - odd
            real = lanes(high[:, :HALF], low[:, :HALF])
            imag = lanes(high[:, HALF:], low[:, HALF:])
            probe_real = probe[mode, 0]
            probe_imag = probe[mode, 1]
            grad_real += probe_real * real + probe_imag * imag
            grad_imag += probe_real * imag - probe_imag * real
            total[:, 2 * mode] += (object_real * real + object_imag * imag).reshape(32, 8, SIDE)
            total[:, 2 * mode + 1] += (object_real * imag - object_imag * real).reshape(32, 8, SIDE)
        for part, grad in ((0, grad_real), (1, grad_imag)):
            moved = pltpu.roll(grad, col_at, 1)
            first = jnp.where(in_left, moved, 0.0)
            second = jnp.where(in_left, 0.0, moved)
            window = pl.ds(row_at, SIDE)
            for block, piece in enumerate((first[:, :HALF], first[:, HALF:], second[:, :HALF], second[:, HALF:])):
                target[part, block, window, :] += piece
        return carry

    lax.fori_loop(0, counts[row_id, col_id], visit, 0)
    stores = [
        pltpu.make_async_copy(total.at[pl.ds((1 - core) * 16, 16)], send_out, sems.at[0]),
        pltpu.make_async_copy(total.at[pl.ds(core * 16, 16)], keep_out, sems.at[1]),
    ]
    for piece, up, back in ((core_out, 0, 0), (right_out, 0, 1), (lower_out, 1, 0), (corner_out, 1, 1)):
        for block in range(2):
            stores.append(
                pltpu.make_async_copy(
                    target.at[:, 2 * back + block, pl.ds(up * SIDE, SIDE), :],
                    piece.at[:, :, pl.ds(block * HALF, HALF)],
                    sems.at[len(stores)],
                )
            )
    for store in stores:
        store.start()
    for store in stores:
        store.wait()


def visit_patterns(place, counts, points, own, right, lower, corner, probe, amplitude, table):
    tile = jax.ShapeDtypeStruct((2, SIDE, SIDE), F32)
    part = jax.ShapeDtypeStruct((16, PLANES, 8, SIDE), F32)
    return pl.pallas_call(
        pattern_kernel,
        out_shape=(tile, tile, tile, tile, part, part),
        in_specs=[pl.BlockSpec(memory_space=SMEM)] * 3
        + [pl.BlockSpec(memory_space=pl.ANY)] * 4
        + [pl.BlockSpec(memory_space=VMEM)] * 3,
        out_specs=(pl.BlockSpec(memory_space=pl.ANY),) * 6,
        scratch_shapes=[
            VMEM((2, 4, 2 * SIDE, HALF), F32),
            VMEM((2, 4, 2 * SIDE, HALF), F32),
            VMEM((32, PLANES, 8, SIDE), F32),
            VMEM((MODES, 2, SIDE, SIDE), F32),
            pltpu.SemaphoreType.DMA((10,)),
        ],
        compiler_params=pltpu.CompilerParams(vmem_limit_bytes=48 * 1024 * 1024),
        cost_estimate=pl.CostEstimate(flops=10_000_000_000, bytes_accessed=10_000_000, transcendentals=0),
        name="patterns",
    )(place, counts, points, own, right, lower, corner, probe, amplitude, table)


def scatter_kernel(slot, place, *refs):
    pieces, outs = refs[:-4], refs[-4:]
    length = outs[0].shape[0]
    mine = place[slot]
    for step in range(4):
        start = lax.rem(mine + step, 4) * length
        block = pieces[0][pl.ds(start, length)]
        for piece in pieces[1:]:
            block = block + piece[pl.ds(start, length)]
        outs[step][...] = block


def scatter_sum(slot, place, pieces):
    shape = (pieces[0].shape[0] // 4,) + pieces[0].shape[1:]

    def body(*refs):
        scatter_kernel(slot, *refs)

    return pl.pallas_call(
        body,
        out_shape=(jax.ShapeDtypeStruct(shape, F32),) * 4,
        in_specs=[pl.BlockSpec(memory_space=SMEM)] + [pl.BlockSpec(memory_space=VMEM)] * len(pieces),
        out_specs=(pl.BlockSpec(memory_space=VMEM),) * 4,
        compiler_params=pltpu.CompilerParams(vmem_limit_bytes=32 * 1024 * 1024),
        name="scatter_sum",
    )(place, *pieces)


def plain_sum(pieces):
    def body(*refs):
        block = refs[0][...]
        for piece in refs[1:-1]:
            block = block + piece[...]
        refs[-1][...] = block

    return pl.pallas_call(
        body,
        out_shape=jax.ShapeDtypeStruct(pieces[0].shape, F32),
        in_specs=[pl.BlockSpec(memory_space=VMEM)] * len(pieces),
        out_specs=pl.BlockSpec(memory_space=VMEM),
        name="plain_sum",
    )(*pieces)


def update_probe(place, pieces, probe):
    def body(place, *refs):
        probe_ref, out = refs[-2], refs[-1]
        block = refs[0][0]
        for piece in refs[1:-2]:
            block = block + piece[0]
        group = place[2] * 16 + place[3] * 4 + place[4]
        scale = 1.0 / (block[PLANES - 1] + 1.0)
        for plane in range(PLANES - 1):
            out[0, plane] = (probe_ref[plane, group] + block[plane]) * scale

    return pl.pallas_call(
        body,
        out_shape=jax.ShapeDtypeStruct((1, PLANES - 1, 8, SIDE), F32),
        in_specs=[pl.BlockSpec(memory_space=SMEM)] + [pl.BlockSpec(memory_space=VMEM)] * (len(pieces) + 1),
        out_specs=pl.BlockSpec(memory_space=VMEM),
        name="update_probe",
    )(place, *pieces, probe.reshape(PLANES - 1, 32, 8, SIDE))


def gather_parts(slot, place, pieces):
    length = pieces[0].shape[0]

    def body(place, *refs):
        out = refs[-1]
        for step, piece in enumerate(refs[:-1]):
            start = lax.rem(place[slot] + 4 - step, 4) * length
            out[pl.ds(start, length)] = piece[...]

    return pl.pallas_call(
        body,
        out_shape=jax.ShapeDtypeStruct((4 * length,) + pieces[0].shape[1:], F32),
        in_specs=[pl.BlockSpec(memory_space=SMEM)] + [pl.BlockSpec(memory_space=VMEM)] * 4,
        out_specs=pl.BlockSpec(memory_space=VMEM),
        name="gather_parts",
    )(place, *pieces)


def join_halves(place, mine, other):
    def body(place, mine_ref, other_ref, out):
        core = place[2]
        for plane in range(PLANES - 1):
            for piece, start in ((mine_ref, core * 16), (other_ref, 16 - core * 16)):
                out[plane, pl.ds(start, 16)] = piece[:, plane]

    out = pl.pallas_call(
        body,
        out_shape=jax.ShapeDtypeStruct((PLANES - 1, 32, 8, SIDE), F32),
        in_specs=[pl.BlockSpec(memory_space=SMEM)] + [pl.BlockSpec(memory_space=VMEM)] * 2,
        out_specs=pl.BlockSpec(memory_space=VMEM),
        name="join_halves",
    )(place, mine, other)
    return out.reshape(MODES, 2, SIDE, SIDE)


def update_object(own, pieces, weight):
    def body(own_ref, *refs):
        weight_ref, out = refs[-2], refs[-1]
        scale = 1.0 / weight_ref[...]
        for part in range(2):
            block = own_ref[part]
            for piece in refs[:-2]:
                block = block + piece[part]
            out[part] = block * scale

    return pl.pallas_call(
        body,
        out_shape=jax.ShapeDtypeStruct((2, SIDE, SIDE), F32),
        in_specs=[pl.BlockSpec(memory_space=VMEM)] * (len(pieces) + 2),
        out_specs=pl.BlockSpec(memory_space=VMEM),
        compiler_params=pltpu.CompilerParams(vmem_limit_bytes=32 * 1024 * 1024),
        name="update_object",
    )(own, *pieces, weight)


def shards(object_field, probe, amplitudes, positions, counts):
    row_id = lax.axis_index("gy")
    col_id = lax.axis_index("gx")
    core = row_id % 2
    x_at = row_id // 4
    y_at = (row_id // 2) % 2 * 2 + col_id // 8
    first = jnp.where(core == 0, x_at, y_at)
    second = jnp.where(core == 0, y_at, x_at)
    place = jnp.stack([row_id, col_id, core, first, second]).astype(jnp.int32)
    table = jnp.asarray(transform_tables())
    order = jnp.asarray(order_table())

    points = positions[0, 0]
    right_strip = shifted(object_field, "gx", -1)
    lower_strip = shifted(object_field, "gy", -1)
    points_left = shifted(points, "gx", 1)
    points_pair = shifted(jnp.concatenate([points, points_left], 0), "gy", 1)
    diagonal = shifted(right_strip, "gy", -1)
    amplitude, weight = prepare(
        place, counts, points, points_left, points_pair[:SLOTS], points_pair[SLOTS:],
        probe, amplitudes[0, 0], order,
    )
    core_grad, right_grad, lower_grad, corner_grad, other_half, half = visit_patterns(
        place, counts, points, object_field, right_strip, lower_strip, diagonal, probe, amplitude, table
    )

    half_in = send(other_half, core_pair())
    parts = scatter_sum(3, place, [half, half_in])
    arrived = [send(parts[step], first_ring(step)) for step in (1, 2, 3)]
    corner_step = shifted(corner_grad, "gy", 1)
    parts = scatter_sum(4, place, [parts[0]] + arrived)
    arrived = [send(parts[step], second_ring(step)) for step in (1, 2, 3)]
    from_above = shifted(lower_grad, "gy", 1)
    block = plain_sum([parts[0]] + arrived)
    block = plain_sum([block, send(block, depth_pair())])
    chunk = update_probe(place, [block] + [send(block, depth_ring(step)) for step in (2, 4, 6)], probe)
    from_left = shifted(right_grad, "gx", 1)
    from_corner = shifted(corner_step, "gx", 1)
    chunk = gather_parts(4, place, [chunk] + [send(chunk, second_ring(step)) for step in (1, 2, 3)])
    chunk = gather_parts(3, place, [chunk] + [send(chunk, first_ring(step)) for step in (1, 2, 3)])
    new_probe = join_halves(place, chunk, send(chunk, core_pair()))
    new_object = update_object(
        object_field, [core_grad, from_left, from_above, from_corner], weight
    )
    return (new_object, new_probe)


def solution(mesh):
    in_specs = (
        P(None, "gy", "gx"),
        P(),
        P("gy", "gx", None, None, None),
        P("gy", "gx", None, None),
        P(),
    )
    out_specs = (P(None, "gy", "gx"), P())
    return jax.shard_map(shards, mesh=mesh, in_specs=in_specs, out_specs=out_specs, check_vma=False)
```

time: 608 us -> 177 us (0.29)
  waiting for transfers between devices: 301 us -> 51.5 us
  matrix products: 113 us -> 0 us
  Pallas kernels: 0 us -> 37.3 us
  other arithmetic: 31 us -> 0.01 us
  local copies, waits for them, and re-layouts: 40.9 us -> 13 us
  loops' own time: 18.2 us -> 0 us
  between operations: 14.5 us -> 0.93 us
  starting transfers between devices: 85.3 us -> 73.7 us
    psum x1 -> x0, waiting for transfers between devices: 276 us -> none  [shards(): grad_total, density_total = lax.psum((probe_sum, density_sum), ('gx', 'gy'))]
    dot_general x48 -> x0, matrix products: 113 us -> none  [the longest x24 57.5 us: apply_right(): jnp.einsum('mjk,kl->mjl', values, table_matrix, precision=lax.Precision.H...]
    ppermute x7 -> x9, starting transfers between devices: 85.2 us -> 33.2 us  [shifted(): lax.ppermute(value, axis, [(source, source + steps) for source in range(l...]
    ppermute x0 -> x18, starting transfers between devices: none -> 40.5 us  [send(): return lax.ppermute(value, AXES, pairs)]
    pallas_call x0 -> x11, Pallas kernels: none -> 37.3 us  [the longest x1 20.5 us: visit_patterns(): pl.pallas_call(pattern_kernel, out_shape=(tile, tile, tile, tile, part, p...]
    dynamic_update_slice x3 -> x0, local copies, waits for them, and re-layouts: 26.9 us -> none  [deposit(): lax.dynamic_update_slice(target, current + patch_piece, (zero_index, row_...]
    ppermute x0 -> x18, waiting for transfers between devices: none -> 24 us  [send(): return lax.ppermute(value, AXES, pairs)]
    add x11 -> x0, other arithmetic: 20.4 us -> none  [the longest x3 8.28 us: visit_own(): probe_sum + probe_part]
  transfers between devices with their start and end apart: 8 -> 27, of which waited for: 5 -> 15; matrix products, arithmetic and copies ran while one was open for 2% -> 0% of each run, Pallas kernels for 0% -> 6%
where the time goes in v1:
time: 177 us; the launch traced here: 176 us
  starting transfers between devices  73.7 us (42%)
  waiting for transfers between devices  51.5 us (29%)
  Pallas kernels  37.3 us (21%)
  local copies, waits for them, and re-layouts  13 us (7%)
    ppermute x18, starting transfers between devices, send(): return lax.ppermute(value, AXES, pairs)  40.5 us
    ppermute x9, starting transfers between devices, shifted(): lax.ppermute(value, axis, [(source, source + steps) for source in range(l...  33.2 us
    ppermute x9, waiting for transfers between devices, shifted(): lax.ppermute(value, axis, [(source, source + steps) for source in range(l...  27.6 us
    ppermute x18, waiting for transfers between devices, send(): return lax.ppermute(value, AXES, pairs)  24 us
    pallas_call x1, Pallas kernels, visit_patterns(): pl.pallas_call(pattern_kernel, out_shape=(tile, tile, tile, tile, part, p...  20.5 us
    unnamed x50, local copies, waits for them, and re-layouts  12.1 us
    pallas_call x2, Pallas kernels, gather_parts(): pl.pallas_call(body, out_shape=jax.ShapeDtypeStruct((4 * length,) + piece...  3.76 us
  transfers between devices with their start and end apart: 27, of which 15 were waited for; matrix products, arithmetic and copies ran while one was open for 0% of the time, Pallas kernels for 6%

profile of v1, /device:TPU:1, one launch (start us, length us, event | category | flops | bytes accessed | tf_op | source)
XLA Modules:
  0.0 176.5 jit_solution(17540753812657630848)
XLA Ops:
  1.9 5.2 %collective-permute-start.1 = (f32[2,256,256]{2,1,0:T(8,128)}, f32[2,256,256]{2,1,0:T(8,128)S(1)}, u32[]{:S(2)}, u32[]{:S(2)}) collective-permute-start(f32[2,256,256]{2,1,0:T(8,128)} %own_ref.1), channel_id=1, source_target_pairs={{1,0},{2,1},{3,2},{4,3},{5,4},{6,5},{7,6},{8,7},{9,8},{10,9},{11,1... | collective-permute-start | bytes 1572872 | tf_op jit(solution)/shard_map/ppermute | solution.py:65
  7.9 4.3 %collective-permute-start.3 = (s32[4,2]{1,0:T(4,128)S(1)}, s32[4,2]{1,0:T(4,128)S(1)}, u32[]{:S(2)}, u32[]{:S(2)}) collective-permute-start(s32[4,2]{1,0:T(4,128)S(1)} %copy.21.own.points), channel_id=1, source_target_pairs={{0,16},{16,32},{32,48},{48,64},{64,80},{80,96},{96,112},{112,128},... | collective-permute-start | bytes 104 | tf_op jit(solution)/shard_map/ppermute | solution.py:65
  12.2 2.8 %collective-permute-done.right = f32[2,256,256]{2,1,0:T(8,128)S(1)} collective-permute-done((f32[2,256,256]{2,1,0:T(8,128)}, f32[2,256,256]{2,1,0:T(8,128)S(1)}, u32[]{:S(2)}, u32[]{:S(2)}) %collective-permute-start) | collective-permute-done | bytes 524320 | tf_op jit(solution)/shard_map/ppermute | solution.py:65
  14.9 5.0 %collective-permute-start.2 = (f32[2,256,256]{2,1,0:T(8,128)S(1)}, f32[2,256,256]{2,1,0:T(8,128)S(1)}, u32[]{:S(2)}, u32[]{:S(2)}) collective-permute-start(f32[2,256,256]{2,1,0:T(8,128)S(1)} %collective-permute-done.right), channel_id=1, source_target_pairs={{1,0},{2,1},{3,2},{4,3},{5,4},{6,5},{7,6},{8,7},{9,8},{10,9},{11,1... | collective-permute-start | bytes 1572872 | tf_op jit(solution)/shard_map/ppermute | solution.py:65
  20.0 4.7 %collective-permute-start.4 = (s32[8,2]{1,0:T(8,128)S(1)}, s32[8,2]{1,0:T(8,128)S(1)}, u32[]{:S(2)}, u32[]{:S(2)}) collective-permute-start(s32[8,2]{1,0:T(8,128)S(1)} %pad_add_fusion), channel_id=1, source_target_pairs={{0,1},{1,2},{2,3},{3,4},{4,5},{5,6},{6,7},{7,8},{8,9},{9,10},{10,1... | collective-permute-start | bytes 200 | tf_op jit(solution)/shard_map/ppermute | solution.py:65
  29.7 2.9 %prepare.1 = (f32[4,256,256]{2,1,0:T(8,128)S(1)}, f32[256,256]{1,0:T(8,128)S(1)}) custom-call(s32[5]{0:T(128)S(1)} %stack.23.place.refs_0_, s32[16,16]{1,0:T(8,128)S(1)} %copy-done.9, s32[4,2]{1,0:T(4,128)S(1)} %copy.21.own.points, s32[4,2]{1,0:T(4,128)S(1)} %collective-permute-done.3.left, s32[4,2]{1,0:T(4,128)S(1)} %get-tuple-element.35.above, ...), custom_call_target="tpu_custom_call" | custom-call | flops 2000000000 | bytes 4000000 | tf_op jit(solution)/shard_map/prepare/pallas_call | solution.py:177
  37.3 20.5 %patterns.1 = (f32[2,256,256]{2,1,0:T(8,128)S(1)}, f32[2,256,256]{2,1,0:T(8,128)S(1)}, f32[2,256,256]{2,1,0:T(8,128)S(1)}, f32[2,256,256]{2,1,0:T(8,128)S(1)}, f...) custom-call(s32[5]{0:T(128)S(1)} %stack.23.place.refs_0_, s32[16,16]{1,0:T(8,128)S(1)} %copy-done.10, ...), custom_call_target="tpu_custom_call" | custom-call | flops 10000000000 | bytes 10000000 | tf_op jit(solution)/shard_map/patterns/pallas_call | solution.py:318
  61.0 7.3 %collective-permute-start.10 = (f32[4,7,8,256]{3,2,1,0:T(8,128)S(1)}, f32[4,7,8,256]{3,2,1,0:T(8,128)S(1)}, u32[]{:S(2)}, u32[]{:S(2)}) collective-permute-start(f32[4,7,8,256]{3,2,1,0:T(8,128)S(1)} %get-tuple-element.27), channel_id=1, source_target_pairs={{0,4},{1,129},{16,20},{17,145},{32,36},{33,161},{48,52},{49,177},{... | collective-permute-start | bytes 688136 | tf_op jit(solution)/shard_map/ppermute | solution.py:59
  68.3 4.5 %collective-permute-start.11 = (f32[4,7,8,256]{3,2,1,0:T(8,128)S(1)}, f32[4,7,8,256]{3,2,1,0:T(8,128)S(1)}, u32[]{:S(2)}, u32[]{:S(2)}) collective-permute-start(f32[4,7,8,256]{3,2,1,0:T(8,128)S(1)} %get-tuple-element.28), channel_id=1, source_target_pairs={{0,8},{1,3},{16,24},{17,19},{32,40},{33,35},{48,56},{49,51},{64,72... | collective-permute-start | bytes 688136 | tf_op jit(solution)/shard_map/ppermute | solution.py:59
  72.8 2.5 %collective-permute-done.10.refs_2_ = f32[4,7,8,256]{3,2,1,0:T(8,128)S(1)} collective-permute-done((f32[4,7,8,256]{3,2,1,0:T(8,128)S(1)}, f32[4,7,8,256]{3,2,1,0:T(8,128)S(1)}, u32[]{:S(2)}, u32[]{:S(2)}) %collective-permute-start.10) | collective-permute-done | bytes 229408 | tf_op jit(solution)/shard_map/ppermute | solution.py:59
  75.3 3.3 %collective-permute-done.11.refs_3_ = f32[4,7,8,256]{3,2,1,0:T(8,128)S(1)} collective-permute-done((f32[4,7,8,256]{3,2,1,0:T(8,128)S(1)}, f32[4,7,8,256]{3,2,1,0:T(8,128)S(1)}, u32[]{:S(2)}, u32[]{:S(2)}) %collective-permute-start.11) | collective-permute-done | bytes 229408 | tf_op jit(solution)/shard_map/ppermute | solution.py:59
  88.5 3.2 %collective-permute-done.16.refs_1_ = f32[1,7,8,256]{3,2,1,0:T(8,128)S(1)} collective-permute-done((f32[1,7,8,256]{3,2,1,0:T(8,128)}, f32[1,7,8,256]{3,2,1,0:T(8,128)S(1)}, u32[]{:S(2)}, u32[]{:S(2)}) %collective-permute-start.16) | collective-permute-done | bytes 57376 | tf_op jit(solution)/shard_map/ppermute | solution.py:59
  93.9 6.6 %collective-permute-start.19 = (f32[1,7,8,256]{3,2,1,0:T(8,128)}, f32[1,7,8,256]{3,2,1,0:T(8,128)S(1)}, u32[]{:S(2)}, u32[]{:S(2)}) collective-permute-start(f32[1,7,8,256]{3,2,1,0:T(8,128)} %plain_sum.3.refs_0_), channel_id=1, source_target_pairs={{0,96},{1,97},{16,112},{17,113},{32,0},{33,1},{48,16},{49,17},{64,... | collective-permute-start | bytes 172040 | tf_op jit(solution)/shard_map/ppermute | solution.py:59
  102.5 5.3 %collective-permute-start.7 = (f32[2,256,256]{2,1,0:T(8,128)S(1)}, f32[2,256,256]{2,1,0:T(8,128)}, u32[]{:S(2)}, u32[]{:S(2)}) collective-permute-start(f32[2,256,256]{2,1,0:T(8,128)S(1)} %get-tuple-element.22), channel_id=1, source_target_pairs={{0,1},{1,2},{2,3},{3,4},{4,5},{5,6},{6,7},{7,8},{8,9},{9,10},{10,1... | collective-permute-start | bytes 1572872 | tf_op jit(solution)/shard_map/ppermute | solution.py:65
  110.7 3.1 %collective-permute-start.22 = (f32[1,6,8,256]{3,2,1,0:T(8,128)}, f32[1,6,8,256]{3,2,1,0:T(8,128)S(1)}, u32[]{:S(2)}, u32[]{:S(2)}) collective-permute-start(f32[1,6,8,256]{3,2,1,0:T(8,128)} %update_probe.1.refs_0_), channel_id=1, source_target_pairs={{0,130},{1,13},{16,146},{17,29},{32,162},{33,45},{48,178},{49,61},... | collective-permute-start | bytes 147464 | tf_op jit(solution)/shard_map/ppermute | solution.py:59
  115.4 3.1 %collective-permute-done.21.refs_2_ = f32[1,6,8,256]{3,2,1,0:T(8,128)S(1)} collective-permute-done((f32[1,6,8,256]{3,2,1,0:T(8,128)}, f32[1,6,8,256]{3,2,1,0:T(8,128)S(1)}, u32[]{:S(2)}, u32[]{:S(2)}) %collective-permute-start.21) | collective-permute-done | bytes 49184 | tf_op jit(solution)/shard_map/ppermute | solution.py:59
  121.3 3.7 %collective-permute-start.25 = (f32[4,6,8,256]{3,2,1,0:T(8,128)}, f32[4,6,8,256]{3,2,1,0:T(8,128)S(1)}, u32[]{:S(2)}, u32[]{:S(2)}) collective-permute-start(f32[4,6,8,256]{3,2,1,0:T(8,128)} %gather_parts.2.refs_0_), channel_id=1, source_target_pairs={{0,12},{1,131},{16,28},{17,147},{32,44},{33,163},{48,60},{49,179},... | collective-permute-start | bytes 589832 | tf_op jit(solution)/shard_map/ppermute | solution.py:59
  125.5 4.5 %collective-permute-done.25.refs_3_ = f32[4,6,8,256]{3,2,1,0:T(8,128)S(1)} collective-permute-done((f32[4,6,8,256]{3,2,1,0:T(8,128)}, f32[4,6,8,256]{3,2,1,0:T(8,128)S(1)}, u32[]{:S(2)}, u32[]{:S(2)}) %collective-permute-start.25) | collective-permute-done | bytes 196640 | tf_op jit(solution)/shard_map/ppermute | solution.py:59
  135.3 5.9 %collective-permute-start.26 = (f32[16,6,8,256]{3,2,1,0:T(8,128)}, f32[16,6,8,256]{3,2,1,0:T(8,128)}, u32[]{:S(2)}, u32[]{:S(2)}) collective-permute-start(f32[16,6,8,256]{3,2,1,0:T(8,128)} %gather_parts.3.mine_ref), channel_id=1, source_target_pairs={{0,1},{1,0},{16,17},{17,16},{32,33},{33,32},{48,49},{49,48},{64,65... | collective-permute-start | bytes 2359304 | tf_op jit(solution)/shard_map/ppermute | solution.py:59
  141.2 2.8 %collective-permute-start.5 = (f32[2,256,256]{2,1,0:T(8,128)S(1)}, f32[2,256,256]{2,1,0:T(8,128)S(1)}, u32[]{:S(2)}, u32[]{:S(2)}) collective-permute-start(f32[2,256,256]{2,1,0:T(8,128)S(1)} %get-tuple-element.20), channel_id=1, source_target_pairs={{0,16},{16,32},{32,48},{48,64},{64,80},{80,96},{96,112},{112,128},... | collective-permute-start | bytes 1572872 | tf_op jit(solution)/shard_map/ppermute | solution.py:65
  144.0 3.0 %collective-permute-start.6 = (f32[2,256,256]{2,1,0:T(8,128)S(1)}, f32[2,256,256]{2,1,0:T(8,128)S(1)}, u32[]{:S(2)}, u32[]{:S(2)}) collective-permute-start(f32[2,256,256]{2,1,0:T(8,128)S(1)} %get-tuple-element.21), channel_id=1, source_target_pairs={{0,1},{1,2},{2,3},{3,4},{4,5},{5,6},{6,7},{7,8},{8,9},{9,10},{10,1... | collective-permute-start | bytes 1572872 | tf_op jit(solution)/shard_map/ppermute | solution.py:65
  148.7 6.6 %collective-permute-done.5.refs_1_ = f32[2,256,256]{2,1,0:T(8,128)S(1)} collective-permute-done((f32[2,256,256]{2,1,0:T(8,128)S(1)}, f32[2,256,256]{2,1,0:T(8,128)S(1)}, u32[]{:S(2)}, u32[]{:S(2)}) %collective-permute-start.5) | collective-permute-done | bytes 524320 | tf_op jit(solution)/shard_map/ppermute | solution.py:65
  155.3 17.5 %collective-permute-done.6.refs_2_ = f32[2,256,256]{2,1,0:T(8,128)S(1)} collective-permute-done((f32[2,256,256]{2,1,0:T(8,128)S(1)}, f32[2,256,256]{2,1,0:T(8,128)S(1)}, u32[]{:S(2)}, u32[]{:S(2)}) %collective-permute-start.6) | collective-permute-done | bytes 524320 | tf_op jit(solution)/shard_map/ppermute | solution.py:65
  173.8 2.6 %join_halves.1 = f32[6,32,8,256]{3,2,1,0:T(8,128)} custom-call(s32[5]{0:T(128)} %copy-done.3, f32[16,6,8,256]{3,2,1,0:T(8,128)} %gather_parts.3.mine_ref, f32[16,6,8,256]{3,2,1,0:T(8,128)} %collective-permute-done.26.other_ref), custom_call_target="tpu_custom_call" | custom-call | tf_op jit(solution)/shard_map/join_halves/pallas_call | solution.py:427
  (95 shorter events, 44.7 us)
Async XLA Ops:
  0.6 14.3 %collective-permute-start = (f32[2,256,256]{2,1,0:T(8,128)}, f32[2,256,256]{2,1,0:T(8,128)S(1)}, u32[]{:S(2)}, u32[]{:S(2)}) collective-permute-start(f32[2,256,256]{2,1,0:T(8,128)} %own_ref.1), channel_id=1, source_target_pairs={{16,0},{32,16},{48,32},{64,48},{80,64},{96,80},{112,96},{128,112},... | collective-permute-start | bytes 1572872 | tf_op jit(solution)/shard_map/ppermute | solution.py:65
  1.9 31.7 %collective-permute-start.1 = (f32[2,256,256]{2,1,0:T(8,128)}, f32[2,256,256]{2,1,0:T(8,128)S(1)}, u32[]{:S(2)}, u32[]{:S(2)}) collective-permute-start(f32[2,256,256]{2,1,0:T(8,128)} %own_ref.1), channel_id=1, source_target_pairs={{1,0},{2,1},{3,2},{4,3},{5,4},{6,5},{7,6},{8,7},{9,8},{10,9},{11,1... | collective-permute-start | bytes 1572872 | tf_op jit(solution)/shard_map/ppermute | solution.py:65
  7.9 12.1 %collective-permute-start.3 = (s32[4,2]{1,0:T(4,128)S(1)}, s32[4,2]{1,0:T(4,128)S(1)}, u32[]{:S(2)}, u32[]{:S(2)}) collective-permute-start(s32[4,2]{1,0:T(4,128)S(1)} %copy.21.own.points), channel_id=1, source_target_pairs={{0,16},{16,32},{32,48},{48,64},{64,80},{80,96},{96,112},{112,128},... | collective-permute-start | bytes 104 | tf_op jit(solution)/shard_map/ppermute | solution.py:65
  14.9 19.5 %collective-permute-start.2 = (f32[2,256,256]{2,1,0:T(8,128)S(1)}, f32[2,256,256]{2,1,0:T(8,128)S(1)}, u32[]{:S(2)}, u32[]{:S(2)}) collective-permute-start(f32[2,256,256]{2,1,0:T(8,128)S(1)} %collective-permute-done.right), channel_id=1, source_target_pairs={{1,0},{2,1},{3,2},{4,3},{5,4},{6,5},{7,6},{8,7},{9,8},{10,9},{11,1... | collective-permute-start | bytes 1572872 | tf_op jit(solution)/shard_map/ppermute | solution.py:65
  20.0 5.5 %collective-permute-start.4 = (s32[8,2]{1,0:T(8,128)S(1)}, s32[8,2]{1,0:T(8,128)S(1)}, u32[]{:S(2)}, u32[]{:S(2)}) collective-permute-start(s32[8,2]{1,0:T(8,128)S(1)} %pad_add_fusion), channel_id=1, source_target_pairs={{0,1},{1,2},{2,3},{3,4},{4,5},{5,6},{6,7},{7,8},{8,9},{9,10},{10,1... | collective-permute-start | bytes 200 | tf_op jit(solution)/shard_map/ppermute | solution.py:65
  61.0 14.3 %collective-permute-start.10 = (f32[4,7,8,256]{3,2,1,0:T(8,128)S(1)}, f32[4,7,8,256]{3,2,1,0:T(8,128)S(1)}, u32[]{:S(2)}, u32[]{:S(2)}) collective-permute-start(f32[4,7,8,256]{3,2,1,0:T(8,128)S(1)} %get-tuple-element.27), channel_id=1, source_target_pairs={{0,4},{1,129},{16,20},{17,145},{32,36},{33,161},{48,52},{49,177},{... | collective-permute-start | bytes 688136 | tf_op jit(solution)/shard_map/ppermute | solution.py:59
  68.3 10.4 %collective-permute-start.11 = (f32[4,7,8,256]{3,2,1,0:T(8,128)S(1)}, f32[4,7,8,256]{3,2,1,0:T(8,128)S(1)}, u32[]{:S(2)}, u32[]{:S(2)}) collective-permute-start(f32[4,7,8,256]{3,2,1,0:T(8,128)S(1)} %get-tuple-element.28), channel_id=1, source_target_pairs={{0,8},{1,3},{16,24},{17,19},{32,40},{33,35},{48,56},{49,51},{64,72... | collective-permute-start | bytes 688136 | tf_op jit(solution)/shard_map/ppermute | solution.py:59
  72.8 5.9 %collective-permute-start.12 = (f32[4,7,8,256]{3,2,1,0:T(8,128)S(1)}, f32[4,7,8,256]{3,2,1,0:T(8,128)S(1)}, u32[]{:S(2)}, u32[]{:S(2)}) collective-permute-start(f32[4,7,8,256]{3,2,1,0:T(8,128)S(1)} %get-tuple-element.29), channel_id=1, source_target_pairs={{0,12},{1,131},{16,28},{17,147},{32,44},{33,163},{48,60},{49,179},... | collective-permute-start | bytes 688136 | tf_op jit(solution)/shard_map/ppermute | solution.py:59
  79.9 5.2 %collective-permute-start.13 = (f32[1,7,8,256]{3,2,1,0:T(8,128)S(1)}, f32[1,7,8,256]{3,2,1,0:T(8,128)S(1)}, u32[]{:S(2)}, u32[]{:S(2)}) collective-permute-start(f32[1,7,8,256]{3,2,1,0:T(8,128)S(1)} %get-tuple-element.31), channel_id=1, source_target_pairs={{0,128},{1,5},{16,144},{17,21},{32,160},{33,37},{48,176},{49,53},{... | collective-permute-start | bytes 172040 | tf_op jit(solution)/shard_map/ppermute | solution.py:59
  81.4 4.5 %collective-permute-start.14 = (f32[1,7,8,256]{3,2,1,0:T(8,128)S(1)}, f32[1,7,8,256]{3,2,1,0:T(8,128)S(1)}, u32[]{:S(2)}, u32[]{:S(2)}) collective-permute-start(f32[1,7,8,256]{3,2,1,0:T(8,128)S(1)} %get-tuple-element.32), channel_id=1, source_target_pairs={{0,2},{1,9},{16,18},{17,25},{32,34},{33,41},{48,50},{49,57},{64,66... | collective-permute-start | bytes 172040 | tf_op jit(solution)/shard_map/ppermute | solution.py:59
  93.9 14.0 %collective-permute-start.19 = (f32[1,7,8,256]{3,2,1,0:T(8,128)}, f32[1,7,8,256]{3,2,1,0:T(8,128)S(1)}, u32[]{:S(2)}, u32[]{:S(2)}) collective-permute-start(f32[1,7,8,256]{3,2,1,0:T(8,128)} %plain_sum.3.refs_0_), channel_id=1, source_target_pairs={{0,96},{1,97},{16,112},{17,113},{32,0},{33,1},{48,16},{49,17},{64,... | collective-permute-start | bytes 172040 | tf_op jit(solution)/shard_map/ppermute | solution.py:59
  100.4 7.4 %collective-permute-start.18 = (f32[1,7,8,256]{3,2,1,0:T(8,128)}, f32[1,7,8,256]{3,2,1,0:T(8,128)S(1)}, u32[]{:S(2)}, u32[]{:S(2)}) collective-permute-start(f32[1,7,8,256]{3,2,1,0:T(8,128)} %plain_sum.3.refs_0_), channel_id=1, source_target_pairs={{0,64},{1,65},{16,80},{17,81},{32,96},{33,97},{48,112},{49,113},{6... | collective-permute-start | bytes 172040 | tf_op jit(solution)/shard_map/ppermute | solution.py:59
  100.5 7.5 %collective-permute-start.17 = (f32[1,7,8,256]{3,2,1,0:T(8,128)}, f32[1,7,8,256]{3,2,1,0:T(8,128)S(1)}, u32[]{:S(2)}, u32[]{:S(2)}) collective-permute-start(f32[1,7,8,256]{3,2,1,0:T(8,128)} %plain_sum.3.refs_0_), channel_id=1, source_target_pairs={{0,32},{1,33},{16,48},{17,49},{32,64},{33,65},{48,80},{49,81},{64,... | collective-permute-start | bytes 172040 | tf_op jit(solution)/shard_map/ppermute | solution.py:59
  102.5 44.5 %collective-permute-start.7 = (f32[2,256,256]{2,1,0:T(8,128)S(1)}, f32[2,256,256]{2,1,0:T(8,128)}, u32[]{:S(2)}, u32[]{:S(2)}) collective-permute-start(f32[2,256,256]{2,1,0:T(8,128)S(1)} %get-tuple-element.22), channel_id=1, source_target_pairs={{0,1},{1,2},{2,3},{3,4},{4,5},{5,6},{6,7},{7,8},{8,9},{9,10},{10,1... | collective-permute-start | bytes 1572872 | tf_op jit(solution)/shard_map/ppermute | solution.py:65
  110.7 4.6 %collective-permute-start.22 = (f32[1,6,8,256]{3,2,1,0:T(8,128)}, f32[1,6,8,256]{3,2,1,0:T(8,128)S(1)}, u32[]{:S(2)}, u32[]{:S(2)}) collective-permute-start(f32[1,6,8,256]{3,2,1,0:T(8,128)} %update_probe.1.refs_0_), channel_id=1, source_target_pairs={{0,130},{1,13},{16,146},{17,29},{32,162},{33,45},{48,178},{49,61},... | collective-permute-start | bytes 147464 | tf_op jit(solution)/shard_map/ppermute | solution.py:59
  113.8 4.7 %collective-permute-start.21 = (f32[1,6,8,256]{3,2,1,0:T(8,128)}, f32[1,6,8,256]{3,2,1,0:T(8,128)S(1)}, u32[]{:S(2)}, u32[]{:S(2)}) collective-permute-start(f32[1,6,8,256]{3,2,1,0:T(8,128)} %update_probe.1.refs_0_), channel_id=1, source_target_pairs={{0,2},{1,9},{16,18},{17,25},{32,34},{33,41},{48,50},{49,57},{64,66... | collective-permute-start | bytes 147464 | tf_op jit(solution)/shard_map/ppermute | solution.py:59
  114.5 4.5 %collective-permute-start.20 = (f32[1,6,8,256]{3,2,1,0:T(8,128)}, f32[1,6,8,256]{3,2,1,0:T(8,128)S(1)}, u32[]{:S(2)}, u32[]{:S(2)}) collective-permute-start(f32[1,6,8,256]{3,2,1,0:T(8,128)} %update_probe.1.refs_0_), channel_id=1, source_target_pairs={{0,128},{1,5},{16,144},{17,21},{32,160},{33,37},{48,176},{49,53},{... | collective-permute-start | bytes 147464 | tf_op jit(solution)/shard_map/ppermute | solution.py:59
  121.3 8.7 %collective-permute-start.25 = (f32[4,6,8,256]{3,2,1,0:T(8,128)}, f32[4,6,8,256]{3,2,1,0:T(8,128)S(1)}, u32[]{:S(2)}, u32[]{:S(2)}) collective-permute-start(f32[4,6,8,256]{3,2,1,0:T(8,128)} %gather_parts.2.refs_0_), channel_id=1, source_target_pairs={{0,12},{1,131},{16,28},{17,147},{32,44},{33,163},{48,60},{49,179},... | collective-permute-start | bytes 589832 | tf_op jit(solution)/shard_map/ppermute | solution.py:59
  124.9 6.3 %collective-permute-start.24 = (f32[4,6,8,256]{3,2,1,0:T(8,128)}, f32[4,6,8,256]{3,2,1,0:T(8,128)S(1)}, u32[]{:S(2)}, u32[]{:S(2)}) collective-permute-start(f32[4,6,8,256]{3,2,1,0:T(8,128)} %gather_parts.2.refs_0_), channel_id=1, source_target_pairs={{0,8},{1,3},{16,24},{17,19},{32,40},{33,35},{48,56},{49,51},{64,72... | collective-permute-start | bytes 589832 | tf_op jit(solution)/shard_map/ppermute | solution.py:59
  124.9 8.2 %collective-permute-start.23 = (f32[4,6,8,256]{3,2,1,0:T(8,128)}, f32[4,6,8,256]{3,2,1,0:T(8,128)}, u32[]{:S(2)}, u32[]{:S(2)}) collective-permute-start(f32[4,6,8,256]{3,2,1,0:T(8,128)} %gather_parts.2.refs_0_), channel_id=1, source_target_pairs={{0,4},{1,129},{16,20},{17,145},{32,36},{33,161},{48,52},{49,177},{... | collective-permute-start | bytes 589832 | tf_op jit(solution)/shard_map/ppermute | solution.py:59
  135.3 38.5 %collective-permute-start.26 = (f32[16,6,8,256]{3,2,1,0:T(8,128)}, f32[16,6,8,256]{3,2,1,0:T(8,128)}, u32[]{:S(2)}, u32[]{:S(2)}) collective-permute-start(f32[16,6,8,256]{3,2,1,0:T(8,128)} %gather_parts.3.mine_ref), channel_id=1, source_target_pairs={{0,1},{1,0},{16,17},{17,16},{32,33},{33,32},{48,49},{49,48},{64,65... | collective-permute-start | bytes 2359304 | tf_op jit(solution)/shard_map/ppermute | solution.py:59
  141.2 14.1 %collective-permute-start.5 = (f32[2,256,256]{2,1,0:T(8,128)S(1)}, f32[2,256,256]{2,1,0:T(8,128)S(1)}, u32[]{:S(2)}, u32[]{:S(2)}) collective-permute-start(f32[2,256,256]{2,1,0:T(8,128)S(1)} %get-tuple-element.20), channel_id=1, source_target_pairs={{0,16},{16,32},{32,48},{48,64},{64,80},{80,96},{96,112},{112,128},... | collective-permute-start | bytes 1572872 | tf_op jit(solution)/shard_map/ppermute | solution.py:65
  144.0 28.8 %collective-permute-start.6 = (f32[2,256,256]{2,1,0:T(8,128)S(1)}, f32[2,256,256]{2,1,0:T(8,128)S(1)}, u32[]{:S(2)}, u32[]{:S(2)}) collective-permute-start(f32[2,256,256]{2,1,0:T(8,128)S(1)} %get-tuple-element.21), channel_id=1, source_target_pairs={{0,1},{1,2},{2,3},{3,4},{4,5},{5,6},{6,7},{7,8},{8,9},{9,10},{10,1... | collective-permute-start | bytes 1572872 | tf_op jit(solution)/shard_map/ppermute | solution.py:65
  147.0 25.8 %collective-permute-start.8 = (f32[2,256,256]{2,1,0:T(8,128)}, f32[2,256,256]{2,1,0:T(8,128)S(1)}, u32[]{:S(2)}, u32[]{:S(2)}) collective-permute-start(f32[2,256,256]{2,1,0:T(8,128)} %collective-permute-done.7), channel_id=1, source_target_pairs={{0,16},{16,32},{32,48},{48,64},{64,80},{80,96},{96,112},{112,128},... | collective-permute-start | bytes 1572872 | tf_op jit(solution)/shard_map/ppermute | solution.py:65
  (28 other events, 98.4 us)

commit v2 on v1

--- a/solution.py
+++ b/solution.py
@@ -14,6 +14,8 @@
 SLOTS = 4
 PLANES = 2 * MODES + 1
 AXES = ("gx", "gy")
+SMALL = 16 * 1024 * 1024
+LARGE = 60 * 1024 * 1024
 VMEM = pltpu.VMEM
 SMEM = pltpu.SMEM
 F32 = jnp.float32
@@ -61,8 +63,7 @@
 
 def shifted(value, axis, steps):
     count = lax.axis_size(axis)
-    leading, last = (max(0, -steps), min(count, count - steps))
-    return lax.ppermute(value, axis, [(source, source + steps) for source in range(leading, last)])
+    return lax.ppermute(value, axis, [(source, (source + steps) % count) for source in range(count)])
 
 
 def split_table(matrix):
@@ -119,7 +120,7 @@
     return jnp.concatenate(parts, axis=0)
 
 
-def prepare_kernel(place, counts, own, left, above, corner, probe, amplitude, order, amp_out, weight_out, doubled, measured, sems):
+def sort_kernel(amplitude, order, amp_out, measured, sems):
     loads = [
         pltpu.make_async_copy(
             amplitude.at[:, :, pl.ds(block * HALF, HALF)], measured.at[:, block], sems.at[block]
@@ -141,6 +142,22 @@
         rest32 = sorted_rows - high.astype(F32)
         middle, low = split(rest32)
         amp_out[item] = dot(high, order[...]) + (dot(middle, order[...]) + dot(low, order[...]))
+
+
+def sort_amplitude(amplitude, order):
+    return pl.pallas_call(
+        sort_kernel,
+        out_shape=jax.ShapeDtypeStruct((SLOTS, SIDE, SIDE), F32),
+        in_specs=[pl.BlockSpec(memory_space=pl.ANY), pl.BlockSpec(memory_space=VMEM)],
+        out_specs=pl.BlockSpec(memory_space=VMEM),
+        scratch_shapes=[VMEM((SLOTS, 2, SIDE, HALF), F32), pltpu.SemaphoreType.DMA((2,))],
+        compiler_params=pltpu.CompilerParams(vmem_limit_bytes=LARGE),
+        cost_estimate=pl.CostEstimate(flops=2_000_000_000, bytes_accessed=4_000_000, transcendentals=0),
+        name="sort_amplitude",
+    )(amplitude, order)
+
+
+def cover_kernel(place, counts, own, left, above, corner, probe, weight_out, doubled):
     coverage = probe[0, 0] * probe[0, 0]
     for mode in range(MODES):
         for part in range(2):
@@ -173,31 +190,23 @@
         lax.fori_loop(0, count, visit, 0)
 
 
-def prepare(place, counts, own, left, above, corner, probe, amplitude, order):
+def cover(place, counts, own, left, above, corner, probe):
     return pl.pallas_call(
-        prepare_kernel,
-        out_shape=(
-            jax.ShapeDtypeStruct((SLOTS, SIDE, SIDE), F32),
-            jax.ShapeDtypeStruct((SIDE, SIDE), F32),
-        ),
-        in_specs=[pl.BlockSpec(memory_space=SMEM)] * 6
-        + [pl.BlockSpec(memory_space=VMEM), pl.BlockSpec(memory_space=pl.ANY), pl.BlockSpec(memory_space=VMEM)],
-        out_specs=(pl.BlockSpec(memory_space=VMEM),) * 2,
-        scratch_shapes=[
-            VMEM((2, 2 * SIDE, HALF), F32),
-            VMEM((SLOTS, 2, SIDE, HALF), F32),
-            pltpu.SemaphoreType.DMA((2,)),
-        ],
-        compiler_params=pltpu.CompilerParams(vmem_limit_bytes=32 * 1024 * 1024),
+        cover_kernel,
+        out_shape=jax.ShapeDtypeStruct((SIDE, SIDE), F32),
+        in_specs=[pl.BlockSpec(memory_space=SMEM)] * 6 + [pl.BlockSpec(memory_space=VMEM)],
+        out_specs=pl.BlockSpec(memory_space=VMEM),
+        scratch_shapes=[VMEM((2, 2 * SIDE, HALF), F32)],
+        compiler_params=pltpu.CompilerParams(vmem_limit_bytes=LARGE),
         cost_estimate=pl.CostEstimate(flops=2_000_000_000, bytes_accessed=4_000_000, transcendentals=0),
-        name="prepare",
-    )(place, counts, own, left, above, corner, probe, amplitude, order)
+        name="cover",
+    )(place, counts, own, left, above, corner, probe)
 
 
 def pattern_kernel(
-    place, counts, points, own, right, lower, corner, probe, amplitude, table,
-    core_out, right_out, lower_out, corner_out, send_out, keep_out,
-    field, target, total, spectrum, sems,
+    place, counts, points, own, right, lower, corner, probe_in, amplitude_in, table_in,
+    core_out, right_out, lower_out, send_out, keep_out,
+    field, target, total, spectrum, probe, amplitude, table, sems,
 ):
     row_id = place[0]
     col_id = place[1]
@@ -212,6 +221,8 @@
                     sems.at[len(loads)],
                 )
             )
+    for source, dest in ((probe_in, probe), (table_in, table), (amplitude_in, amplitude)):
+        loads.append(pltpu.make_async_copy(source, dest, sems.at[len(loads)]))
     for load in loads:
         load.start()
     target[...] = jnp.zeros_like(target)
@@ -297,11 +308,11 @@
         pltpu.make_async_copy(total.at[pl.ds((1 - core) * 16, 16)], send_out, sems.at[0]),
         pltpu.make_async_copy(total.at[pl.ds(core * 16, 16)], keep_out, sems.at[1]),
     ]
-    for piece, up, back in ((core_out, 0, 0), (right_out, 0, 1), (lower_out, 1, 0), (corner_out, 1, 1)):
+    for piece, up, tall, back in ((core_out, 0, 1, 0), (right_out, 0, 2, 1), (lower_out, 1, 1, 0)):
         for block in range(2):
             stores.append(
                 pltpu.make_async_copy(
-                    target.at[:, 2 * back + block, pl.ds(up * SIDE, SIDE), :],
+                    target.at[:, 2 * back + block, pl.ds(up * SIDE, tall * SIDE), :],
                     piece.at[:, :, pl.ds(block * HALF, HALF)],
                     sems.at[len(stores)],
                 )
@@ -314,53 +325,60 @@
 
 def visit_patterns(place, counts, points, own, right, lower, corner, probe, amplitude, table):
     tile = jax.ShapeDtypeStruct((2, SIDE, SIDE), F32)
+    tall = jax.ShapeDtypeStruct((2, 2 * SIDE, SIDE), F32)
     part = jax.ShapeDtypeStruct((16, PLANES, 8, SIDE), F32)
     return pl.pallas_call(
         pattern_kernel,
-        out_shape=(tile, tile, tile, tile, part, part),
-        in_specs=[pl.BlockSpec(memory_space=SMEM)] * 3
-        + [pl.BlockSpec(memory_space=pl.ANY)] * 4
-        + [pl.BlockSpec(memory_space=VMEM)] * 3,
-        out_specs=(pl.BlockSpec(memory_space=pl.ANY),) * 6,
+        out_shape=(tile, tall, tile, part, part),
+        in_specs=[pl.BlockSpec(memory_space=SMEM)] * 3 + [pl.BlockSpec(memory_space=pl.ANY)] * 7,
+        out_specs=(pl.BlockSpec(memory_space=pl.ANY),) * 5,
         scratch_shapes=[
             VMEM((2, 4, 2 * SIDE, HALF), F32),
             VMEM((2, 4, 2 * SIDE, HALF), F32),
             VMEM((32, PLANES, 8, SIDE), F32),
             VMEM((MODES, 2, SIDE, SIDE), F32),
-            pltpu.SemaphoreType.DMA((10,)),
+            VMEM(probe.shape, F32),
+            VMEM(amplitude.shape, F32),
+            VMEM(table.shape, BF16),
+            pltpu.SemaphoreType.DMA((11,)),
         ],
-        compiler_params=pltpu.CompilerParams(vmem_limit_bytes=48 * 1024 * 1024),
+        compiler_params=pltpu.CompilerParams(vmem_limit_bytes=LARGE),
         cost_estimate=pl.CostEstimate(flops=10_000_000_000, bytes_accessed=10_000_000, transcendentals=0),
         name="patterns",
     )(place, counts, points, own, right, lower, corner, probe, amplitude, table)
 
 
-def scatter_kernel(slot, place, *refs):
-    pieces, outs = refs[:-4], refs[-4:]
-    length = outs[0].shape[0]
-    mine = place[slot]
-    for step in range(4):
-        start = lax.rem(mine + step, 4) * length
-        block = pieces[0][pl.ds(start, length)]
-        for piece in pieces[1:]:
-            block = block + piece[pl.ds(start, length)]
-        outs[step][...] = block
-
-
-def scatter_sum(slot, place, pieces):
-    shape = (pieces[0].shape[0] // 4,) + pieces[0].shape[1:]
-
-    def body(*refs):
-        scatter_kernel(slot, *refs)
-
+def small_call(body, name, out_shape, operands, scalars=0, unread=0, **options):
+    held = len(operands) - scalars - unread
+    out_specs = jax.tree.map(lambda _: pl.BlockSpec(memory_space=VMEM), out_shape)
     return pl.pallas_call(
         body,
-        out_shape=(jax.ShapeDtypeStruct(shape, F32),) * 4,
-        in_specs=[pl.BlockSpec(memory_space=SMEM)] + [pl.BlockSpec(memory_space=VMEM)] * len(pieces),
-        out_specs=(pl.BlockSpec(memory_space=VMEM),) * 4,
-        compiler_params=pltpu.CompilerParams(vmem_limit_bytes=32 * 1024 * 1024),
-        name="scatter_sum",
-    )(place, *pieces)
+        out_shape=out_shape,
+        in_specs=[pl.BlockSpec(memory_space=SMEM)] * scalars
+        + [pl.BlockSpec(memory_space=VMEM)] * held
+        + [pl.BlockSpec(memory_space=pl.ANY)] * unread,
+        out_specs=out_specs,
+        compiler_params=pltpu.CompilerParams(vmem_limit_bytes=SMALL),
+        name=name,
+        **options,
+    )(*operands)
+
+
+def scatter_sum(slot, place, pieces):
+    length = pieces[0].shape[0] // 4
+    shape = (length,) + pieces[0].shape[1:]
+    number = len(pieces)
+
+    def body(place, *refs):
+        outs = refs[-4:]
+        for step in range(4):
+            start = lax.rem(place[slot] + step, 4) * length
+            block = refs[0][pl.ds(start, length)]
+            for piece in refs[1:number]:
+                block = block + piece[pl.ds(start, length)]
+            outs[step][...] = block
+
+    return small_call(body, "scatter_sum", (jax.ShapeDtypeStruct(shape, F32),) * 4, (place, *pieces), scalars=1)
 
 
 def plain_sum(pieces):
@@ -370,88 +388,99 @@
             block = block + piece[...]
         refs[-1][...] = block
 
-    return pl.pallas_call(
-        body,
-        out_shape=jax.ShapeDtypeStruct(pieces[0].shape, F32),
-        in_specs=[pl.BlockSpec(memory_space=VMEM)] * len(pieces),
-        out_specs=pl.BlockSpec(memory_space=VMEM),
-        name="plain_sum",
-    )(*pieces)
-
-
-def update_probe(place, pieces, probe):
-    def body(place, *refs):
-        probe_ref, out = refs[-2], refs[-1]
+    return small_call(body, "plain_sum", jax.ShapeDtypeStruct(pieces[0].shape, F32), pieces)
+
+
+def update_probe(pieces, old):
+    def body(*refs):
+        old_ref, out = refs[-2:]
         block = refs[0][0]
         for piece in refs[1:-2]:
             block = block + piece[0]
-        group = place[2] * 16 + place[3] * 4 + place[4]
         scale = 1.0 / (block[PLANES - 1] + 1.0)
         for plane in range(PLANES - 1):
-            out[0, plane] = (probe_ref[plane, group] + block[plane]) * scale
+            out[0, plane] = (old_ref[0, plane] + block[plane]) * scale
+
+    return small_call(body, "update_probe", jax.ShapeDtypeStruct(old.shape, F32), (*pieces, old))
+
+
+def own_rows(place, probe):
+    def body(place, probe_ref, out):
+        group = place[2] * 16 + place[3] * 4 + place[4]
+        for plane in range(PLANES - 1):
+            out[0, plane] = probe_ref[plane, group]
 
     return pl.pallas_call(
         body,
         out_shape=jax.ShapeDtypeStruct((1, PLANES - 1, 8, SIDE), F32),
-        in_specs=[pl.BlockSpec(memory_space=SMEM)] + [pl.BlockSpec(memory_space=VMEM)] * (len(pieces) + 1),
+        in_specs=[pl.BlockSpec(memory_space=SMEM), pl.BlockSpec(memory_space=VMEM)],
         out_specs=pl.BlockSpec(memory_space=VMEM),
-        name="update_probe",
-    )(place, *pieces, probe.reshape(PLANES - 1, 32, 8, SIDE))
-
-
-def gather_parts(slot, place, pieces):
+        compiler_params=pltpu.CompilerParams(vmem_limit_bytes=LARGE),
+        name="own_rows",
+    )(place, probe.reshape(PLANES - 1, 32, 8, SIDE))
+
+
+def gather_parts(pieces):
     length = pieces[0].shape[0]
 
-    def body(place, *refs):
-        out = refs[-1]
+    def body(*refs):
         for step, piece in enumerate(refs[:-1]):
-            start = lax.rem(place[slot] + 4 - step, 4) * length
-            out[pl.ds(start, length)] = piece[...]
-
-    return pl.pallas_call(
-        body,
-        out_shape=jax.ShapeDtypeStruct((4 * length,) + pieces[0].shape[1:], F32),
-        in_specs=[pl.BlockSpec(memory_space=SMEM)] + [pl.BlockSpec(memory_space=VMEM)] * 4,
-        out_specs=pl.BlockSpec(memory_space=VMEM),
-        name="gather_parts",
-    )(place, *pieces)
+            refs[-1][pl.ds(step * length, length)] = piece[...]
+
+    shape = (4 * length,) + pieces[0].shape[1:]
+    return small_call(body, "gather_parts", jax.ShapeDtypeStruct(shape, F32), pieces)
 
 
 def join_halves(place, mine, other):
-    def body(place, mine_ref, other_ref, out):
-        core = place[2]
-        for plane in range(PLANES - 1):
-            for piece, start in ((mine_ref, core * 16), (other_ref, 16 - core * 16)):
-                out[plane, pl.ds(start, 16)] = piece[:, plane]
+    def body(place, mine_ref, other_ref, out, sem):
+        core, first, second = place[2], place[3], place[4]
+        copies = []
+        for piece, half, outer, inner in (
+            (mine_ref, core, first, second), (other_ref, 1 - core, second, first)
+        ):
+            for one in range(4):
+                for two in range(4):
+                    group = half * 16 + lax.rem(outer + 4 - one, 4) * 4 + lax.rem(inner + 4 - two, 4)
+                    copies.append(
+                        pltpu.make_async_copy(piece.at[one * 4 + two], out.at[:, group], sem.at[len(copies)])
+                    )
+        for copy in copies:
+            copy.start()
+        for copy in copies:
+            copy.wait()
 
     out = pl.pallas_call(
         body,
         out_shape=jax.ShapeDtypeStruct((PLANES - 1, 32, 8, SIDE), F32),
-        in_specs=[pl.BlockSpec(memory_space=SMEM)] + [pl.BlockSpec(memory_space=VMEM)] * 2,
-        out_specs=pl.BlockSpec(memory_space=VMEM),
+        in_specs=[pl.BlockSpec(memory_space=SMEM)] + [pl.BlockSpec(memory_space=pl.ANY)] * 2,
+        out_specs=pl.BlockSpec(memory_space=pl.ANY),
+        scratch_shapes=[pltpu.SemaphoreType.DMA((32,))],
+        compiler_params=pltpu.CompilerParams(vmem_limit_bytes=SMALL),
         name="join_halves",
     )(place, mine, other)
     return out.reshape(MODES, 2, SIDE, SIDE)
 
 
-def update_object(own, pieces, weight):
-    def body(own_ref, *refs):
-        weight_ref, out = refs[-2], refs[-1]
+def add_corner(lower, side, after):
+    def body(lower_ref, side_ref, after_ref, out):
+        out[...] = lower_ref[...] + side_ref[:, SIDE:, :]
+
+    return small_call(
+        body, "add_corner", jax.ShapeDtypeStruct(lower.shape, F32), (lower, side, after), unread=1
+    )
+
+
+def update_object(own, core, side, above, weight, after):
+    def body(own_ref, core_ref, side_ref, above_ref, weight_ref, after_ref, out):
         scale = 1.0 / weight_ref[...]
         for part in range(2):
-            block = own_ref[part]
-            for piece in refs[:-2]:
-                block = block + piece[part]
-            out[part] = block * scale
-
-    return pl.pallas_call(
-        body,
-        out_shape=jax.ShapeDtypeStruct((2, SIDE, SIDE), F32),
-        in_specs=[pl.BlockSpec(memory_space=VMEM)] * (len(pieces) + 2),
-        out_specs=pl.BlockSpec(memory_space=VMEM),
-        compiler_params=pltpu.CompilerParams(vmem_limit_bytes=32 * 1024 * 1024),
-        name="update_object",
-    )(own, *pieces, weight)
+            block = own_ref[part] + core_ref[part]
+            out[part] = (block + side_ref[part, :SIDE, :] + above_ref[part]) * scale
+
+    return small_call(
+        body, "update_object", jax.ShapeDtypeStruct(own.shape, F32),
+        (own, core, side, above, weight, after), unread=1,
+    )
 
 
 def shards(object_field, probe, amplitudes, positions, counts):
@@ -470,34 +499,29 @@
     right_strip = shifted(object_field, "gx", -1)
     lower_strip = shifted(object_field, "gy", -1)
     points_left = shifted(points, "gx", 1)
+    amplitude = sort_amplitude(amplitudes[0, 0], order)
+    old_rows = own_rows(place, probe)
     points_pair = shifted(jnp.concatenate([points, points_left], 0), "gy", 1)
     diagonal = shifted(right_strip, "gy", -1)
-    amplitude, weight = prepare(
-        place, counts, points, points_left, points_pair[:SLOTS], points_pair[SLOTS:],
-        probe, amplitudes[0, 0], order,
-    )
-    core_grad, right_grad, lower_grad, corner_grad, other_half, half = visit_patterns(
+    weight = cover(place, counts, points, points_left, points_pair[:SLOTS], points_pair[SLOTS:], probe)
+    core_grad, side_grad, lower_grad, other_half, half = visit_patterns(
         place, counts, points, object_field, right_strip, lower_strip, diagonal, probe, amplitude, table
     )
 
     half_in = send(other_half, core_pair())
+    from_left = shifted(side_grad, "gx", 1)
     parts = scatter_sum(3, place, [half, half_in])
     arrived = [send(parts[step], first_ring(step)) for step in (1, 2, 3)]
-    corner_step = shifted(corner_grad, "gy", 1)
     parts = scatter_sum(4, place, [parts[0]] + arrived)
     arrived = [send(parts[step], second_ring(step)) for step in (1, 2, 3)]
-    from_above = shifted(lower_grad, "gy", 1)
     block = plain_sum([parts[0]] + arrived)
+    from_above = shifted(add_corner(lower_grad, from_left, block), "gy", 1)
     block = plain_sum([block, send(block, depth_pair())])
-    chunk = update_probe(place, [block] + [send(block, depth_ring(step)) for step in (2, 4, 6)], probe)
-    from_left = shifted(right_grad, "gx", 1)
-    from_corner = shifted(corner_step, "gx", 1)
-    chunk = gather_parts(4, place, [chunk] + [send(chunk, second_ring(step)) for step in (1, 2, 3)])
-    chunk = gather_parts(3, place, [chunk] + [send(chunk, first_ring(step)) for step in (1, 2, 3)])
+    chunk = update_probe([block] + [send(block, depth_ring(step)) for step in (2, 4, 6)], old_rows)
+    chunk = gather_parts([chunk] + [send(chunk, second_ring(step)) for step in (1, 2, 3)])
+    new_object = update_object(object_field, core_grad, from_left, from_above, weight, chunk)
+    chunk = gather_parts([chunk] + [send(chunk, first_ring(step)) for step in (1, 2, 3)])
     new_probe = join_halves(place, chunk, send(chunk, core_pair()))
-    new_object = update_object(
-        object_field, [core_grad, from_left, from_above, from_corner], weight
-    )
     return (new_object, new_probe)
 
 

time: 177 us -> 152 us (0.86)
  the two profiles are of different devices: /device:TPU:1 before, /device:TPU:70 now
where the time goes in v2:
time: 152 us; the launch traced here: 151 us
  starting transfers between devices  56.1 us (37%)
  waiting for transfers between devices  52.8 us (35%)
  Pallas kernels  34.9 us (23%)
  local copies, waits for them, and re-layouts  6.31 us (4%)
    ppermute x18, starting transfers between devices, send(): return lax.ppermute(value, AXES, pairs)  42.5 us
    ppermute x18, waiting for transfers between devices, send(): return lax.ppermute(value, AXES, pairs)  30.2 us
    ppermute x7, waiting for transfers between devices, shifted(): lax.ppermute(value, axis, [(source, (source + steps) % count) for source...  22.5 us
    pallas_call x1, Pallas kernels, visit_patterns(): pl.pallas_call(pattern_kernel, out_shape=(tile, tall, tile, part, part),...  18.5 us
    ppermute x7, starting transfers between devices, shifted(): lax.ppermute(value, axis, [(source, (source + steps) % count) for source...  13.6 us
    pallas_call x1, Pallas kernels, cover(): pl.pallas_call(cover_kernel, out_shape=jax.ShapeDtypeStruct((SIDE, SIDE),...  4.51 us
    pallas_call x9, Pallas kernels, small_call(): pl.pallas_call(body, out_shape=out_shape, in_specs=[pl.BlockSpec(memory_s...  4.15 us
    unnamed x26, local copies, waits for them, and re-layouts  3.76 us
  transfers between devices with their start and end apart: 25, of which 18 were waited for; matrix products, arithmetic and copies ran while one was open for 2% of the time, Pallas kernels for 10%

profile of v2, /device:TPU:70, one launch (start us, length us, event | category | flops | bytes accessed | tf_op | source)
XLA Modules:
  0.0 151.1 jit_solution(15564167558219244853)
XLA Ops:
  0.8 2.9 %collective-permute-start.1 = (f32[2,256,256]{2,1,0:T(8,128)}, f32[2,256,256]{2,1,0:T(8,128)S(1)}, u32[]{:S(2)}, u32[]{:S(2)}) collective-permute-start(f32[2,256,256]{2,1,0:T(8,128)} %own_ref.1), channel_id=1, source_target_pairs={{0,15},{1,0},{2,1},{3,2},{4,3},{5,4},{6,5},{7,6},{8,7},{9,8},{10,9... | collective-permute-start | bytes 1572872 | tf_op jit(solution)/shard_map/ppermute | solution.py:66
  3.7 11.1 %collective-permute-done.right = f32[2,256,256]{2,1,0:T(8,128)S(1)} collective-permute-done((f32[2,256,256]{2,1,0:T(8,128)}, f32[2,256,256]{2,1,0:T(8,128)S(1)}, u32[]{:S(2)}, u32[]{:S(2)}) %collective-permute-start) | collective-permute-done | bytes 524320 | tf_op jit(solution)/shard_map/ppermute | solution.py:66
  14.8 2.2 %collective-permute-start.2 = (f32[2,256,256]{2,1,0:T(8,128)S(1)}, f32[2,256,256]{2,1,0:T(8,128)S(1)}, u32[]{:S(2)}, u32[]{:S(2)}) collective-permute-start(f32[2,256,256]{2,1,0:T(8,128)S(1)} %collective-permute-done.right), channel_id=1, source_target_pairs={{0,15},{1,0},{2,1},{3,2},{4,3},{5,4},{6,5},{7,6},{8,7},{9,8},{10,9... | collective-permute-start | bytes 1572872 | tf_op jit(solution)/shard_map/ppermute | solution.py:66
  18.9 3.7 %sort_amplitude.1.amplitude_in = f32[4,256,256]{2,1,0:T(8,128)} custom-call(f32[4,256,256]{2,1,0:T(8,128)} %bitcast.12, bf16[256,256]{1,0:T(8,128)(2,1)} %constant.61.clone.order), custom_call_target="tpu_custom_call" | custom-call | flops 2000000000 | bytes 4000000 | tf_op jit(solution)/shard_map/sort_amplitude/pallas_call | solution.py:148
  24.5 18.5 %patterns.1 = (f32[2,256,256]{2,1,0:T(8,128)}, f32[2,512,256]{2,1,0:T(8,128)}, f32[2,256,256]{2,1,0:T(8,128)}, f32[16,7,8,256]{3,2,1,0:T(8,128)}, f32[16,7,8,256]{3,2,1,0:T(8,128)}) custom-call(s32[5]{0:T(128)} %stack.23.place, s32[16,16]{1,0:T(8,128)} %counts.3, s32[4,2]{1,0:T(4,128)} %copy.18.points.own, f32[2,256,256]{2,1,0:T(8,128)} %own_ref.1, ...), custom_call_target="tpu_custom_call" | custom-call | flops 10000000000 | bytes 10000000 | tf_op jit(solution)/shard_map/patterns/pallas_call | solution.py:330
  44.3 7.5 %collective-permute-start.3 = (f32[2,512,256]{2,1,0:T(8,128)}, f32[2,512,256]{2,1,0:T(8,128)S(1)}, u32[]{:S(2)}, u32[]{:S(2)}) collective-permute-start(f32[2,512,256]{2,1,0:T(8,128)} %get-tuple-element.16), channel_id=1, source_target_pairs={{0,16},{16,32},{32,48},{48,64},{64,80},{80,96},{96,112},{112,128},... | collective-permute-start | bytes 3145736 | tf_op jit(solution)/shard_map/ppermute | solution.py:66
  56.6 3.1 %collective-permute-done.5.refs_1_ = f32[4,7,8,256]{3,2,1,0:T(8,128)S(1)} collective-permute-done((f32[4,7,8,256]{3,2,1,0:T(8,128)S(1)}, f32[4,7,8,256]{3,2,1,0:T(8,128)S(1)}, u32[]{:S(2)}, u32[]{:S(2)}) %collective-permute-start.5) | collective-permute-done | bytes 229408 | tf_op jit(solution)/shard_map/ppermute | solution.py:61
  59.7 2.9 %collective-permute-done.6.refs_2_ = f32[4,7,8,256]{3,2,1,0:T(8,128)S(1)} collective-permute-done((f32[4,7,8,256]{3,2,1,0:T(8,128)S(1)}, f32[4,7,8,256]{3,2,1,0:T(8,128)S(1)}, u32[]{:S(2)}, u32[]{:S(2)}) %collective-permute-start.6) | collective-permute-done | bytes 229408 | tf_op jit(solution)/shard_map/ppermute | solution.py:61
  62.6 2.4 %collective-permute-done.7.refs_3_ = f32[4,7,8,256]{3,2,1,0:T(8,128)S(1)} collective-permute-done((f32[4,7,8,256]{3,2,1,0:T(8,128)S(1)}, f32[4,7,8,256]{3,2,1,0:T(8,128)S(1)}, u32[]{:S(2)}, u32[]{:S(2)}) %collective-permute-start.7) | collective-permute-done | bytes 229408 | tf_op jit(solution)/shard_map/ppermute | solution.py:61
  65.5 2.3 %collective-permute-start.10 = (f32[1,7,8,256]{3,2,1,0:T(8,128)S(1)}, f32[1,7,8,256]{3,2,1,0:T(8,128)S(1)}, u32[]{:S(2)}, u32[]{:S(2)}) collective-permute-start(f32[1,7,8,256]{3,2,1,0:T(8,128)S(1)} %get-tuple-element.27), channel_id=1, source_target_pairs={{0,130},{1,13},{16,146},{17,29},{32,162},{33,45},{48,178},{49,61},... | collective-permute-start | bytes 172040 | tf_op jit(solution)/shard_map/ppermute | solution.py:61
  69.8 4.1 %collective-permute-done.8.refs_1_ = f32[1,7,8,256]{3,2,1,0:T(8,128)S(1)} collective-permute-done((f32[1,7,8,256]{3,2,1,0:T(8,128)S(1)}, f32[1,7,8,256]{3,2,1,0:T(8,128)S(1)}, u32[]{:S(2)}, u32[]{:S(2)}) %collective-permute-start.8) | collective-permute-done | bytes 57376 | tf_op jit(solution)/shard_map/ppermute | solution.py:61
  73.9 2.4 %collective-permute-start.14 = (f32[1,7,8,256]{3,2,1,0:T(8,128)S(1)}, f32[1,7,8,256]{3,2,1,0:T(8,128)S(1)}, u32[]{:S(2)}, u32[]{:S(2)}) collective-permute-start(f32[1,7,8,256]{3,2,1,0:T(8,128)S(1)} %plain_sum.2.after_ref.refs_0_), channel_id=1, source_target_pairs={{0,16},{1,17},{16,0},{17,1},{32,48},{33,49},{48,32},{49,33},{64,80... | collective-permute-start | bytes 172040 | tf_op jit(solution)/shard_map/ppermute | solution.py:61
  76.3 2.2 %collective-permute-done.14.refs_1_ = f32[1,7,8,256]{3,2,1,0:T(8,128)S(1)} collective-permute-done((f32[1,7,8,256]{3,2,1,0:T(8,128)S(1)}, f32[1,7,8,256]{3,2,1,0:T(8,128)S(1)}, u32[]{:S(2)}, u32[]{:S(2)}) %collective-permute-start.14) | collective-permute-done | bytes 57376 | tf_op jit(solution)/shard_map/ppermute | solution.py:61
  78.4 3.1 %collective-permute-start.15 = (f32[1,7,8,256]{3,2,1,0:T(8,128)S(1)}, f32[1,7,8,256]{3,2,1,0:T(8,128)S(1)}, u32[]{:S(2)}, u32[]{:S(2)}) collective-permute-start(f32[1,7,8,256]{3,2,1,0:T(8,128)S(1)} %plain_sum.3.refs_0_), channel_id=1, source_target_pairs={{0,32},{1,33},{16,48},{17,49},{32,64},{33,65},{48,80},{49,81},{64,... | collective-permute-start | bytes 172040 | tf_op jit(solution)/shard_map/ppermute | solution.py:61
  81.6 12.7 %collective-permute-start.16 = (f32[1,7,8,256]{3,2,1,0:T(8,128)S(1)}, f32[1,7,8,256]{3,2,1,0:T(8,128)S(1)}, u32[]{:S(2)}, u32[]{:S(2)}) collective-permute-start(f32[1,7,8,256]{3,2,1,0:T(8,128)S(1)} %plain_sum.3.refs_0_), channel_id=1, source_target_pairs={{0,64},{1,65},{16,80},{17,81},{32,96},{33,97},{48,112},{49,113},{6... | collective-permute-start | bytes 172040 | tf_op jit(solution)/shard_map/ppermute | solution.py:61
  94.2 2.1 %own_rows.1.refs_4_ = f32[1,6,8,256]{3,2,1,0:T(8,128)} custom-call(s32[5]{0:T(128)} %stack.23.place, f32[6,32,8,256]{3,2,1,0:T(8,128)} %bitcast.9), custom_call_target="tpu_custom_call" | custom-call | tf_op jit(solution)/shard_map/own_rows/pallas_call | solution.py:413
  97.0 3.6 %collective-permute-done.17.refs_3_ = f32[1,7,8,256]{3,2,1,0:T(8,128)S(1)} collective-permute-done((f32[1,7,8,256]{3,2,1,0:T(8,128)S(1)}, f32[1,7,8,256]{3,2,1,0:T(8,128)S(1)}, u32[]{:S(2)}, u32[]{:S(2)}) %collective-permute-start.17) | collective-permute-done | bytes 57376 | tf_op jit(solution)/shard_map/ppermute | solution.py:61
  102.4 4.5 %collective-permute-start.19 = (f32[1,6,8,256]{3,2,1,0:T(8,128)S(1)}, f32[1,6,8,256]{3,2,1,0:T(8,128)S(1)}, u32[]{:S(2)}, u32[]{:S(2)}) collective-permute-start(f32[1,6,8,256]{3,2,1,0:T(8,128)S(1)} %update_probe.1.refs_0_), channel_id=1, source_target_pairs={{0,2},{1,9},{16,18},{17,25},{32,34},{33,41},{48,50},{49,57},{64,66... | collective-permute-start | bytes 147464 | tf_op jit(solution)/shard_map/ppermute | solution.py:61
  113.8 3.5 %collective-permute-done.21.refs_1_ = f32[4,6,8,256]{3,2,1,0:T(8,128)S(1)} collective-permute-done((f32[4,6,8,256]{3,2,1,0:T(8,128)S(1)}, f32[4,6,8,256]{3,2,1,0:T(8,128)S(1)}, u32[]{:S(2)}, u32[]{:S(2)}) %collective-permute-start.21) | collective-permute-done | bytes 196640 | tf_op jit(solution)/shard_map/ppermute | solution.py:61
  117.3 2.2 %collective-permute-done.22.refs_2_ = f32[4,6,8,256]{3,2,1,0:T(8,128)S(1)} collective-permute-done((f32[4,6,8,256]{3,2,1,0:T(8,128)S(1)}, f32[4,6,8,256]{3,2,1,0:T(8,128)S(1)}, u32[]{:S(2)}, u32[]{:S(2)}) %collective-permute-start.22) | collective-permute-done | bytes 196640 | tf_op jit(solution)/shard_map/ppermute | solution.py:61
  121.6 7.1 %collective-permute-start.24 = (f32[16,6,8,256]{3,2,1,0:T(8,128)S(1)}, f32[16,6,8,256]{3,2,1,0:T(8,128)S(1)}, u32[]{:S(2)}, u32[]{:S(2)}) collective-permute-start(f32[16,6,8,256]{3,2,1,0:T(8,128)S(1)} %gather_parts.3.mine_ref), channel_id=1, source_target_pairs={{0,1},{1,0},{16,17},{17,16},{32,33},{33,32},{48,49},{49,48},{64,65... | collective-permute-start | bytes 2359304 | tf_op jit(solution)/shard_map/ppermute | solution.py:61
  129.6 3.6 %collective-permute-done.12.left = s32[4,2]{1,0:T(4,128)S(1)} collective-permute-done((s32[4,2]{1,0:T(4,128)S(1)}, s32[4,2]{1,0:T(4,128)S(1)}, u32[]{:S(2)}, u32[]{:S(2)}) %collective-permute-start.12) | collective-permute-done | bytes 64 | tf_op jit(solution)/shard_map/ppermute | solution.py:66
  134.0 6.9 %collective-permute-done.13 = s32[8,2]{1,0:T(8,128)S(1)} collective-permute-done((s32[8,2]{1,0:T(8,128)S(1)}, s32[8,2]{1,0:T(8,128)S(1)}, u32[]{:S(2)}, u32[]{:S(2)}) %collective-permute-start.13) | collective-permute-done | bytes 96 | tf_op jit(solution)/shard_map/ppermute | solution.py:66
  141.5 4.5 %cover.1.weight_ref = f32[256,256]{1,0:T(8,128)} custom-call(s32[5]{0:T(128)} %stack.23.place, s32[16,16]{1,0:T(8,128)} %counts.3, s32[4,2]{1,0:T(4,128)} %copy.18.points.own, s32[4,2]{1,0:T(4,128)} %copy-done.9, s32[4,2]{1,0:T(4,128)} %get-tuple-element.29.above, s32[4,2]{1,0:T(4,128)} %get-tuple-element.28.corner, f32[3,2,256,256]{3,2,1,0:T(8,128)} %probe.1), custom_call_target="tpu_custom_call" | custom-call | flops 2000000000 | bytes 4000000 | tf_op jit(solution)/shard_map/cover/pallas_call | solution.py:194
  (70 shorter events, 31.3 us)
Async XLA Ops:
  0.6 14.1 %collective-permute-start = (f32[2,256,256]{2,1,0:T(8,128)}, f32[2,256,256]{2,1,0:T(8,128)S(1)}, u32[]{:S(2)}, u32[]{:S(2)}) collective-permute-start(f32[2,256,256]{2,1,0:T(8,128)} %own_ref.1), channel_id=1, source_target_pairs={{0,240},{16,0},{32,16},{48,32},{64,48},{80,64},{96,80},{112,96},{1... | collective-permute-start | bytes 1572872 | tf_op jit(solution)/shard_map/ppermute | solution.py:66
  0.8 21.9 %collective-permute-start.1 = (f32[2,256,256]{2,1,0:T(8,128)}, f32[2,256,256]{2,1,0:T(8,128)S(1)}, u32[]{:S(2)}, u32[]{:S(2)}) collective-permute-start(f32[2,256,256]{2,1,0:T(8,128)} %own_ref.1), channel_id=1, source_target_pairs={{0,15},{1,0},{2,1},{3,2},{4,3},{5,4},{6,5},{7,6},{8,7},{9,8},{10,9... | collective-permute-start | bytes 1572872 | tf_op jit(solution)/shard_map/ppermute | solution.py:66
  14.8 8.9 %collective-permute-start.2 = (f32[2,256,256]{2,1,0:T(8,128)S(1)}, f32[2,256,256]{2,1,0:T(8,128)S(1)}, u32[]{:S(2)}, u32[]{:S(2)}) collective-permute-start(f32[2,256,256]{2,1,0:T(8,128)S(1)} %collective-permute-done.right), channel_id=1, source_target_pairs={{0,15},{1,0},{2,1},{3,2},{4,3},{5,4},{6,5},{7,6},{8,7},{9,8},{10,9... | collective-permute-start | bytes 1572872 | tf_op jit(solution)/shard_map/ppermute | solution.py:66
  43.0 8.8 %collective-permute-start.4 = (f32[16,7,8,256]{3,2,1,0:T(8,128)}, f32[16,7,8,256]{3,2,1,0:T(8,128)S(1)}, u32[]{:S(2)}, u32[]{:S(2)}) collective-permute-start(f32[16,7,8,256]{3,2,1,0:T(8,128)} %get-tuple-element.19), channel_id=1, source_target_pairs={{0,1},{1,0},{16,17},{17,16},{32,33},{33,32},{48,49},{49,48},{64,65... | collective-permute-start | bytes 2752520 | tf_op jit(solution)/shard_map/ppermute | solution.py:61
  44.3 84.5 %collective-permute-start.3 = (f32[2,512,256]{2,1,0:T(8,128)}, f32[2,512,256]{2,1,0:T(8,128)S(1)}, u32[]{:S(2)}, u32[]{:S(2)}) collective-permute-start(f32[2,512,256]{2,1,0:T(8,128)} %get-tuple-element.16), channel_id=1, source_target_pairs={{0,16},{16,32},{32,48},{48,64},{64,80},{80,96},{96,112},{112,128},... | collective-permute-start | bytes 3145736 | tf_op jit(solution)/shard_map/ppermute | solution.py:66
  53.6 6.1 %collective-permute-start.5 = (f32[4,7,8,256]{3,2,1,0:T(8,128)S(1)}, f32[4,7,8,256]{3,2,1,0:T(8,128)S(1)}, u32[]{:S(2)}, u32[]{:S(2)}) collective-permute-start(f32[4,7,8,256]{3,2,1,0:T(8,128)S(1)} %get-tuple-element.21), channel_id=1, source_target_pairs={{0,4},{1,129},{16,20},{17,145},{32,36},{33,161},{48,52},{49,177},{... | collective-permute-start | bytes 688136 | tf_op jit(solution)/shard_map/ppermute | solution.py:61
  55.0 7.6 %collective-permute-start.6 = (f32[4,7,8,256]{3,2,1,0:T(8,128)S(1)}, f32[4,7,8,256]{3,2,1,0:T(8,128)S(1)}, u32[]{:S(2)}, u32[]{:S(2)}) collective-permute-start(f32[4,7,8,256]{3,2,1,0:T(8,128)S(1)} %get-tuple-element.22), channel_id=1, source_target_pairs={{0,8},{1,3},{16,24},{17,19},{32,40},{33,35},{48,56},{49,51},{64,72... | collective-permute-start | bytes 688136 | tf_op jit(solution)/shard_map/ppermute | solution.py:61
  56.6 8.3 %collective-permute-start.7 = (f32[4,7,8,256]{3,2,1,0:T(8,128)S(1)}, f32[4,7,8,256]{3,2,1,0:T(8,128)S(1)}, u32[]{:S(2)}, u32[]{:S(2)}) collective-permute-start(f32[4,7,8,256]{3,2,1,0:T(8,128)S(1)} %get-tuple-element.23), channel_id=1, source_target_pairs={{0,12},{1,131},{16,28},{17,147},{32,44},{33,163},{48,60},{49,179},... | collective-permute-start | bytes 688136 | tf_op jit(solution)/shard_map/ppermute | solution.py:61
  65.5 4.3 %collective-permute-start.10 = (f32[1,7,8,256]{3,2,1,0:T(8,128)S(1)}, f32[1,7,8,256]{3,2,1,0:T(8,128)S(1)}, u32[]{:S(2)}, u32[]{:S(2)}) collective-permute-start(f32[1,7,8,256]{3,2,1,0:T(8,128)S(1)} %get-tuple-element.27), channel_id=1, source_target_pairs={{0,130},{1,13},{16,146},{17,29},{32,162},{33,45},{48,178},{49,61},... | collective-permute-start | bytes 172040 | tf_op jit(solution)/shard_map/ppermute | solution.py:61
  67.9 6.0 %collective-permute-start.8 = (f32[1,7,8,256]{3,2,1,0:T(8,128)S(1)}, f32[1,7,8,256]{3,2,1,0:T(8,128)S(1)}, u32[]{:S(2)}, u32[]{:S(2)}) collective-permute-start(f32[1,7,8,256]{3,2,1,0:T(8,128)S(1)} %get-tuple-element.25), channel_id=1, source_target_pairs={{0,128},{1,5},{16,144},{17,21},{32,160},{33,37},{48,176},{49,53},{... | collective-permute-start | bytes 172040 | tf_op jit(solution)/shard_map/ppermute | solution.py:61
  67.9 6.0 %collective-permute-start.9 = (f32[1,7,8,256]{3,2,1,0:T(8,128)S(1)}, f32[1,7,8,256]{3,2,1,0:T(8,128)S(1)}, u32[]{:S(2)}, u32[]{:S(2)}) collective-permute-start(f32[1,7,8,256]{3,2,1,0:T(8,128)S(1)} %get-tuple-element.26), channel_id=1, source_target_pairs={{0,2},{1,9},{16,18},{17,25},{32,34},{33,41},{48,50},{49,57},{64,66... | collective-permute-start | bytes 172040 | tf_op jit(solution)/shard_map/ppermute | solution.py:61
  73.9 4.5 %collective-permute-start.14 = (f32[1,7,8,256]{3,2,1,0:T(8,128)S(1)}, f32[1,7,8,256]{3,2,1,0:T(8,128)S(1)}, u32[]{:S(2)}, u32[]{:S(2)}) collective-permute-start(f32[1,7,8,256]{3,2,1,0:T(8,128)S(1)} %plain_sum.2.after_ref.refs_0_), channel_id=1, source_target_pairs={{0,16},{1,17},{16,0},{17,1},{32,48},{33,49},{48,32},{49,33},{64,80... | collective-permute-start | bytes 172040 | tf_op jit(solution)/shard_map/ppermute | solution.py:61
  78.4 17.9 %collective-permute-start.15 = (f32[1,7,8,256]{3,2,1,0:T(8,128)S(1)}, f32[1,7,8,256]{3,2,1,0:T(8,128)S(1)}, u32[]{:S(2)}, u32[]{:S(2)}) collective-permute-start(f32[1,7,8,256]{3,2,1,0:T(8,128)S(1)} %plain_sum.3.refs_0_), channel_id=1, source_target_pairs={{0,32},{1,33},{16,48},{17,49},{32,64},{33,65},{48,80},{49,81},{64,... | collective-permute-start | bytes 172040 | tf_op jit(solution)/shard_map/ppermute | solution.py:61
  81.6 15.4 %collective-permute-start.16 = (f32[1,7,8,256]{3,2,1,0:T(8,128)S(1)}, f32[1,7,8,256]{3,2,1,0:T(8,128)S(1)}, u32[]{:S(2)}, u32[]{:S(2)}) collective-permute-start(f32[1,7,8,256]{3,2,1,0:T(8,128)S(1)} %plain_sum.3.refs_0_), channel_id=1, source_target_pairs={{0,64},{1,65},{16,80},{17,81},{32,96},{33,97},{48,112},{49,113},{6... | collective-permute-start | bytes 172040 | tf_op jit(solution)/shard_map/ppermute | solution.py:61
  94.2 6.3 %collective-permute-start.17 = (f32[1,7,8,256]{3,2,1,0:T(8,128)S(1)}, f32[1,7,8,256]{3,2,1,0:T(8,128)S(1)}, u32[]{:S(2)}, u32[]{:S(2)}) collective-permute-start(f32[1,7,8,256]{3,2,1,0:T(8,128)S(1)} %plain_sum.3.refs_0_), channel_id=1, source_target_pairs={{0,96},{1,97},{16,112},{17,113},{32,0},{33,1},{48,16},{49,17},{64,... | collective-permute-start | bytes 172040 | tf_op jit(solution)/shard_map/ppermute | solution.py:61
  101.4 6.0 %collective-permute-start.18 = (f32[1,6,8,256]{3,2,1,0:T(8,128)S(1)}, f32[1,6,8,256]{3,2,1,0:T(8,128)S(1)}, u32[]{:S(2)}, u32[]{:S(2)}) collective-permute-start(f32[1,6,8,256]{3,2,1,0:T(8,128)S(1)} %update_probe.1.refs_0_), channel_id=1, source_target_pairs={{0,128},{1,5},{16,144},{17,21},{32,160},{33,37},{48,176},{49,53},{... | collective-permute-start | bytes 147464 | tf_op jit(solution)/shard_map/ppermute | solution.py:61
  102.4 7.0 %collective-permute-start.19 = (f32[1,6,8,256]{3,2,1,0:T(8,128)S(1)}, f32[1,6,8,256]{3,2,1,0:T(8,128)S(1)}, u32[]{:S(2)}, u32[]{:S(2)}) collective-permute-start(f32[1,6,8,256]{3,2,1,0:T(8,128)S(1)} %update_probe.1.refs_0_), channel_id=1, source_target_pairs={{0,2},{1,9},{16,18},{17,25},{32,34},{33,41},{48,50},{49,57},{64,66... | collective-permute-start | bytes 147464 | tf_op jit(solution)/shard_map/ppermute | solution.py:61
  106.8 4.1 %collective-permute-start.20 = (f32[1,6,8,256]{3,2,1,0:T(8,128)S(1)}, f32[1,6,8,256]{3,2,1,0:T(8,128)S(1)}, u32[]{:S(2)}, u32[]{:S(2)}) collective-permute-start(f32[1,6,8,256]{3,2,1,0:T(8,128)S(1)} %update_probe.1.refs_0_), channel_id=1, source_target_pairs={{0,130},{1,13},{16,146},{17,29},{32,162},{33,45},{48,178},{49,61},... | collective-permute-start | bytes 147464 | tf_op jit(solution)/shard_map/ppermute | solution.py:61
  110.9 6.4 %collective-permute-start.21 = (f32[4,6,8,256]{3,2,1,0:T(8,128)S(1)}, f32[4,6,8,256]{3,2,1,0:T(8,128)S(1)}, u32[]{:S(2)}, u32[]{:S(2)}) collective-permute-start(f32[4,6,8,256]{3,2,1,0:T(8,128)S(1)} %gather_parts.2.after_ref.refs_0_), channel_id=1, source_target_pairs={{0,4},{1,129},{16,20},{17,145},{32,36},{33,161},{48,52},{49,177},{... | collective-permute-start | bytes 589832 | tf_op jit(solution)/shard_map/ppermute | solution.py:61
  111.5 8.0 %collective-permute-start.22 = (f32[4,6,8,256]{3,2,1,0:T(8,128)S(1)}, f32[4,6,8,256]{3,2,1,0:T(8,128)S(1)}, u32[]{:S(2)}, u32[]{:S(2)}) collective-permute-start(f32[4,6,8,256]{3,2,1,0:T(8,128)S(1)} %gather_parts.2.after_ref.refs_0_), channel_id=1, source_target_pairs={{0,8},{1,3},{16,24},{17,19},{32,40},{33,35},{48,56},{49,51},{64,72... | collective-permute-start | bytes 589832 | tf_op jit(solution)/shard_map/ppermute | solution.py:61
  113.1 8.5 %collective-permute-start.23 = (f32[4,6,8,256]{3,2,1,0:T(8,128)S(1)}, f32[4,6,8,256]{3,2,1,0:T(8,128)S(1)}, u32[]{:S(2)}, u32[]{:S(2)}) collective-permute-start(f32[4,6,8,256]{3,2,1,0:T(8,128)S(1)} %gather_parts.2.after_ref.refs_0_), channel_id=1, source_target_pairs={{0,12},{1,131},{16,28},{17,147},{32,44},{33,163},{48,60},{49,179},... | collective-permute-start | bytes 589832 | tf_op jit(solution)/shard_map/ppermute | solution.py:61
  121.6 27.3 %collective-permute-start.24 = (f32[16,6,8,256]{3,2,1,0:T(8,128)S(1)}, f32[16,6,8,256]{3,2,1,0:T(8,128)S(1)}, u32[]{:S(2)}, u32[]{:S(2)}) collective-permute-start(f32[16,6,8,256]{3,2,1,0:T(8,128)S(1)} %gather_parts.3.mine_ref), channel_id=1, source_target_pairs={{0,1},{1,0},{16,17},{17,16},{32,33},{33,32},{48,49},{49,48},{64,65... | collective-permute-start | bytes 2359304 | tf_op jit(solution)/shard_map/ppermute | solution.py:61
  129.6 16.4 %collective-permute-start.11 = (f32[2,256,256]{2,1,0:T(8,128)}, f32[2,256,256]{2,1,0:T(8,128)}, u32[]{:S(2)}, u32[]{:S(2)}) collective-permute-start(f32[2,256,256]{2,1,0:T(8,128)} %add_corner.1), channel_id=1, source_target_pairs={{0,1},{1,2},{2,3},{3,4},{4,5},{5,6},{6,7},{7,8},{8,9},{9,10},{10,1... | collective-permute-start | bytes 1572872 | tf_op jit(solution)/shard_map/ppermute | solution.py:66
  133.2 7.7 %collective-permute-start.13 = (s32[8,2]{1,0:T(8,128)S(1)}, s32[8,2]{1,0:T(8,128)S(1)}, u32[]{:S(2)}, u32[]{:S(2)}) collective-permute-start(s32[8,2]{1,0:T(8,128)S(1)} %pad_add_fusion), channel_id=1, source_target_pairs={{0,1},{1,2},{2,3},{3,4},{4,5},{5,6},{6,7},{7,8},{8,9},{9,10},{10,1... | collective-permute-start | bytes 200 | tf_op jit(solution)/shard_map/ppermute | solution.py:66
  (14 other events, 117.9 us)

commit v3 on v2

--- a/solution.py
+++ b/solution.py
@@ -15,7 +15,7 @@
 PLANES = 2 * MODES + 1
 AXES = ("gx", "gy")
 SMALL = 16 * 1024 * 1024
-LARGE = 60 * 1024 * 1024
+LARGE = 40 * 1024 * 1024
 VMEM = pltpu.VMEM
 SMEM = pltpu.SMEM
 F32 = jnp.float32
@@ -37,12 +37,12 @@
     return pairs
 
 
-def first_ring(step):
-    return routes(lambda x, y, z, c: (x + step, y, z, c) if c == 0 else (x, y + step, z, c))
-
-
-def second_ring(step):
-    return routes(lambda x, y, z, c: (x, y + step, z, c) if c == 0 else (x + step, y, z, c))
+def x_ring(step):
+    return routes(lambda x, y, z, c: (x + step, y, z, c))
+
+
+def y_ring(step):
+    return routes(lambda x, y, z, c: (x, y + step, z, c))
 
 
 def depth_ring(step):
@@ -55,6 +55,16 @@
 
 def core_pair():
     return routes(lambda x, y, z, c: (x, y, z, 1 - c))
+
+
+def plane_groups():
+    return [
+        [flat_index(x, y, z, core) for x in range(4) for y in range(4)] for z in range(8) for core in range(2)
+    ]
+
+
+def swap_in_plane(value):
+    return lax.all_to_all(value, AXES, split_axis=0, concat_axis=0, tiled=True, axis_index_groups=plane_groups())
 
 
 def send(value, pairs):
@@ -151,13 +161,17 @@
         in_specs=[pl.BlockSpec(memory_space=pl.ANY), pl.BlockSpec(memory_space=VMEM)],
         out_specs=pl.BlockSpec(memory_space=VMEM),
         scratch_shapes=[VMEM((SLOTS, 2, SIDE, HALF), F32), pltpu.SemaphoreType.DMA((2,))],
-        compiler_params=pltpu.CompilerParams(vmem_limit_bytes=LARGE),
+        compiler_params=pltpu.CompilerParams(vmem_limit_bytes=SMALL),
         cost_estimate=pl.CostEstimate(flops=2_000_000_000, bytes_accessed=4_000_000, transcendentals=0),
         name="sort_amplitude",
     )(amplitude, order)
 
 
-def cover_kernel(place, counts, own, left, above, corner, probe, weight_out, doubled):
+def cover_kernel(place, counts, own, left, above, probe, weight_out, rows_out, doubled):
+    start = pl.multiple_of((place[2] * 16 + place[3] * 4 + place[4]) * 8, 8)
+    for mode in range(MODES):
+        for part in range(2):
+            rows_out[0, 2 * mode + part] = probe[mode, part, pl.ds(start, 8), :]
     coverage = probe[0, 0] * probe[0, 0]
     for mode in range(MODES):
         for part in range(2):
@@ -171,15 +185,15 @@
     row_iota = lax.broadcasted_iota(jnp.int32, (SIDE, SIDE), 0)
     lane_iota = lax.broadcasted_iota(jnp.int32, (SIDE, SIDE), 1)
     weight_out[...] = jnp.ones((SIDE, SIDE), F32)
-    for up, back, points in ((0, 0, own), (0, 1, left), (1, 0, above), (1, 1, corner)):
+    for up, back, points, skip in ((0, 0, own, 0), (0, 1, left, 0), (1, 0, above, 0), (1, 1, above, SLOTS)):
         tile_row = row_id - up
         tile_col = col_id - back
         inside = jnp.logical_and(tile_row >= 0, tile_col >= 0)
         count = jnp.where(inside, counts[jnp.maximum(tile_row, 0), jnp.maximum(tile_col, 0)], 0)
 
-        def visit(item, carry, points=points, tile_row=tile_row, tile_col=tile_col, up=up, back=back):
-            row_at = points[item, 0] - tile_row * SIDE
-            col_at = points[item, 1] - tile_col * SIDE
+        def visit(item, carry, points=points, skip=skip, tile_row=tile_row, tile_col=tile_col, up=up, back=back):
+            row_at = points[skip + item, 0] - tile_row * SIDE
+            col_at = points[skip + item, 1] - tile_col * SIDE
             window = pl.ds(SIDE - row_at, SIDE)
             moved = pltpu.roll(lanes(doubled[0, window, :], doubled[1, window, :]), col_at, 1)
             row_ok = row_iota < row_at if up else row_iota >= row_at
@@ -190,21 +204,24 @@
         lax.fori_loop(0, count, visit, 0)
 
 
-def cover(place, counts, own, left, above, corner, probe):
+def cover(place, counts, own, left, above, probe):
     return pl.pallas_call(
         cover_kernel,
-        out_shape=jax.ShapeDtypeStruct((SIDE, SIDE), F32),
-        in_specs=[pl.BlockSpec(memory_space=SMEM)] * 6 + [pl.BlockSpec(memory_space=VMEM)],
-        out_specs=pl.BlockSpec(memory_space=VMEM),
+        out_shape=(
+            jax.ShapeDtypeStruct((SIDE, SIDE), F32),
+            jax.ShapeDtypeStruct((1, PLANES - 1, 8, SIDE), F32),
+        ),
+        in_specs=[pl.BlockSpec(memory_space=SMEM)] * 5 + [pl.BlockSpec(memory_space=VMEM)],
+        out_specs=(pl.BlockSpec(memory_space=VMEM),) * 2,
         scratch_shapes=[VMEM((2, 2 * SIDE, HALF), F32)],
-        compiler_params=pltpu.CompilerParams(vmem_limit_bytes=LARGE),
+        compiler_params=pltpu.CompilerParams(vmem_limit_bytes=SMALL),
         cost_estimate=pl.CostEstimate(flops=2_000_000_000, bytes_accessed=4_000_000, transcendentals=0),
         name="cover",
-    )(place, counts, own, left, above, corner, probe)
+    )(place, counts, own, left, above, probe)
 
 
 def pattern_kernel(
-    place, counts, points, own, right, lower, corner, probe_in, amplitude_in, table_in,
+    place, counts, points, own, right, lower, corner, probe_in, amplitude_in, table_in, weight, old_rows,
     core_out, right_out, lower_out, send_out, keep_out,
     field, target, total, spectrum, probe, amplitude, table, sems,
 ):
@@ -323,14 +340,14 @@
         store.wait()
 
 
-def visit_patterns(place, counts, points, own, right, lower, corner, probe, amplitude, table):
+def visit_patterns(place, counts, points, own, right, lower, corner, probe, amplitude, table, *before):
     tile = jax.ShapeDtypeStruct((2, SIDE, SIDE), F32)
     tall = jax.ShapeDtypeStruct((2, 2 * SIDE, SIDE), F32)
     part = jax.ShapeDtypeStruct((16, PLANES, 8, SIDE), F32)
     return pl.pallas_call(
         pattern_kernel,
         out_shape=(tile, tall, tile, part, part),
-        in_specs=[pl.BlockSpec(memory_space=SMEM)] * 3 + [pl.BlockSpec(memory_space=pl.ANY)] * 7,
+        in_specs=[pl.BlockSpec(memory_space=SMEM)] * 3 + [pl.BlockSpec(memory_space=pl.ANY)] * 9,
         out_specs=(pl.BlockSpec(memory_space=pl.ANY),) * 5,
         scratch_shapes=[
             VMEM((2, 4, 2 * SIDE, HALF), F32),
@@ -345,7 +362,7 @@
         compiler_params=pltpu.CompilerParams(vmem_limit_bytes=LARGE),
         cost_estimate=pl.CostEstimate(flops=10_000_000_000, bytes_accessed=10_000_000, transcendentals=0),
         name="patterns",
-    )(place, counts, points, own, right, lower, corner, probe, amplitude, table)
+    )(place, counts, points, own, right, lower, corner, probe, amplitude, table, *before)
 
 
 def small_call(body, name, out_shape, operands, scalars=0, unread=0, **options):
@@ -364,6 +381,20 @@
     )(*operands)
 
 
+def plain_sum(pieces, *before):
+    number = len(pieces)
+
+    def body(*refs):
+        block = refs[0][...]
+        for piece in refs[1:number]:
+            block = block + piece[...]
+        refs[-1][...] = block
+
+    return small_call(
+        body, "plain_sum", jax.ShapeDtypeStruct(pieces[0].shape, F32), (*pieces, *before), unread=len(before)
+    )
+
+
 def scatter_sum(slot, place, pieces):
     length = pieces[0].shape[0] // 4
     shape = (length,) + pieces[0].shape[1:]
@@ -381,69 +412,37 @@
     return small_call(body, "scatter_sum", (jax.ShapeDtypeStruct(shape, F32),) * 4, (place, *pieces), scalars=1)
 
 
-def plain_sum(pieces):
+def update_probe(pieces, old, *before):
+    number = len(pieces)
+
     def body(*refs):
-        block = refs[0][...]
-        for piece in refs[1:-1]:
-            block = block + piece[...]
-        refs[-1][...] = block
-
-    return small_call(body, "plain_sum", jax.ShapeDtypeStruct(pieces[0].shape, F32), pieces)
-
-
-def update_probe(pieces, old):
-    def body(*refs):
-        old_ref, out = refs[-2:]
+        old_ref, out = refs[number], refs[-1]
         block = refs[0][0]
-        for piece in refs[1:-2]:
+        for piece in refs[1:number]:
             block = block + piece[0]
         scale = 1.0 / (block[PLANES - 1] + 1.0)
         for plane in range(PLANES - 1):
-            out[0, plane] = (old_ref[0, plane] + block[plane]) * scale
-
-    return small_call(body, "update_probe", jax.ShapeDtypeStruct(old.shape, F32), (*pieces, old))
-
-
-def own_rows(place, probe):
-    def body(place, probe_ref, out):
-        group = place[2] * 16 + place[3] * 4 + place[4]
-        for plane in range(PLANES - 1):
-            out[0, plane] = probe_ref[plane, group]
-
-    return pl.pallas_call(
-        body,
-        out_shape=jax.ShapeDtypeStruct((1, PLANES - 1, 8, SIDE), F32),
-        in_specs=[pl.BlockSpec(memory_space=SMEM), pl.BlockSpec(memory_space=VMEM)],
-        out_specs=pl.BlockSpec(memory_space=VMEM),
-        compiler_params=pltpu.CompilerParams(vmem_limit_bytes=LARGE),
-        name="own_rows",
-    )(place, probe.reshape(PLANES - 1, 32, 8, SIDE))
-
-
-def gather_parts(pieces):
-    length = pieces[0].shape[0]
-
-    def body(*refs):
-        for step, piece in enumerate(refs[:-1]):
-            refs[-1][pl.ds(step * length, length)] = piece[...]
-
-    shape = (4 * length,) + pieces[0].shape[1:]
-    return small_call(body, "gather_parts", jax.ShapeDtypeStruct(shape, F32), pieces)
+            new = (old_ref[0, plane] + block[plane]) * scale
+            for copy in range(16):
+                out[copy, plane] = new
+
+    return small_call(
+        body, "update_probe", jax.ShapeDtypeStruct((16,) + old.shape[1:], F32), (*pieces, old, *before),
+        unread=len(before),
+    )
 
 
 def join_halves(place, mine, other):
     def body(place, mine_ref, other_ref, out, sem):
-        core, first, second = place[2], place[3], place[4]
+        core = place[2]
         copies = []
-        for piece, half, outer, inner in (
-            (mine_ref, core, first, second), (other_ref, 1 - core, second, first)
-        ):
-            for one in range(4):
-                for two in range(4):
-                    group = half * 16 + lax.rem(outer + 4 - one, 4) * 4 + lax.rem(inner + 4 - two, 4)
-                    copies.append(
-                        pltpu.make_async_copy(piece.at[one * 4 + two], out.at[:, group], sem.at[len(copies)])
+        for piece, half in ((mine_ref, core), (other_ref, 1 - core)):
+            for plane in range(PLANES - 1):
+                copies.append(
+                    pltpu.make_async_copy(
+                        piece.at[:, plane], out.at[plane, pl.ds(half * 16, 16)], sem.at[len(copies)]
                     )
+                )
         for copy in copies:
             copy.start()
         for copy in copies:
@@ -454,32 +453,46 @@
         out_shape=jax.ShapeDtypeStruct((PLANES - 1, 32, 8, SIDE), F32),
         in_specs=[pl.BlockSpec(memory_space=SMEM)] + [pl.BlockSpec(memory_space=pl.ANY)] * 2,
         out_specs=pl.BlockSpec(memory_space=pl.ANY),
-        scratch_shapes=[pltpu.SemaphoreType.DMA((32,))],
+        scratch_shapes=[pltpu.SemaphoreType.DMA((12,))],
         compiler_params=pltpu.CompilerParams(vmem_limit_bytes=SMALL),
         name="join_halves",
     )(place, mine, other)
     return out.reshape(MODES, 2, SIDE, SIDE)
 
 
-def add_corner(lower, side, after):
-    def body(lower_ref, side_ref, after_ref, out):
-        out[...] = lower_ref[...] + side_ref[:, SIDE:, :]
+def after(value, *events):
+    def body(*refs):
+        pass
+
+    return pl.pallas_call(
+        body,
+        out_shape=jax.ShapeDtypeStruct(value.shape, value.dtype),
+        in_specs=[pl.BlockSpec(memory_space=pl.ANY)] * (1 + len(events)),
+        out_specs=pl.BlockSpec(memory_space=pl.ANY),
+        input_output_aliases={0: 0},
+        compiler_params=pltpu.CompilerParams(vmem_limit_bytes=SMALL),
+        name="after",
+    )(value, *events)
+
+
+def add_corner(lower, left, *before):
+    def body(lower_ref, left_ref, *refs):
+        refs[-1][...] = lower_ref[...] + left_ref[:, SIDE:, :]
 
     return small_call(
-        body, "add_corner", jax.ShapeDtypeStruct(lower.shape, F32), (lower, side, after), unread=1
+        body, "add_corner", jax.ShapeDtypeStruct(lower.shape, F32), (lower, left, *before), unread=len(before)
     )
 
 
-def update_object(own, core, side, above, weight, after):
-    def body(own_ref, core_ref, side_ref, above_ref, weight_ref, after_ref, out):
+def update_object(own, core, left, above, weight):
+    def body(own_ref, core_ref, left_ref, above_ref, weight_ref, out):
         scale = 1.0 / weight_ref[...]
         for part in range(2):
             block = own_ref[part] + core_ref[part]
-            out[part] = (block + side_ref[part, :SIDE, :] + above_ref[part]) * scale
+            out[part] = (block + left_ref[part, :SIDE, :] + above_ref[part]) * scale
 
     return small_call(
-        body, "update_object", jax.ShapeDtypeStruct(own.shape, F32),
-        (own, core, side, above, weight, after), unread=1,
+        body, "update_object", jax.ShapeDtypeStruct(own.shape, F32), (own, core, left, above, weight)
     )
 
 
@@ -489,9 +502,7 @@
     core = row_id % 2
     x_at = row_id // 4
     y_at = (row_id // 2) % 2 * 2 + col_id // 8
-    first = jnp.where(core == 0, x_at, y_at)
-    second = jnp.where(core == 0, y_at, x_at)
-    place = jnp.stack([row_id, col_id, core, first, second]).astype(jnp.int32)
+    place = jnp.stack([row_id, col_id, core, x_at, y_at]).astype(jnp.int32)
     table = jnp.asarray(transform_tables())
     order = jnp.asarray(order_table())
 
@@ -500,27 +511,27 @@
     lower_strip = shifted(object_field, "gy", -1)
     points_left = shifted(points, "gx", 1)
     amplitude = sort_amplitude(amplitudes[0, 0], order)
-    old_rows = own_rows(place, probe)
     points_pair = shifted(jnp.concatenate([points, points_left], 0), "gy", 1)
+    right_strip = after(right_strip, amplitude, points_pair, place)
     diagonal = shifted(right_strip, "gy", -1)
-    weight = cover(place, counts, points, points_left, points_pair[:SLOTS], points_pair[SLOTS:], probe)
+    weight, old_rows = cover(place, counts, points, points_left, points_pair, probe)
     core_grad, side_grad, lower_grad, other_half, half = visit_patterns(
-        place, counts, points, object_field, right_strip, lower_strip, diagonal, probe, amplitude, table
+        place, counts, points, object_field, right_strip, lower_strip, diagonal, probe, amplitude, table,
+        weight, old_rows,
     )
 
     half_in = send(other_half, core_pair())
     from_left = shifted(side_grad, "gx", 1)
     parts = scatter_sum(3, place, [half, half_in])
-    arrived = [send(parts[step], first_ring(step)) for step in (1, 2, 3)]
+    arrived = [send(parts[step], x_ring(step)) for step in (1, 2, 3)]
     parts = scatter_sum(4, place, [parts[0]] + arrived)
-    arrived = [send(parts[step], second_ring(step)) for step in (1, 2, 3)]
+    arrived = [send(parts[step], y_ring(step)) for step in (1, 2, 3)]
     block = plain_sum([parts[0]] + arrived)
     from_above = shifted(add_corner(lower_grad, from_left, block), "gy", 1)
     block = plain_sum([block, send(block, depth_pair())])
-    chunk = update_probe([block] + [send(block, depth_ring(step)) for step in (2, 4, 6)], old_rows)
-    chunk = gather_parts([chunk] + [send(chunk, second_ring(step)) for step in (1, 2, 3)])
-    new_object = update_object(object_field, core_grad, from_left, from_above, weight, chunk)
-    chunk = gather_parts([chunk] + [send(chunk, first_ring(step)) for step in (1, 2, 3)])
+    fours = [send(block, depth_ring(step)) for step in (2, 4, 6)]
+    chunk = swap_in_plane(update_probe([block] + fours, old_rows, from_above))
+    new_object = update_object(object_field, core_grad, from_left, from_above, weight)
     new_probe = join_halves(place, chunk, send(chunk, core_pair()))
     return (new_object, new_probe)
 

time: 152 us -> 127 us (0.84)
  the two profiles are of different devices: /device:TPU:70 before, /device:TPU:1 now
where the time goes in v3:
time: 127 us; the launch traced here: 126 us
  waiting for transfers between devices  43.8 us (34%)
  starting transfers between devices  34.4 us (27%)
  Pallas kernels  22.3 us (18%)
  blocking collectives  22 us (17%)
  local copies, waits for them, and re-layouts  3 us (2%)
    ppermute x12, waiting for transfers between devices, send(): return lax.ppermute(value, AXES, pairs)  31.9 us
    all_to_all x1, blocking collectives, swap_in_plane(): lax.all_to_all(value, AXES, split_axis=0, concat_axis=0, tiled=True, axis...  22 us
    ppermute x7, starting transfers between devices, shifted(): lax.ppermute(value, axis, [(source, (source + steps) % count) for source...  17.2 us
    ppermute x12, starting transfers between devices, send(): return lax.ppermute(value, AXES, pairs)  17.2 us
    pallas_call x1, Pallas kernels, visit_patterns(): pl.pallas_call(pattern_kernel, out_shape=(tile, tall, tile, part, part),...  15.6 us
    ppermute x7, waiting for transfers between devices, shifted(): lax.ppermute(value, axis, [(source, (source + steps) % count) for source...  11.9 us
  transfers between devices with their start and end apart: 19, of which 14 were waited for; matrix products, arithmetic and copies ran while one was open for 1% of the time, Pallas kernels for 4%

profile of v3, /device:TPU:1, one launch (start us, length us, event | category | flops | bytes accessed | tf_op | source)
XLA Modules:
  0.0 126.4 jit_solution(10312827744128139562)
XLA Ops:
  0.6 7.5 %collective-permute-start = (f32[2,256,256]{2,1,0:T(8,128)}, f32[2,256,256]{2,1,0:T(8,128)S(1)}, u32[]{:S(2)}, u32[]{:S(2)}) collective-permute-start(f32[2,256,256]{2,1,0:T(8,128)} %own_ref.1), channel_id=1, source_target_pairs={{0,240},{16,0},{32,16},{48,32},{64,48},{80,64},{96,80},{112,96},{1... | collective-permute-start | bytes 1572872 | tf_op jit(solution)/shard_map/ppermute | solution.py:76
  12.7 1.7 %collective-permute-done.1.left = s32[4,2]{1,0:T(4,128)S(1)} collective-permute-done((s32[4,2]{1,0:T(4,128)S(1)}, s32[4,2]{1,0:T(4,128)S(1)}, u32[]{:S(2)}, u32[]{:S(2)}) %collective-permute-start.1) | collective-permute-done | bytes 64 | tf_op jit(solution)/shard_map/ppermute | solution.py:76
  14.4 3.7 %collective-permute-start.2 = (s32[8,2]{1,0:T(8,128)S(1)}, s32[8,2]{1,0:T(8,128)S(1)}, u32[]{:S(2)}, u32[]{:S(2)}) collective-permute-start(s32[8,2]{1,0:T(8,128)S(1)} %pad_add_fusion), channel_id=1, source_target_pairs={{0,1},{1,2},{2,3},{3,4},{4,5},{5,6},{6,7},{7,8},{8,9},{9,10},{10,1... | collective-permute-start | bytes 200 | tf_op jit(solution)/shard_map/ppermute | solution.py:76
  18.2 2.3 %collective-permute-done.2.refs_2_.above = s32[8,2]{1,0:T(8,128)S(1)} collective-permute-done((s32[8,2]{1,0:T(8,128)S(1)}, s32[8,2]{1,0:T(8,128)S(1)}, u32[]{:S(2)}, u32[]{:S(2)}) %collective-permute-start.2) | collective-permute-done | bytes 96 | tf_op jit(solution)/shard_map/ppermute | solution.py:76
  20.5 2.8 %collective-permute-done.refs_0_ = f32[2,256,256]{2,1,0:T(8,128)S(1)} collective-permute-done((f32[2,256,256]{2,1,0:T(8,128)}, f32[2,256,256]{2,1,0:T(8,128)S(1)}, u32[]{:S(2)}, u32[]{:S(2)}) %collective-permute-start) | collective-permute-done | bytes 524320 | tf_op jit(solution)/shard_map/ppermute | solution.py:76
  23.4 3.2 %collective-permute-start.4 = (f32[2,256,256]{2,1,0:T(8,128)S(1)}, f32[2,256,256]{2,1,0:T(8,128)S(1)}, u32[]{:S(2)}, u32[]{:S(2)}) collective-permute-start(f32[2,256,256]{2,1,0:T(8,128)S(1)} %after.1.right), channel_id=1, source_target_pairs={{0,15},{1,0},{2,1},{3,2},{4,3},{5,4},{6,5},{7,6},{8,7},{9,8},{10,9... | collective-permute-start | bytes 1572872 | tf_op jit(solution)/shard_map/ppermute | solution.py:76
  26.6 1.9 %cover.1 = (f32[256,256]{1,0:T(8,128)S(1)}, f32[1,6,8,256]{3,2,1,0:T(8,128)S(1)}) custom-call(s32[5]{0:T(128)S(1)} %stack.23.refs_3_.place, s32[16,16]{1,0:T(8,128)S(1)} %copy-done.3, s32[4,2]{1,0:T(4,128)S(1)} %copy.22.own.points, s32[4,2]{1,0:T(4,128)S(1)} %collective-permute-done.1.left, s32[8,2]{1,0:T(8,128)S(1)} %collective-permute-done.2.refs_2_.above, ...), custom_call_target="tpu_custom_call" | custom-call | flops 2000000000 | bytes 4000000 | tf_op jit(solution)/shard_map/cover/pallas_call | solution.py:208
  28.5 5.0 %collective-permute-done.4.corner = f32[2,256,256]{2,1,0:T(8,128)S(1)} collective-permute-done((f32[2,256,256]{2,1,0:T(8,128)S(1)}, f32[2,256,256]{2,1,0:T(8,128)S(1)}, u32[]{:S(2)}, u32[]{:S(2)}) %collective-permute-start.4) | collective-permute-done | bytes 524320 | tf_op jit(solution)/shard_map/ppermute | solution.py:76
  33.5 15.6 %patterns.1 = (f32[2,256,256]{2,1,0:T(8,128)S(1)}, f32[2,512,256]{2,1,0:T(8,128)S(1)}, f32[2,256,256]{2,1,0:T(8,128)S(1)}, f32[16,7,8,256]{3,2,1,0:T(8,128)S(1)}, f32[16,7,8,256]{3,2,1,0:T(8,128)S(1)}) custom-call(s32[5]{0:T(128)S(1)} %stack.23.refs_3_.place, s32[16,16]{1,0:T(8,128)S(1)} %copy-done.3, s32[4,2]{1,0:T(4,128)S(1)} %copy.22.own.points, ...), custom_call_target="tpu_custom_call" | custom-call | flops 10000000000 | bytes 10000000 | tf_op jit(solution)/shard_map/patterns/pallas_call | solution.py:347
  49.2 1.8 %collective-permute-start.5 = (f32[2,512,256]{2,1,0:T(8,128)S(1)}, f32[2,512,256]{2,1,0:T(8,128)S(1)}, u32[]{:S(2)}, u32[]{:S(2)}) collective-permute-start(f32[2,512,256]{2,1,0:T(8,128)S(1)} %get-tuple-element.20), channel_id=1, source_target_pairs={{0,16},{16,32},{32,48},{48,64},{64,80},{80,96},{96,112},{112,128},... | collective-permute-start | bytes 3145736 | tf_op jit(solution)/shard_map/ppermute | solution.py:76
  52.4 5.6 %collective-permute-start.7 = (f32[4,7,8,256]{3,2,1,0:T(8,128)S(1)}, f32[4,7,8,256]{3,2,1,0:T(8,128)S(1)}, u32[]{:S(2)}, u32[]{:S(2)}) collective-permute-start(f32[4,7,8,256]{3,2,1,0:T(8,128)S(1)} %get-tuple-element.25), channel_id=1, source_target_pairs={{0,4},{1,5},{16,20},{17,21},{32,36},{33,37},{48,52},{49,53},{64,68... | collective-permute-start | bytes 688136 | tf_op jit(solution)/shard_map/ppermute | solution.py:71
  57.9 3.1 %collective-permute-start.8 = (f32[4,7,8,256]{3,2,1,0:T(8,128)S(1)}, f32[4,7,8,256]{3,2,1,0:T(8,128)S(1)}, u32[]{:S(2)}, u32[]{:S(2)}) collective-permute-start(f32[4,7,8,256]{3,2,1,0:T(8,128)S(1)} %get-tuple-element.26), channel_id=1, source_target_pairs={{0,8},{1,9},{16,24},{17,25},{32,40},{33,41},{48,56},{49,57},{64,72... | collective-permute-start | bytes 688136 | tf_op jit(solution)/shard_map/ppermute | solution.py:71
  61.0 4.7 %collective-permute-done.7.refs_1_ = f32[4,7,8,256]{3,2,1,0:T(8,128)S(1)} collective-permute-done((f32[4,7,8,256]{3,2,1,0:T(8,128)S(1)}, f32[4,7,8,256]{3,2,1,0:T(8,128)S(1)}, u32[]{:S(2)}, u32[]{:S(2)}) %collective-permute-start.7) | collective-permute-done | bytes 229408 | tf_op jit(solution)/shard_map/ppermute | solution.py:71
  65.7 5.9 %collective-permute-done.8.refs_2_ = f32[4,7,8,256]{3,2,1,0:T(8,128)S(1)} collective-permute-done((f32[4,7,8,256]{3,2,1,0:T(8,128)S(1)}, f32[4,7,8,256]{3,2,1,0:T(8,128)S(1)}, u32[]{:S(2)}, u32[]{:S(2)}) %collective-permute-start.8) | collective-permute-done | bytes 229408 | tf_op jit(solution)/shard_map/ppermute | solution.py:71
  72.2 2.4 %collective-permute-start.11 = (f32[1,7,8,256]{3,2,1,0:T(8,128)S(1)}, f32[1,7,8,256]{3,2,1,0:T(8,128)S(1)}, u32[]{:S(2)}, u32[]{:S(2)}) collective-permute-start(f32[1,7,8,256]{3,2,1,0:T(8,128)S(1)} %get-tuple-element.30), channel_id=1, source_target_pairs={{0,2},{1,3},{16,18},{17,19},{32,34},{33,35},{48,50},{49,51},{64,66... | collective-permute-start | bytes 172040 | tf_op jit(solution)/shard_map/ppermute | solution.py:71
  74.7 1.6 %collective-permute-start.12 = (f32[1,7,8,256]{3,2,1,0:T(8,128)S(1)}, f32[1,7,8,256]{3,2,1,0:T(8,128)S(1)}, u32[]{:S(2)}, u32[]{:S(2)}) collective-permute-start(f32[1,7,8,256]{3,2,1,0:T(8,128)S(1)} %get-tuple-element.31), channel_id=1, source_target_pairs={{0,130},{1,131},{16,146},{17,147},{32,162},{33,163},{48,178},{49,1... | collective-permute-start | bytes 172040 | tf_op jit(solution)/shard_map/ppermute | solution.py:71
  76.2 3.7 %collective-permute-done.10.refs_1_ = f32[1,7,8,256]{3,2,1,0:T(8,128)S(1)} collective-permute-done((f32[1,7,8,256]{3,2,1,0:T(8,128)S(1)}, f32[1,7,8,256]{3,2,1,0:T(8,128)S(1)}, u32[]{:S(2)}, u32[]{:S(2)}) %collective-permute-start.10) | collective-permute-done | bytes 57376 | tf_op jit(solution)/shard_map/ppermute | solution.py:71
  80.0 6.0 %collective-permute-done.11.refs_2_ = f32[1,7,8,256]{3,2,1,0:T(8,128)S(1)} collective-permute-done((f32[1,7,8,256]{3,2,1,0:T(8,128)S(1)}, f32[1,7,8,256]{3,2,1,0:T(8,128)S(1)}, u32[]{:S(2)}, u32[]{:S(2)}) %collective-permute-start.11) | collective-permute-done | bytes 57376 | tf_op jit(solution)/shard_map/ppermute | solution.py:71
  86.3 3.0 %collective-permute-done.14.refs_1_ = f32[1,7,8,256]{3,2,1,0:T(8,128)S(1)} collective-permute-done((f32[1,7,8,256]{3,2,1,0:T(8,128)S(1)}, f32[1,7,8,256]{3,2,1,0:T(8,128)S(1)}, u32[]{:S(2)}, u32[]{:S(2)}) %collective-permute-start.14) | collective-permute-done | bytes 57376 | tf_op jit(solution)/shard_map/ppermute | solution.py:71
  89.5 2.3 %collective-permute-start.15 = (f32[1,7,8,256]{3,2,1,0:T(8,128)S(1)}, f32[1,7,8,256]{3,2,1,0:T(8,128)S(1)}, u32[]{:S(2)}, u32[]{:S(2)}) collective-permute-start(f32[1,7,8,256]{3,2,1,0:T(8,128)S(1)} %plain_sum.3.refs_0_), channel_id=1, source_target_pairs={{0,32},{1,33},{16,48},{17,49},{32,64},{33,65},{48,80},{49,81},{64,... | collective-permute-start | bytes 172040 | tf_op jit(solution)/shard_map/ppermute | solution.py:71
  91.8 4.6 %collective-permute-done.17.refs_3_ = f32[1,7,8,256]{3,2,1,0:T(8,128)S(1)} collective-permute-done((f32[1,7,8,256]{3,2,1,0:T(8,128)S(1)}, f32[1,7,8,256]{3,2,1,0:T(8,128)S(1)}, u32[]{:S(2)}, u32[]{:S(2)}) %collective-permute-start.17) | collective-permute-done | bytes 57376 | tf_op jit(solution)/shard_map/ppermute | solution.py:71
  98.8 22.0 %all_to_all.5.mine_ref = f32[16,6,8,256]{3,2,1,0:T(8,128)S(1)} all-to-all(f32[16,6,8,256]{3,2,1,0:T(8,128)S(1)} %update_probe.1), channel_id=1, replica_groups={{0,128,2,130,4,132,6,134,8,136,10,138,12,140,14,142},{1,129,3,131,5,133..., dimensions={0} | all-to-all | bytes 1572864 | tf_op jit(solution)/shard_map/all_to_all | solution.py:67
  120.8 1.8 %collective-permute-start.18 = (f32[16,6,8,256]{3,2,1,0:T(8,128)S(1)}, f32[16,6,8,256]{3,2,1,0:T(8,128)S(1)}, u32[]{:S(2)}, u32[]{:S(2)}) collective-permute-start(f32[16,6,8,256]{3,2,1,0:T(8,128)S(1)} %all_to_all.5.mine_ref), channel_id=1, source_target_pairs={{0,1},{1,0},{16,17},{17,16},{32,33},{33,32},{48,49},{49,48},{64,65... | collective-permute-start | bytes 2359304 | tf_op jit(solution)/shard_map/ppermute | solution.py:71
  124.5 1.8 %join_halves.1 = f32[6,32,8,256]{3,2,1,0:T(8,128)} custom-call(s32[5]{0:T(128)S(1)} %stack.23.refs_3_.place, f32[16,6,8,256]{3,2,1,0:T(8,128)S(1)} %all_to_all.5.mine_ref, f32[16,6,8,256]{3,2,1,0:T(8,128)S(1)} %collective-permute-done.18.other_ref), custom_call_target="tpu_custom_call" | custom-call | tf_op jit(solution)/shard_map/join_halves/pallas_call | solution.py:451
  (42 shorter events, 11.5 us)
Async XLA Ops:
  0.6 22.8 %collective-permute-start = (f32[2,256,256]{2,1,0:T(8,128)}, f32[2,256,256]{2,1,0:T(8,128)S(1)}, u32[]{:S(2)}, u32[]{:S(2)}) collective-permute-start(f32[2,256,256]{2,1,0:T(8,128)} %own_ref.1), channel_id=1, source_target_pairs={{0,240},{16,0},{32,16},{48,32},{64,48},{80,64},{96,80},{112,96},{1... | collective-permute-start | bytes 1572872 | tf_op jit(solution)/shard_map/ppermute | solution.py:76
  8.1 20.4 %collective-permute-start.3 = (f32[2,256,256]{2,1,0:T(8,128)}, f32[2,256,256]{2,1,0:T(8,128)}, u32[]{:S(2)}, u32[]{:S(2)}) collective-permute-start(f32[2,256,256]{2,1,0:T(8,128)} %own_ref.1), channel_id=1, source_target_pairs={{0,15},{1,0},{2,1},{3,2},{4,3},{5,4},{6,5},{7,6},{8,7},{9,8},{10,9... | collective-permute-start | bytes 1572872 | tf_op jit(solution)/shard_map/ppermute | solution.py:76
  9.8 4.6 %collective-permute-start.1 = (s32[4,2]{1,0:T(4,128)S(1)}, s32[4,2]{1,0:T(4,128)S(1)}, u32[]{:S(2)}, u32[]{:S(2)}) collective-permute-start(s32[4,2]{1,0:T(4,128)S(1)} %copy.22.own.points), channel_id=1, source_target_pairs={{0,16},{16,32},{32,48},{48,64},{64,80},{80,96},{96,112},{112,128},... | collective-permute-start | bytes 104 | tf_op jit(solution)/shard_map/ppermute | solution.py:76
  9.8 1.2 copy-start.2
  12.7 14.0 %copy-start.1 = (f32[3,2,256,256]{3,2,1,0:T(8,128)S(1)}, f32[3,2,256,256]{3,2,1,0:T(8,128)}, u32[]{:S(2)}) copy-start(f32[3,2,256,256]{3,2,1,0:T(8,128)} %probe_in.1) | copy-start | bytes 4718596
  12.7 13.9 %copy-start.3 = (s32[16,16]{1,0:T(8,128)S(1)}, s32[16,16]{1,0:T(8,128)}, u32[]{:S(2)}) copy-start(s32[16,16]{1,0:T(8,128)} %counts.3) | copy-start | bytes 3076
  14.4 6.1 %collective-permute-start.2 = (s32[8,2]{1,0:T(8,128)S(1)}, s32[8,2]{1,0:T(8,128)S(1)}, u32[]{:S(2)}, u32[]{:S(2)}) collective-permute-start(s32[8,2]{1,0:T(8,128)S(1)} %pad_add_fusion), channel_id=1, source_target_pairs={{0,1},{1,2},{2,3},{3,4},{4,5},{5,6},{6,7},{7,8},{8,9},{9,10},{10,1... | collective-permute-start | bytes 200 | tf_op jit(solution)/shard_map/ppermute | solution.py:76
  23.4 10.1 %copy-start = (f32[2,256,256]{2,1,0:T(8,128)S(1)}, f32[2,256,256]{2,1,0:T(8,128)}, u32[]{:S(2)}) copy-start(f32[2,256,256]{2,1,0:T(8,128)} %own_ref.1) | copy-start | bytes 1572868
  23.4 10.1 %copy-start.4 = (bf16[8,256,256]{2,1,0:T(8,128)(2,1)S(1)}, bf16[8,256,256]{2,1,0:T(8,128)(2,1)}, u32[]{:S(2)}) copy-start(bf16[8,256,256]{2,1,0:T(8,128)(2,1)} %constant.59.clone.table_in) | copy-start | bytes 3145732
  23.4 10.1 %collective-permute-start.4 = (f32[2,256,256]{2,1,0:T(8,128)S(1)}, f32[2,256,256]{2,1,0:T(8,128)S(1)}, u32[]{:S(2)}, u32[]{:S(2)}) collective-permute-start(f32[2,256,256]{2,1,0:T(8,128)S(1)} %after.1.right), channel_id=1, source_target_pairs={{0,15},{1,0},{2,1},{3,2},{4,3},{5,4},{6,5},{7,6},{8,7},{9,8},{10,9... | collective-permute-start | bytes 1572872 | tf_op jit(solution)/shard_map/ppermute | solution.py:76
  49.1 2.6 %collective-permute-start.6 = (f32[16,7,8,256]{3,2,1,0:T(8,128)S(1)}, f32[16,7,8,256]{3,2,1,0:T(8,128)S(1)}, u32[]{:S(2)}, u32[]{:S(2)}) collective-permute-start(f32[16,7,8,256]{3,2,1,0:T(8,128)S(1)} %get-tuple-element.23), channel_id=1, source_target_pairs={{0,1},{1,0},{16,17},{17,16},{32,33},{33,32},{48,49},{49,48},{64,65... | collective-permute-start | bytes 2752520 | tf_op jit(solution)/shard_map/ppermute | solution.py:71
  49.2 36.8 %collective-permute-start.5 = (f32[2,512,256]{2,1,0:T(8,128)S(1)}, f32[2,512,256]{2,1,0:T(8,128)S(1)}, u32[]{:S(2)}, u32[]{:S(2)}) collective-permute-start(f32[2,512,256]{2,1,0:T(8,128)S(1)} %get-tuple-element.20), channel_id=1, source_target_pairs={{0,16},{16,32},{32,48},{48,64},{64,80},{80,96},{96,112},{112,128},... | collective-permute-start | bytes 3145736 | tf_op jit(solution)/shard_map/ppermute | solution.py:76
  52.4 13.3 %collective-permute-start.7 = (f32[4,7,8,256]{3,2,1,0:T(8,128)S(1)}, f32[4,7,8,256]{3,2,1,0:T(8,128)S(1)}, u32[]{:S(2)}, u32[]{:S(2)}) collective-permute-start(f32[4,7,8,256]{3,2,1,0:T(8,128)S(1)} %get-tuple-element.25), channel_id=1, source_target_pairs={{0,4},{1,5},{16,20},{17,21},{32,36},{33,37},{48,52},{49,53},{64,68... | collective-permute-start | bytes 688136 | tf_op jit(solution)/shard_map/ppermute | solution.py:71
  57.9 13.6 %collective-permute-start.8 = (f32[4,7,8,256]{3,2,1,0:T(8,128)S(1)}, f32[4,7,8,256]{3,2,1,0:T(8,128)S(1)}, u32[]{:S(2)}, u32[]{:S(2)}) collective-permute-start(f32[4,7,8,256]{3,2,1,0:T(8,128)S(1)} %get-tuple-element.26), channel_id=1, source_target_pairs={{0,8},{1,9},{16,24},{17,25},{32,40},{33,41},{48,56},{49,57},{64,72... | collective-permute-start | bytes 688136 | tf_op jit(solution)/shard_map/ppermute | solution.py:71
  61.0 10.5 %collective-permute-start.9 = (f32[4,7,8,256]{3,2,1,0:T(8,128)S(1)}, f32[4,7,8,256]{3,2,1,0:T(8,128)S(1)}, u32[]{:S(2)}, u32[]{:S(2)}) collective-permute-start(f32[4,7,8,256]{3,2,1,0:T(8,128)S(1)} %get-tuple-element.27), channel_id=1, source_target_pairs={{0,12},{1,13},{16,28},{17,29},{32,44},{33,45},{48,60},{49,61},{64,... | collective-permute-start | bytes 688136 | tf_op jit(solution)/shard_map/ppermute | solution.py:71
  72.1 7.8 %collective-permute-start.10 = (f32[1,7,8,256]{3,2,1,0:T(8,128)S(1)}, f32[1,7,8,256]{3,2,1,0:T(8,128)S(1)}, u32[]{:S(2)}, u32[]{:S(2)}) collective-permute-start(f32[1,7,8,256]{3,2,1,0:T(8,128)S(1)} %get-tuple-element.29), channel_id=1, source_target_pairs={{0,128},{1,129},{16,144},{17,145},{32,160},{33,161},{48,176},{49,1... | collective-permute-start | bytes 172040 | tf_op jit(solution)/shard_map/ppermute | solution.py:71
  72.2 13.8 %collective-permute-start.11 = (f32[1,7,8,256]{3,2,1,0:T(8,128)S(1)}, f32[1,7,8,256]{3,2,1,0:T(8,128)S(1)}, u32[]{:S(2)}, u32[]{:S(2)}) collective-permute-start(f32[1,7,8,256]{3,2,1,0:T(8,128)S(1)} %get-tuple-element.30), channel_id=1, source_target_pairs={{0,2},{1,3},{16,18},{17,19},{32,34},{33,35},{48,50},{49,51},{64,66... | collective-permute-start | bytes 172040 | tf_op jit(solution)/shard_map/ppermute | solution.py:71
  74.7 11.4 %collective-permute-start.12 = (f32[1,7,8,256]{3,2,1,0:T(8,128)S(1)}, f32[1,7,8,256]{3,2,1,0:T(8,128)S(1)}, u32[]{:S(2)}, u32[]{:S(2)}) collective-permute-start(f32[1,7,8,256]{3,2,1,0:T(8,128)S(1)} %get-tuple-element.31), channel_id=1, source_target_pairs={{0,130},{1,131},{16,146},{17,147},{32,162},{33,163},{48,178},{49,1... | collective-permute-start | bytes 172040 | tf_op jit(solution)/shard_map/ppermute | solution.py:71
  86.1 12.6 %collective-permute-start.13 = (f32[2,256,256]{2,1,0:T(8,128)S(1)}, f32[2,256,256]{2,1,0:T(8,128)S(1)}, u32[]{:S(2)}, u32[]{:S(2)}) collective-permute-start(f32[2,256,256]{2,1,0:T(8,128)S(1)} %add_corner.1), channel_id=1, source_target_pairs={{0,1},{1,2},{2,3},{3,4},{4,5},{5,6},{6,7},{7,8},{8,9},{9,10},{10,1... | collective-permute-start | bytes 1572872 | tf_op jit(solution)/shard_map/ppermute | solution.py:76
  86.2 3.1 %collective-permute-start.14 = (f32[1,7,8,256]{3,2,1,0:T(8,128)S(1)}, f32[1,7,8,256]{3,2,1,0:T(8,128)S(1)}, u32[]{:S(2)}, u32[]{:S(2)}) collective-permute-start(f32[1,7,8,256]{3,2,1,0:T(8,128)S(1)} %plain_sum.2.refs_0_), channel_id=1, source_target_pairs={{0,16},{1,17},{16,0},{17,1},{32,48},{33,49},{48,32},{49,33},{64,80... | collective-permute-start | bytes 172040 | tf_op jit(solution)/shard_map/ppermute | solution.py:71
  89.3 7.1 %collective-permute-start.17 = (f32[1,7,8,256]{3,2,1,0:T(8,128)S(1)}, f32[1,7,8,256]{3,2,1,0:T(8,128)S(1)}, u32[]{:S(2)}, u32[]{:S(2)}) collective-permute-start(f32[1,7,8,256]{3,2,1,0:T(8,128)S(1)} %plain_sum.3.refs_0_), channel_id=1, source_target_pairs={{0,96},{1,97},{16,112},{17,113},{32,0},{33,1},{48,16},{49,17},{64,... | collective-permute-start | bytes 172040 | tf_op jit(solution)/shard_map/ppermute | solution.py:71
  89.4 7.9 %collective-permute-start.16 = (f32[1,7,8,256]{3,2,1,0:T(8,128)S(1)}, f32[1,7,8,256]{3,2,1,0:T(8,128)S(1)}, u32[]{:S(2)}, u32[]{:S(2)}) collective-permute-start(f32[1,7,8,256]{3,2,1,0:T(8,128)S(1)} %plain_sum.3.refs_0_), channel_id=1, source_target_pairs={{0,64},{1,65},{16,80},{17,81},{32,96},{33,97},{48,112},{49,113},{6... | collective-permute-start | bytes 172040 | tf_op jit(solution)/shard_map/ppermute | solution.py:71
  89.5 9.2 %collective-permute-start.15 = (f32[1,7,8,256]{3,2,1,0:T(8,128)S(1)}, f32[1,7,8,256]{3,2,1,0:T(8,128)S(1)}, u32[]{:S(2)}, u32[]{:S(2)}) collective-permute-start(f32[1,7,8,256]{3,2,1,0:T(8,128)S(1)} %plain_sum.3.refs_0_), channel_id=1, source_target_pairs={{0,32},{1,33},{16,48},{17,49},{32,64},{33,65},{48,80},{49,81},{64,... | collective-permute-start | bytes 172040 | tf_op jit(solution)/shard_map/ppermute | solution.py:71
  120.8 3.7 %collective-permute-start.18 = (f32[16,6,8,256]{3,2,1,0:T(8,128)S(1)}, f32[16,6,8,256]{3,2,1,0:T(8,128)S(1)}, u32[]{:S(2)}, u32[]{:S(2)}) collective-permute-start(f32[16,6,8,256]{3,2,1,0:T(8,128)S(1)} %all_to_all.5.mine_ref), channel_id=1, source_target_pairs={{0,1},{1,0},{16,17},{17,16},{32,33},{33,32},{48,49},{49,48},{64,65... | collective-permute-start | bytes 2359304 | tf_op jit(solution)/shard_map/ppermute | solution.py:71
  (1 other events, 0.9 us)

commit v4 on v3

--- a/solution.py
+++ b/solution.py
@@ -112,14 +112,27 @@
     return jnp.dot(left, right, preferred_element_type=F32)
 
 
-def apply_right(value, table, which):
-    high, low = split(value)
-    return dot(low, table[which]) + dot(high, table[which + 1]) + dot(high, table[which])
-
-
-def apply_left(table, which, value):
-    high, low = split(value)
-    return dot(table[which], low) + dot(table[which + 1], high) + dot(table[which], high)
+STEP = 64
+LAG = 6
+
+
+def add_split(parts, even, odd):
+    for index, value in enumerate((even, odd)):
+        high, low = split(value)
+        parts[2 * index].append(high)
+        parts[2 * index + 1].append(low)
+
+
+def run_staggered(chains):
+    step = 0
+    while chains:
+        for index, chain in enumerate(list(chains)):
+            if chain is not None and step >= index * LAG:
+                if next(chain, "end") == "end":
+                    chains[index] = None
+        step += 1
+        if all(chain is None for chain in chains):
+            return
 
 
 def lanes(*parts):
@@ -221,7 +234,7 @@
 
 
 def pattern_kernel(
-    place, counts, points, own, right, lower, corner, probe_in, amplitude_in, table_in, weight, old_rows,
+    place, counts, points, own, right_real, right_imag, lower, corner_real, corner_imag, probe_in, amplitude_in, table_in, weight, old_rows,
     core_out, right_out, lower_out, send_out, keep_out,
     field, target, total, spectrum, probe, amplitude, table, sems,
 ):
@@ -229,12 +242,16 @@
     col_id = place[1]
     core = place[2]
     loads = []
-    for piece, up, back in ((own, 0, 0), (right, 0, 1), (lower, 1, 0), (corner, 1, 1)):
+    for piece, part, length, up, back in (
+        (own, 0, 2, 0, 0), (lower, 0, 2, 1, 0),
+        (right_real, 0, 1, 0, 1), (right_imag, 1, 1, 0, 1),
+        (corner_real, 0, 1, 1, 1), (corner_imag, 1, 1, 1, 1),
+    ):
         for block in range(2):
             loads.append(
                 pltpu.make_async_copy(
                     piece.at[:, :, pl.ds(block * HALF, HALF)],
-                    field.at[:, 2 * back + block, pl.ds(up * SIDE, SIDE), :],
+                    field.at[pl.ds(part, length), 2 * back + block, pl.ds(up * SIDE, SIDE), :],
                     sems.at[len(loads)],
                 )
             )
@@ -265,52 +282,104 @@
         density = object_real * object_real + object_imag * object_imag
         total[:, PLANES - 1] += density.reshape(32, 8, SIDE)
 
-        even_sum = jnp.zeros((HALF, SIDE), F32)
-        odd_sum = jnp.zeros((HALF, SIDE), F32)
-        for mode in range(MODES):
+        sums = {}
+
+        def forward(mode):
             probe_real = probe[mode, 0]
             probe_imag = probe[mode, 1]
-            real = probe_real * object_real - probe_imag * object_imag
-            imag = probe_real * object_imag + probe_imag * object_real
-            even = apply_right(
-                lanes(real[:, :HALF] + real[:, HALF:], imag[:, :HALF] + imag[:, HALF:]), table, 0
-            )
-            odd = apply_right(
-                lanes(real[:, :HALF] - real[:, HALF:], imag[:, :HALF] - imag[:, HALF:]), table, 4
-            )
-            real = lanes(even[:, :HALF], odd[:, :HALF])
-            imag = lanes(even[:, HALF:], odd[:, HALF:])
-            even = apply_left(table, 2, rows(real[:HALF] + real[HALF:], imag[:HALF] + imag[HALF:]))
-            odd = apply_left(table, 6, rows(real[:HALF] - real[HALF:], imag[:HALF] - imag[HALF:]))
-            spectrum[mode, 0] = even
-            spectrum[mode, 1] = odd
-            even_sum += even[:HALF] * even[:HALF] + even[HALF:] * even[HALF:]
-            odd_sum += odd[:HALF] * odd[:HALF] + odd[HALF:] * odd[HALF:]
-        even_factor = amplitude[item, :HALF] / jnp.maximum(jnp.sqrt(even_sum), 0.5)
-        odd_factor = amplitude[item, HALF:] / jnp.maximum(jnp.sqrt(odd_sum), 0.5)
-        even_factor = rows(even_factor, even_factor)
-        odd_factor = rows(odd_factor, odd_factor)
-        grad_real = jnp.zeros((SIDE, SIDE), F32)
-        grad_imag = jnp.zeros((SIDE, SIDE), F32)
-        for mode in range(MODES):
-            even = apply_left(table, 0, spectrum[mode, 0] * even_factor)
-            odd = apply_left(table, 4, spectrum[mode, 1] * odd_factor)
-            high = even + odd
-            low = even - odd
-            real = rows(high[:HALF], low[:HALF])
-            imag = rows(high[HALF:], low[HALF:])
-            even = apply_right(lanes(real[:, :HALF], imag[:, :HALF]), table, 2)
-            odd = apply_right(lanes(real[:, HALF:], imag[:, HALF:]), table, 6)
-            high = even + odd
-            low = even - odd
-            real = lanes(high[:, :HALF], low[:, :HALF])
-            imag = lanes(high[:, HALF:], low[:, HALF:])
-            probe_real = probe[mode, 0]
-            probe_imag = probe[mode, 1]
-            grad_real += probe_real * real + probe_imag * imag
-            grad_imag += probe_real * imag - probe_imag * real
-            total[:, 2 * mode] += (object_real * real + object_imag * imag).reshape(32, 8, SIDE)
-            total[:, 2 * mode + 1] += (object_real * imag - object_imag * real).reshape(32, 8, SIDE)
+            parts = [[], [], [], []]
+            for at in range(0, SIDE, STEP):
+                cut_rows = slice(at, at + STEP)
+                p_real, p_imag = probe_real[cut_rows], probe_imag[cut_rows]
+                o_real, o_imag = object_real[cut_rows], object_imag[cut_rows]
+                real = p_real * o_real - p_imag * o_imag
+                imag = p_real * o_imag + p_imag * o_real
+                both = lanes(real[:, :HALF], imag[:, :HALF]), lanes(real[:, HALF:], imag[:, HALF:])
+                add_split(parts, both[0] + both[1], both[0] - both[1])
+                yield
+            high, low, odd_high, odd_low = [rows(*part) for part in parts]
+            even = dot(lanes(low, high, high), rows(table[0], table[1], table[0]))
+            yield
+            odd = dot(lanes(odd_low, odd_high, odd_high), rows(table[4], table[5], table[4]))
+            yield
+            parts = [[], [], [], []]
+            for lane in (slice(0, HALF), slice(HALF, SIDE)):
+                for at in range(0, HALF, STEP // 2):
+                    top, bottom = slice(at, at + STEP // 2), slice(HALF + at, HALF + at + STEP // 2)
+                    first = lanes(even[top, lane], odd[top, lane])
+                    second = lanes(even[bottom, lane], odd[bottom, lane])
+                    add_split(parts, first + second, first - second)
+                    yield
+            high, low, odd_high, odd_low = [rows(*part) for part in parts]
+            even = dot(lanes(table[2], table[3], table[2]), rows(low, high, high))
+            yield
+            odd = dot(lanes(table[6], table[7], table[6]), rows(odd_low, odd_high, odd_high))
+            yield
+            for index, values in enumerate((even, odd)):
+                spectrum[mode, index] = values
+                power = values[:HALF] * values[:HALF] + values[HALF:] * values[HALF:]
+                sums[index] = sums[index] + power if index in sums else power
+                yield
+
+        run_staggered([forward(mode) for mode in range(MODES)])
+        factors = []
+        for index in range(2):
+            factor = amplitude[item, index * HALF : index * HALF + HALF] * lax.rsqrt(jnp.maximum(sums[index], 0.25))
+            factors.append(rows(factor, factor))
+        grads = []
+
+        def backward(mode):
+            halves = []
+            for index in range(2):
+                parts = [[], []]
+                for at in range(0, SIDE, STEP):
+                    cut_rows = slice(at, at + STEP)
+                    value = spectrum[mode, index, pl.ds(at, STEP), :] * factors[index][cut_rows]
+                    high, low = split(value)
+                    parts[0].append(high)
+                    parts[1].append(low)
+                    yield
+                halves.append([rows(*part) for part in parts])
+            (high, low), (odd_high, odd_low) = halves
+            even = dot(lanes(table[0], table[1], table[0]), rows(low, high, high))
+            yield
+            odd = dot(lanes(table[4], table[5], table[4]), rows(odd_low, odd_high, odd_high))
+            yield
+            parts = [[], [], [], []]
+            for sign in (1, -1):
+                for at in range(0, HALF, STEP // 2):
+                    real, imag = slice(at, at + STEP // 2), slice(HALF + at, HALF + at + STEP // 2)
+                    if sign == 1:
+                        first, second = even[real] + odd[real], even[imag] + odd[imag]
+                    else:
+                        first, second = even[real] - odd[real], even[imag] - odd[imag]
+                    add_split(
+                        parts, lanes(first[:, :HALF], second[:, :HALF]), lanes(first[:, HALF:], second[:, HALF:])
+                    )
+                    yield
+            high, low, odd_high, odd_low = [rows(*part) for part in parts]
+            even = dot(lanes(low, high, high), rows(table[2], table[3], table[2]))
+            yield
+            odd = dot(lanes(odd_low, odd_high, odd_high), rows(table[6], table[7], table[6]))
+            yield
+            pieces = []
+            for at in range(0, SIDE, STEP):
+                cut_rows = slice(at, at + STEP)
+                first, second = even[cut_rows] + odd[cut_rows], even[cut_rows] - odd[cut_rows]
+                real = lanes(first[:, :HALF], second[:, :HALF])
+                imag = lanes(first[:, HALF:], second[:, HALF:])
+                p_real, p_imag = probe[mode, 0, pl.ds(at, STEP), :], probe[mode, 1, pl.ds(at, STEP), :]
+                o_real, o_imag = object_real[cut_rows], object_imag[cut_rows]
+                pieces.append((p_real * real + p_imag * imag, p_real * imag - p_imag * real))
+                groups = pl.ds(at // 8, STEP // 8)
+                total[groups, 2 * mode] += (o_real * real + o_imag * imag).reshape(STEP // 8, 8, SIDE)
+                total[groups, 2 * mode + 1] += (o_real * imag - o_imag * real).reshape(STEP // 8, 8, SIDE)
+                yield
+            grads.append([rows(*[piece[part] for piece in pieces]) for part in range(2)])
+
+        run_staggered([backward(mode) for mode in range(MODES)])
+        grad_real = grads[0][0] + grads[1][0] + grads[2][0]
+        grad_imag = grads[0][1] + grads[1][1] + grads[2][1]
         for part, grad in ((0, grad_real), (1, grad_imag)):
             moved = pltpu.roll(grad, col_at, 1)
             first = jnp.where(in_left, moved, 0.0)
@@ -347,7 +416,7 @@
     return pl.pallas_call(
         pattern_kernel,
         out_shape=(tile, tall, tile, part, part),
-        in_specs=[pl.BlockSpec(memory_space=SMEM)] * 3 + [pl.BlockSpec(memory_space=pl.ANY)] * 9,
+        in_specs=[pl.BlockSpec(memory_space=SMEM)] * 3 + [pl.BlockSpec(memory_space=pl.ANY)] * 11,
         out_specs=(pl.BlockSpec(memory_space=pl.ANY),) * 5,
         scratch_shapes=[
             VMEM((2, 4, 2 * SIDE, HALF), F32),
@@ -357,12 +426,12 @@
             VMEM(probe.shape, F32),
             VMEM(amplitude.shape, F32),
             VMEM(table.shape, BF16),
-            pltpu.SemaphoreType.DMA((11,)),
+            pltpu.SemaphoreType.DMA((15,)),
         ],
         compiler_params=pltpu.CompilerParams(vmem_limit_bytes=LARGE),
         cost_estimate=pl.CostEstimate(flops=10_000_000_000, bytes_accessed=10_000_000, transcendentals=0),
         name="patterns",
-    )(place, counts, points, own, right, lower, corner, probe, amplitude, table, *before)
+    )(place, counts, points, own, *right, lower, *corner, probe, amplitude, table, *before)
 
 
 def small_call(body, name, out_shape, operands, scalars=0, unread=0, **options):
@@ -507,13 +576,13 @@
     order = jnp.asarray(order_table())
 
     points = positions[0, 0]
-    right_strip = shifted(object_field, "gx", -1)
+    right_strip = [shifted(object_field[part : part + 1], "gx", -1) for part in range(2)]
     lower_strip = shifted(object_field, "gy", -1)
     points_left = shifted(points, "gx", 1)
     amplitude = sort_amplitude(amplitudes[0, 0], order)
     points_pair = shifted(jnp.concatenate([points, points_left], 0), "gy", 1)
-    right_strip = after(right_strip, amplitude, points_pair, place)
-    diagonal = shifted(right_strip, "gy", -1)
+    right_strip[0] = after(right_strip[0], amplitude, points_pair, place)
+    diagonal = [shifted(strip, "gy", -1) for strip in right_strip]
     weight, old_rows = cover(place, counts, points, points_left, points_pair, probe)
     core_grad, side_grad, lower_grad, other_half, half = visit_patterns(
         place, counts, points, object_field, right_strip, lower_strip, diagonal, probe, amplitude, table,

time: 127 us -> 122 us (0.961)
  waiting for transfers between devices: 43.8 us -> 35.5 us
  starting transfers between devices: 34.4 us -> 38.8 us
  blocking collectives: 22 us -> 20.2 us
    ppermute x7 -> x9, waiting for transfers between devices: 11.9 us -> 1.77 us  [shifted(): lax.ppermute(value, axis, [(source, (source + steps) % count) for source...]
    ppermute x7 -> x9, starting transfers between devices: 17.2 us -> 23.2 us  [shifted(): lax.ppermute(value, axis, [(source, (source + steps) % count) for source...]
    ppermute x12, waiting for transfers between devices: 31.9 us -> 33.7 us  [send(): return lax.ppermute(value, AXES, pairs)]
    all_to_all x1, blocking collectives: 22 us -> 20.2 us  [swap_in_plane(): lax.all_to_all(value, AXES, split_axis=0, concat_axis=0, tiled=True, axis...]
    ppermute x12, starting transfers between devices: 17.2 us -> 15.7 us  [send(): return lax.ppermute(value, AXES, pairs)]
  transfers between devices with their start and end apart: 19 -> 21, of which waited for: 14 -> 11; matrix products, arithmetic and copies ran while one was open for 1% -> 1% of each run, Pallas kernels for 4% -> 4%
where the time goes in v4:
time: 122 us
  starting transfers between devices  38.8 us (32%)
  waiting for transfers between devices  35.5 us (29%)
  Pallas kernels  22.9 us (19%)
  blocking collectives  20.2 us (17%)
  local copies, waits for them, and re-layouts  4.06 us (3%)
    ppermute x12, waiting for transfers between devices, send(): return lax.ppermute(value, AXES, pairs)  33.7 us
    ppermute x9, starting transfers between devices, shifted(): lax.ppermute(value, axis, [(source, (source + steps) % count) for source...  23.2 us
    all_to_all x1, blocking collectives, swap_in_plane(): lax.all_to_all(value, AXES, split_axis=0, concat_axis=0, tiled=True, axis...  20.2 us
    pallas_call x1, Pallas kernels, visit_patterns(): pl.pallas_call(pattern_kernel, out_shape=(tile, tall, tile, part, part),...  15.9 us
    ppermute x12, starting transfers between devices, send(): return lax.ppermute(value, AXES, pairs)  15.7 us
  transfers between devices with their start and end apart: 21, of which 11 were waited for; matrix products, arithmetic and copies ran while one was open for 1% of the time, Pallas kernels for 4%

profile of v4, /device:TPU:1, one launch (start us, length us, event | category | flops | bytes accessed | tf_op | source)
XLA Modules:
  0.0 122.4 jit_solution(1683791724573613816)
XLA Ops:
  1.4 2.5 %collective-permute-start.1 = (s32[4,2]{1,0:T(4,128)S(1)}, s32[4,2]{1,0:T(4,128)S(1)}, u32[]{:S(2)}, u32[]{:S(2)}) collective-permute-start(s32[4,2]{1,0:T(4,128)S(1)} %copy.22.own.points), channel_id=1, source_target_pairs={{0,16},{16,32},{32,48},{48,64},{64,80},{80,96},{96,112},{112,128},... | collective-permute-start | bytes 104 | tf_op jit(solution)/shard_map/ppermute | solution.py:76
  5.9 4.8 %collective-permute-start.3 = (f32[1,256,256]{2,1,0:T(8,128)S(1)}, f32[1,256,256]{2,1,0:T(8,128)S(1)}, u32[]{:S(2)}, u32[]{:S(2)}) collective-permute-start(f32[1,256,256]{2,1,0:T(8,128)S(1)} %get-tuple-element.32), channel_id=1, source_target_pairs={{0,240},{16,0},{32,16},{48,32},{64,48},{80,64},{96,80},{112,96},{1... | collective-permute-start | bytes 786440 | tf_op jit(solution)/shard_map/ppermute | solution.py:76
  10.6 1.7 %collective-permute-start = (f32[1,256,256]{2,1,0:T(8,128)S(1)}, f32[1,256,256]{2,1,0:T(8,128)S(1)}, u32[]{:S(2)}, u32[]{:S(2)}) collective-permute-start(f32[1,256,256]{2,1,0:T(8,128)S(1)} %get-tuple-element.33), channel_id=1, source_target_pairs={{0,240},{16,0},{32,16},{48,32},{64,48},{80,64},{96,80},{112,96},{1... | collective-permute-start | bytes 786440 | tf_op jit(solution)/shard_map/ppermute | solution.py:76
  12.5 1.2 copy-done.2
  15.3 3.5 %collective-permute-start.2 = (s32[8,2]{1,0:T(8,128)S(1)}, s32[8,2]{1,0:T(8,128)S(1)}, u32[]{:S(2)}, u32[]{:S(2)}) collective-permute-start(s32[8,2]{1,0:T(8,128)S(1)} %pad_add_fusion), channel_id=1, source_target_pairs={{0,1},{1,2},{2,3},{3,4},{4,5},{5,6},{6,7},{7,8},{8,9},{9,10},{10,1... | collective-permute-start | bytes 200 | tf_op jit(solution)/shard_map/ppermute | solution.py:76
  18.9 5.5 %collective-permute-start.6 = (f32[1,256,256]{2,1,0:T(8,128)S(1)}, f32[1,256,256]{2,1,0:T(8,128)S(1)}, u32[]{:S(2)}, u32[]{:S(2)}) collective-permute-start(f32[1,256,256]{2,1,0:T(8,128)S(1)} %collective-permute-done.3.right_imag), channel_id=1, source_target_pairs={{0,15},{1,0},{2,1},{3,2},{4,3},{5,4},{6,5},{7,6},{8,7},{9,8},{10,9... | collective-permute-start | bytes 786440 | tf_op jit(solution)/shard_map/ppermute | solution.py:76
  24.4 3.4 %collective-permute-start.5 = (f32[1,256,256]{2,1,0:T(8,128)S(1)}, f32[1,256,256]{2,1,0:T(8,128)S(1)}, u32[]{:S(2)}, u32[]{:S(2)}) collective-permute-start(f32[1,256,256]{2,1,0:T(8,128)S(1)} %after.1.right_real), channel_id=1, source_target_pairs={{0,15},{1,0},{2,1},{3,2},{4,3},{5,4},{6,5},{7,6},{8,7},{9,8},{10,9... | collective-permute-start | bytes 786440 | tf_op jit(solution)/shard_map/ppermute | solution.py:76
  27.8 2.2 %cover.1 = (f32[256,256]{1,0:T(8,128)S(1)}, f32[1,6,8,256]{3,2,1,0:T(8,128)S(1)}) custom-call(s32[5]{0:T(128)S(1)} %stack.23.refs_3_.place, s32[16,16]{1,0:T(8,128)S(1)} %copy-done.3, s32[4,2]{1,0:T(4,128)S(1)} %copy.22.own.points, s32[4,2]{1,0:T(4,128)S(1)} %collective-permute-done.1.left, s32[8,2]{1,0:T(8,128)S(1)} %collective-permute-done.2.refs_2_.above, ...), custom_call_target="tpu_custom_call" | custom-call | flops 2000000000 | bytes 4000000 | tf_op jit(solution)/shard_map/cover/pallas_call | solution.py:221
  30.0 1.7 %collective-permute-done.5.corner_real = f32[1,256,256]{2,1,0:T(8,128)S(1)} collective-permute-done((f32[1,256,256]{2,1,0:T(8,128)S(1)}, f32[1,256,256]{2,1,0:T(8,128)S(1)}, u32[]{:S(2)}, u32[]{:S(2)}) %collective-permute-start.5) | collective-permute-done | bytes 262176 | tf_op jit(solution)/shard_map/ppermute | solution.py:76
  31.7 15.9 %patterns.1 = (f32[2,256,256]{2,1,0:T(8,128)S(1)}, f32[2,512,256]{2,1,0:T(8,128)S(1)}, f32[2,256,256]{2,1,0:T(8,128)S(1)}, f32[16,7,8,256]{3,2,1,0:T(8,128)S(1)}, f32[16,7,8,256]{3,2,1,0:T(8,128)S(1)}) custom-call(s32[5]{0:T(128)S(1)} %stack.23.refs_3_.place, s32[16,16]{1,0:T(8,128)S(1)} %copy-done.3, s32[4,2]{1,0:T(4,128)S(1)} %copy.22.own.points, ...), custom_call_target="tpu_custom_call" | custom-call | flops 10000000000 | bytes 10000000 | tf_op jit(solution)/shard_map/patterns/pallas_call | solution.py:416
  47.8 2.4 %collective-permute-done.8.refs_1_ = f32[16,7,8,256]{3,2,1,0:T(8,128)S(1)} collective-permute-done((f32[16,7,8,256]{3,2,1,0:T(8,128)S(1)}, f32[16,7,8,256]{3,2,1,0:T(8,128)S(1)}, u32[]{:S(2)}, u32[]{:S(2)}) %collective-permute-start.8) | collective-permute-done | bytes 917536 | tf_op jit(solution)/shard_map/ppermute | solution.py:71
  51.9 3.9 %collective-permute-start.10 = (f32[4,7,8,256]{3,2,1,0:T(8,128)S(1)}, f32[4,7,8,256]{3,2,1,0:T(8,128)S(1)}, u32[]{:S(2)}, u32[]{:S(2)}) collective-permute-start(f32[4,7,8,256]{3,2,1,0:T(8,128)S(1)} %get-tuple-element.26), channel_id=1, source_target_pairs={{0,8},{1,9},{16,24},{17,25},{32,40},{33,41},{48,56},{49,57},{64,72... | collective-permute-start | bytes 688136 | tf_op jit(solution)/shard_map/ppermute | solution.py:71
  56.4 4.1 %collective-permute-done.9.refs_1_ = f32[4,7,8,256]{3,2,1,0:T(8,128)S(1)} collective-permute-done((f32[4,7,8,256]{3,2,1,0:T(8,128)S(1)}, f32[4,7,8,256]{3,2,1,0:T(8,128)S(1)}, u32[]{:S(2)}, u32[]{:S(2)}) %collective-permute-start.9) | collective-permute-done | bytes 229408 | tf_op jit(solution)/shard_map/ppermute | solution.py:71
  60.5 5.9 %collective-permute-done.10.refs_2_ = f32[4,7,8,256]{3,2,1,0:T(8,128)S(1)} collective-permute-done((f32[4,7,8,256]{3,2,1,0:T(8,128)S(1)}, f32[4,7,8,256]{3,2,1,0:T(8,128)S(1)}, u32[]{:S(2)}, u32[]{:S(2)}) %collective-permute-start.10) | collective-permute-done | bytes 229408 | tf_op jit(solution)/shard_map/ppermute | solution.py:71
  67.0 3.3 %collective-permute-start.13 = (f32[1,7,8,256]{3,2,1,0:T(8,128)S(1)}, f32[1,7,8,256]{3,2,1,0:T(8,128)S(1)}, u32[]{:S(2)}, u32[]{:S(2)}) collective-permute-start(f32[1,7,8,256]{3,2,1,0:T(8,128)S(1)} %get-tuple-element.30), channel_id=1, source_target_pairs={{0,2},{1,3},{16,18},{17,19},{32,34},{33,35},{48,50},{49,51},{64,66... | collective-permute-start | bytes 172040 | tf_op jit(solution)/shard_map/ppermute | solution.py:71
  71.2 5.1 %collective-permute-done.12.refs_1_ = f32[1,7,8,256]{3,2,1,0:T(8,128)S(1)} collective-permute-done((f32[1,7,8,256]{3,2,1,0:T(8,128)S(1)}, f32[1,7,8,256]{3,2,1,0:T(8,128)S(1)}, u32[]{:S(2)}, u32[]{:S(2)}) %collective-permute-start.12) | collective-permute-done | bytes 57376 | tf_op jit(solution)/shard_map/ppermute | solution.py:71
  76.3 4.7 %collective-permute-done.13.refs_2_ = f32[1,7,8,256]{3,2,1,0:T(8,128)S(1)} collective-permute-done((f32[1,7,8,256]{3,2,1,0:T(8,128)S(1)}, f32[1,7,8,256]{3,2,1,0:T(8,128)S(1)}, u32[]{:S(2)}, u32[]{:S(2)}) %collective-permute-start.13) | collective-permute-done | bytes 57376 | tf_op jit(solution)/shard_map/ppermute | solution.py:71
  81.9 3.6 %collective-permute-done.16.refs_1_ = f32[1,7,8,256]{3,2,1,0:T(8,128)S(1)} collective-permute-done((f32[1,7,8,256]{3,2,1,0:T(8,128)S(1)}, f32[1,7,8,256]{3,2,1,0:T(8,128)S(1)}, u32[]{:S(2)}, u32[]{:S(2)}) %collective-permute-start.16) | collective-permute-done | bytes 57376 | tf_op jit(solution)/shard_map/ppermute | solution.py:71
  85.7 2.3 %collective-permute-start.17 = (f32[1,7,8,256]{3,2,1,0:T(8,128)S(1)}, f32[1,7,8,256]{3,2,1,0:T(8,128)S(1)}, u32[]{:S(2)}, u32[]{:S(2)}) collective-permute-start(f32[1,7,8,256]{3,2,1,0:T(8,128)S(1)} %plain_sum.3.refs_0_), channel_id=1, source_target_pairs={{0,32},{1,33},{16,48},{17,49},{32,64},{33,65},{48,80},{49,81},{64,... | collective-permute-start | bytes 172040 | tf_op jit(solution)/shard_map/ppermute | solution.py:71
  88.0 4.5 %collective-permute-done.19.refs_3_ = f32[1,7,8,256]{3,2,1,0:T(8,128)S(1)} collective-permute-done((f32[1,7,8,256]{3,2,1,0:T(8,128)S(1)}, f32[1,7,8,256]{3,2,1,0:T(8,128)S(1)}, u32[]{:S(2)}, u32[]{:S(2)}) %collective-permute-start.19) | collective-permute-done | bytes 57376 | tf_op jit(solution)/shard_map/ppermute | solution.py:71
  93.2 1.8 %collective-permute-done.17.refs_1_ = f32[1,7,8,256]{3,2,1,0:T(8,128)S(1)} collective-permute-done((f32[1,7,8,256]{3,2,1,0:T(8,128)S(1)}, f32[1,7,8,256]{3,2,1,0:T(8,128)S(1)}, u32[]{:S(2)}, u32[]{:S(2)}) %collective-permute-start.17) | collective-permute-done | bytes 57376 | tf_op jit(solution)/shard_map/ppermute | solution.py:71
  95.0 20.2 %all_to_all.5.mine_ref = f32[16,6,8,256]{3,2,1,0:T(8,128)S(1)} all-to-all(f32[16,6,8,256]{3,2,1,0:T(8,128)S(1)} %update_probe.1), channel_id=1, replica_groups={{0,128,2,130,4,132,6,134,8,136,10,138,12,140,14,142},{1,129,3,131,5,133..., dimensions={0} | all-to-all | bytes 1572864 | tf_op jit(solution)/shard_map/all_to_all | solution.py:67
  115.2 3.3 %collective-permute-start.20 = (f32[16,6,8,256]{3,2,1,0:T(8,128)S(1)}, f32[16,6,8,256]{3,2,1,0:T(8,128)S(1)}, u32[]{:S(2)}, u32[]{:S(2)}) collective-permute-start(f32[16,6,8,256]{3,2,1,0:T(8,128)S(1)} %all_to_all.5.mine_ref), channel_id=1, source_target_pairs={{0,1},{1,0},{16,17},{17,16},{32,33},{33,32},{48,49},{49,48},{64,65... | collective-permute-start | bytes 2359304 | tf_op jit(solution)/shard_map/ppermute | solution.py:71
  120.5 1.8 %join_halves.1 = f32[6,32,8,256]{3,2,1,0:T(8,128)} custom-call(s32[5]{0:T(128)S(1)} %stack.23.refs_3_.place, f32[16,6,8,256]{3,2,1,0:T(8,128)S(1)} %all_to_all.5.mine_ref, f32[16,6,8,256]{3,2,1,0:T(8,128)S(1)} %collective-permute-done.20.other_ref), custom_call_target="tpu_custom_call" | custom-call | tf_op jit(solution)/shard_map/join_halves/pallas_call | solution.py:520
  (47 shorter events, 12.2 us)
Async XLA Ops:
  1.4 13.9 %collective-permute-start.1 = (s32[4,2]{1,0:T(4,128)S(1)}, s32[4,2]{1,0:T(4,128)S(1)}, u32[]{:S(2)}, u32[]{:S(2)}) collective-permute-start(s32[4,2]{1,0:T(4,128)S(1)} %copy.22.own.points), channel_id=1, source_target_pairs={{0,16},{16,32},{32,48},{48,64},{64,80},{80,96},{96,112},{112,128},... | collective-permute-start | bytes 104 | tf_op jit(solution)/shard_map/ppermute | solution.py:76
  3.9 26.1 %collective-permute-start.4 = (f32[2,256,256]{2,1,0:T(8,128)}, f32[2,256,256]{2,1,0:T(8,128)S(1)}, u32[]{:S(2)}, u32[]{:S(2)}) collective-permute-start(f32[2,256,256]{2,1,0:T(8,128)} %own_ref.1), channel_id=1, source_target_pairs={{0,15},{1,0},{2,1},{3,2},{4,3},{5,4},{6,5},{7,6},{8,7},{9,8},{10,9... | collective-permute-start | bytes 1572872 | tf_op jit(solution)/shard_map/ppermute | solution.py:76
  5.9 13.0 %collective-permute-start.3 = (f32[1,256,256]{2,1,0:T(8,128)S(1)}, f32[1,256,256]{2,1,0:T(8,128)S(1)}, u32[]{:S(2)}, u32[]{:S(2)}) collective-permute-start(f32[1,256,256]{2,1,0:T(8,128)S(1)} %get-tuple-element.32), channel_id=1, source_target_pairs={{0,240},{16,0},{32,16},{48,32},{64,48},{80,64},{96,80},{112,96},{1... | collective-permute-start | bytes 786440 | tf_op jit(solution)/shard_map/ppermute | solution.py:76
  10.6 13.7 %collective-permute-start = (f32[1,256,256]{2,1,0:T(8,128)S(1)}, f32[1,256,256]{2,1,0:T(8,128)S(1)}, u32[]{:S(2)}, u32[]{:S(2)}) collective-permute-start(f32[1,256,256]{2,1,0:T(8,128)S(1)} %get-tuple-element.33), channel_id=1, source_target_pairs={{0,240},{16,0},{32,16},{48,32},{64,48},{80,64},{96,80},{112,96},{1... | collective-permute-start | bytes 786440 | tf_op jit(solution)/shard_map/ppermute | solution.py:76
  15.3 12.5 %copy-start.1 = (f32[3,2,256,256]{3,2,1,0:T(8,128)S(1)}, f32[3,2,256,256]{3,2,1,0:T(8,128)}, u32[]{:S(2)}) copy-start(f32[3,2,256,256]{3,2,1,0:T(8,128)} %probe_in.1) | copy-start | bytes 4718596
  15.3 12.5 %copy-start.3 = (s32[16,16]{1,0:T(8,128)S(1)}, s32[16,16]{1,0:T(8,128)}, u32[]{:S(2)}) copy-start(s32[16,16]{1,0:T(8,128)} %counts.3) | copy-start | bytes 3076
  15.3 9.0 %collective-permute-start.2 = (s32[8,2]{1,0:T(8,128)S(1)}, s32[8,2]{1,0:T(8,128)S(1)}, u32[]{:S(2)}, u32[]{:S(2)}) collective-permute-start(s32[8,2]{1,0:T(8,128)S(1)} %pad_add_fusion), channel_id=1, source_target_pairs={{0,1},{1,2},{2,3},{3,4},{4,5},{5,6},{6,7},{7,8},{8,9},{9,10},{10,1... | collective-permute-start | bytes 200 | tf_op jit(solution)/shard_map/ppermute | solution.py:76
  18.9 11.1 %collective-permute-start.6 = (f32[1,256,256]{2,1,0:T(8,128)S(1)}, f32[1,256,256]{2,1,0:T(8,128)S(1)}, u32[]{:S(2)}, u32[]{:S(2)}) collective-permute-start(f32[1,256,256]{2,1,0:T(8,128)S(1)} %collective-permute-done.3.right_imag), channel_id=1, source_target_pairs={{0,15},{1,0},{2,1},{3,2},{4,3},{5,4},{6,5},{7,6},{8,7},{9,8},{10,9... | collective-permute-start | bytes 786440 | tf_op jit(solution)/shard_map/ppermute | solution.py:76
  24.3 7.4 %copy-start = (f32[2,256,256]{2,1,0:T(8,128)S(1)}, f32[2,256,256]{2,1,0:T(8,128)}, u32[]{:S(2)}) copy-start(f32[2,256,256]{2,1,0:T(8,128)} %own_ref.1) | copy-start | bytes 1572868
  24.4 7.4 %collective-permute-start.5 = (f32[1,256,256]{2,1,0:T(8,128)S(1)}, f32[1,256,256]{2,1,0:T(8,128)S(1)}, u32[]{:S(2)}, u32[]{:S(2)}) collective-permute-start(f32[1,256,256]{2,1,0:T(8,128)S(1)} %after.1.right_real), channel_id=1, source_target_pairs={{0,15},{1,0},{2,1},{3,2},{4,3},{5,4},{6,5},{7,6},{8,7},{9,8},{10,9... | collective-permute-start | bytes 786440 | tf_op jit(solution)/shard_map/ppermute | solution.py:76
  47.6 2.6 %collective-permute-start.8 = (f32[16,7,8,256]{3,2,1,0:T(8,128)S(1)}, f32[16,7,8,256]{3,2,1,0:T(8,128)S(1)}, u32[]{:S(2)}, u32[]{:S(2)}) collective-permute-start(f32[16,7,8,256]{3,2,1,0:T(8,128)S(1)} %get-tuple-element.23), channel_id=1, source_target_pairs={{0,1},{1,0},{16,17},{17,16},{32,33},{33,32},{48,49},{49,48},{64,65... | collective-permute-start | bytes 2752520 | tf_op jit(solution)/shard_map/ppermute | solution.py:71
  47.7 33.3 %collective-permute-start.7 = (f32[2,512,256]{2,1,0:T(8,128)S(1)}, f32[2,512,256]{2,1,0:T(8,128)S(1)}, u32[]{:S(2)}, u32[]{:S(2)}) collective-permute-start(f32[2,512,256]{2,1,0:T(8,128)S(1)} %get-tuple-element.20), channel_id=1, source_target_pairs={{0,16},{16,32},{32,48},{48,64},{64,80},{80,96},{96,112},{112,128},... | collective-permute-start | bytes 3145736 | tf_op jit(solution)/shard_map/ppermute | solution.py:76
  50.9 9.6 %collective-permute-start.9 = (f32[4,7,8,256]{3,2,1,0:T(8,128)S(1)}, f32[4,7,8,256]{3,2,1,0:T(8,128)S(1)}, u32[]{:S(2)}, u32[]{:S(2)}) collective-permute-start(f32[4,7,8,256]{3,2,1,0:T(8,128)S(1)} %get-tuple-element.25), channel_id=1, source_target_pairs={{0,4},{1,5},{16,20},{17,21},{32,36},{33,37},{48,52},{49,53},{64,68... | collective-permute-start | bytes 688136 | tf_op jit(solution)/shard_map/ppermute | solution.py:71
  51.9 14.5 %collective-permute-start.10 = (f32[4,7,8,256]{3,2,1,0:T(8,128)S(1)}, f32[4,7,8,256]{3,2,1,0:T(8,128)S(1)}, u32[]{:S(2)}, u32[]{:S(2)}) collective-permute-start(f32[4,7,8,256]{3,2,1,0:T(8,128)S(1)} %get-tuple-element.26), channel_id=1, source_target_pairs={{0,8},{1,9},{16,24},{17,25},{32,40},{33,41},{48,56},{49,57},{64,72... | collective-permute-start | bytes 688136 | tf_op jit(solution)/shard_map/ppermute | solution.py:71
  55.8 10.5 %collective-permute-start.11 = (f32[4,7,8,256]{3,2,1,0:T(8,128)S(1)}, f32[4,7,8,256]{3,2,1,0:T(8,128)S(1)}, u32[]{:S(2)}, u32[]{:S(2)}) collective-permute-start(f32[4,7,8,256]{3,2,1,0:T(8,128)S(1)} %get-tuple-element.27), channel_id=1, source_target_pairs={{0,12},{1,13},{16,28},{17,29},{32,44},{33,45},{48,60},{49,61},{64,... | collective-permute-start | bytes 688136 | tf_op jit(solution)/shard_map/ppermute | solution.py:71
  66.9 9.3 %collective-permute-start.12 = (f32[1,7,8,256]{3,2,1,0:T(8,128)S(1)}, f32[1,7,8,256]{3,2,1,0:T(8,128)S(1)}, u32[]{:S(2)}, u32[]{:S(2)}) collective-permute-start(f32[1,7,8,256]{3,2,1,0:T(8,128)S(1)} %get-tuple-element.29), channel_id=1, source_target_pairs={{0,128},{1,129},{16,144},{17,145},{32,160},{33,161},{48,176},{49,1... | collective-permute-start | bytes 172040 | tf_op jit(solution)/shard_map/ppermute | solution.py:71
  67.0 14.0 %collective-permute-start.13 = (f32[1,7,8,256]{3,2,1,0:T(8,128)S(1)}, f32[1,7,8,256]{3,2,1,0:T(8,128)S(1)}, u32[]{:S(2)}, u32[]{:S(2)}) collective-permute-start(f32[1,7,8,256]{3,2,1,0:T(8,128)S(1)} %get-tuple-element.30), channel_id=1, source_target_pairs={{0,2},{1,3},{16,18},{17,19},{32,34},{33,35},{48,50},{49,51},{64,66... | collective-permute-start | bytes 172040 | tf_op jit(solution)/shard_map/ppermute | solution.py:71
  70.3 10.7 %collective-permute-start.14 = (f32[1,7,8,256]{3,2,1,0:T(8,128)S(1)}, f32[1,7,8,256]{3,2,1,0:T(8,128)S(1)}, u32[]{:S(2)}, u32[]{:S(2)}) collective-permute-start(f32[1,7,8,256]{3,2,1,0:T(8,128)S(1)} %get-tuple-element.31), channel_id=1, source_target_pairs={{0,130},{1,131},{16,146},{17,147},{32,162},{33,163},{48,178},{49,1... | collective-permute-start | bytes 172040 | tf_op jit(solution)/shard_map/ppermute | solution.py:71
  81.1 13.8 %collective-permute-start.15 = (f32[2,256,256]{2,1,0:T(8,128)S(1)}, f32[2,256,256]{2,1,0:T(8,128)S(1)}, u32[]{:S(2)}, u32[]{:S(2)}) collective-permute-start(f32[2,256,256]{2,1,0:T(8,128)S(1)} %add_corner.1), channel_id=1, source_target_pairs={{0,1},{1,2},{2,3},{3,4},{4,5},{5,6},{6,7},{7,8},{8,9},{9,10},{10,1... | collective-permute-start | bytes 1572872 | tf_op jit(solution)/shard_map/ppermute | solution.py:76
  81.8 3.6 %collective-permute-start.16 = (f32[1,7,8,256]{3,2,1,0:T(8,128)S(1)}, f32[1,7,8,256]{3,2,1,0:T(8,128)S(1)}, u32[]{:S(2)}, u32[]{:S(2)}) collective-permute-start(f32[1,7,8,256]{3,2,1,0:T(8,128)S(1)} %plain_sum.2.refs_0_), channel_id=1, source_target_pairs={{0,16},{1,17},{16,0},{17,1},{32,48},{33,49},{48,32},{49,33},{64,80... | collective-permute-start | bytes 172040 | tf_op jit(solution)/shard_map/ppermute | solution.py:71
  85.5 6.9 %collective-permute-start.19 = (f32[1,7,8,256]{3,2,1,0:T(8,128)S(1)}, f32[1,7,8,256]{3,2,1,0:T(8,128)S(1)}, u32[]{:S(2)}, u32[]{:S(2)}) collective-permute-start(f32[1,7,8,256]{3,2,1,0:T(8,128)S(1)} %plain_sum.3.refs_0_), channel_id=1, source_target_pairs={{0,96},{1,97},{16,112},{17,113},{32,0},{33,1},{48,16},{49,17},{64,... | collective-permute-start | bytes 172040 | tf_op jit(solution)/shard_map/ppermute | solution.py:71
  85.6 7.6 %collective-permute-start.18 = (f32[1,7,8,256]{3,2,1,0:T(8,128)S(1)}, f32[1,7,8,256]{3,2,1,0:T(8,128)S(1)}, u32[]{:S(2)}, u32[]{:S(2)}) collective-permute-start(f32[1,7,8,256]{3,2,1,0:T(8,128)S(1)} %plain_sum.3.refs_0_), channel_id=1, source_target_pairs={{0,64},{1,65},{16,80},{17,81},{32,96},{33,97},{48,112},{49,113},{6... | collective-permute-start | bytes 172040 | tf_op jit(solution)/shard_map/ppermute | solution.py:71
  85.7 9.2 %collective-permute-start.17 = (f32[1,7,8,256]{3,2,1,0:T(8,128)S(1)}, f32[1,7,8,256]{3,2,1,0:T(8,128)S(1)}, u32[]{:S(2)}, u32[]{:S(2)}) collective-permute-start(f32[1,7,8,256]{3,2,1,0:T(8,128)S(1)} %plain_sum.3.refs_0_), channel_id=1, source_target_pairs={{0,32},{1,33},{16,48},{17,49},{32,64},{33,65},{48,80},{49,81},{64,... | collective-permute-start | bytes 172040 | tf_op jit(solution)/shard_map/ppermute | solution.py:71
  115.2 5.3 %collective-permute-start.20 = (f32[16,6,8,256]{3,2,1,0:T(8,128)S(1)}, f32[16,6,8,256]{3,2,1,0:T(8,128)S(1)}, u32[]{:S(2)}, u32[]{:S(2)}) collective-permute-start(f32[16,6,8,256]{3,2,1,0:T(8,128)S(1)} %all_to_all.5.mine_ref), channel_id=1, source_target_pairs={{0,1},{1,0},{16,17},{17,16},{32,33},{33,32},{48,49},{49,48},{64,65... | collective-permute-start | bytes 2359304 | tf_op jit(solution)/shard_map/ppermute | solution.py:71
  (3 other events, 9.5 us)

commit v5 on v4

--- a/solution.py
+++ b/solution.py
@@ -141,6 +141,29 @@
 
 def rows(*parts):
     return jnp.concatenate(parts, axis=0)
+
+
+def cut_parts(value):
+    def body(value_ref, real, imag, sems):
+        copies = [
+            pltpu.make_async_copy(value_ref.at[pl.ds(part, 1)], out, sems.at[part])
+            for part, out in enumerate((real, imag))
+        ]
+        for copy in copies:
+            copy.start()
+        for copy in copies:
+            copy.wait()
+
+    part = jax.ShapeDtypeStruct((1,) + value.shape[1:], value.dtype)
+    return pl.pallas_call(
+        body,
+        out_shape=(part, part),
+        in_specs=[pl.BlockSpec(memory_space=pl.ANY)],
+        out_specs=(pl.BlockSpec(memory_space=pl.ANY),) * 2,
+        scratch_shapes=[pltpu.SemaphoreType.DMA((2,))],
+        compiler_params=pltpu.CompilerParams(vmem_limit_bytes=SMALL),
+        name="cut_parts",
+    )(value)
 
 
 def sort_kernel(amplitude, order, amp_out, measured, sems):
@@ -234,9 +257,9 @@
 
 
 def pattern_kernel(
-    place, counts, points, own, right_real, right_imag, lower, corner_real, corner_imag, probe_in, amplitude_in, table_in, weight, old_rows,
+    place, counts, points, own, right_real, right_imag, lower, corner_real, corner_imag, probe, amplitude, table, weight, old_rows,
     core_out, right_out, lower_out, send_out, keep_out,
-    field, target, total, spectrum, probe, amplitude, table, sems,
+    field, target, total, spectrum, sems,
 ):
     row_id = place[0]
     col_id = place[1]
@@ -255,8 +278,6 @@
                     sems.at[len(loads)],
                 )
             )
-    for source, dest in ((probe_in, probe), (table_in, table), (amplitude_in, amplitude)):
-        loads.append(pltpu.make_async_copy(source, dest, sems.at[len(loads)]))
     for load in loads:
         load.start()
     target[...] = jnp.zeros_like(target)
@@ -416,17 +437,17 @@
     return pl.pallas_call(
         pattern_kernel,
         out_shape=(tile, tall, tile, part, part),
-        in_specs=[pl.BlockSpec(memory_space=SMEM)] * 3 + [pl.BlockSpec(memory_space=pl.ANY)] * 11,
+        in_specs=[pl.BlockSpec(memory_space=SMEM)] * 3
+        + [pl.BlockSpec(memory_space=pl.ANY)] * 6
+        + [pl.BlockSpec(memory_space=VMEM)] * 3
+        + [pl.BlockSpec(memory_space=pl.ANY)] * 2,
         out_specs=(pl.BlockSpec(memory_space=pl.ANY),) * 5,
         scratch_shapes=[
             VMEM((2, 4, 2 * SIDE, HALF), F32),
             VMEM((2, 4, 2 * SIDE, HALF), F32),
             VMEM((32, PLANES, 8, SIDE), F32),
             VMEM((MODES, 2, SIDE, SIDE), F32),
-            VMEM(probe.shape, F32),
-            VMEM(amplitude.shape, F32),
-            VMEM(table.shape, BF16),
-            pltpu.SemaphoreType.DMA((15,)),
+            pltpu.SemaphoreType.DMA((12,)),
         ],
         compiler_params=pltpu.CompilerParams(vmem_limit_bytes=LARGE),
         cost_estimate=pl.CostEstimate(flops=10_000_000_000, bytes_accessed=10_000_000, transcendentals=0),
@@ -576,7 +597,7 @@
     order = jnp.asarray(order_table())
 
     points = positions[0, 0]
-    right_strip = [shifted(object_field[part : part + 1], "gx", -1) for part in range(2)]
+    right_strip = [shifted(part, "gx", -1) for part in cut_parts(object_field)]
     lower_strip = shifted(object_field, "gy", -1)
     points_left = shifted(points, "gx", 1)
     amplitude = sort_amplitude(amplitudes[0, 0], order)

time: 122 us -> 124 us (1.016)
  waiting for transfers between devices: 35.5 us -> 42.6 us
  Pallas kernels: 22.9 us -> 19 us
  blocking collectives: 20.2 us -> 16.6 us
  starting transfers between devices: 38.8 us -> 40.7 us
    ppermute x9, waiting for transfers between devices: 1.77 us -> 9.36 us  [shifted(): lax.ppermute(value, axis, [(source, (source + steps) % count) for source...]
    ppermute x12, starting transfers between devices: 15.7 us -> 19.9 us  [send(): return lax.ppermute(value, AXES, pairs)]
    pallas_call x1, Pallas kernels: 15.9 us -> 12.2 us  [visit_patterns(): pl.pallas_call(pattern_kernel, out_shape=(tile, tall, tile, part, part),...]
    all_to_all x1, blocking collectives: 20.2 us -> 16.6 us  [swap_in_plane(): lax.all_to_all(value, AXES, split_axis=0, concat_axis=0, tiled=True, axis...]
    ppermute x9, starting transfers between devices: 23.2 us -> 20.8 us  [shifted(): lax.ppermute(value, axis, [(source, (source + steps) % count) for source...]
    unnamed x12 -> x14, local copies, waits for them, and re-layouts: 2.15 us -> 3.19 us
  transfers between devices with their start and end apart: 21 -> 21, of which waited for: 11 -> 13; matrix products, arithmetic and copies ran while one was open for 1% -> 0% of each run, Pallas kernels for 4% -> 4%
where the time goes in v5:
time: 124 us
  waiting for transfers between devices  42.6 us (34%)
  starting transfers between devices  40.7 us (33%)
  Pallas kernels  19 us (15%)
  blocking collectives  16.6 us (13%)
  local copies, waits for them, and re-layouts  4.04 us (3%)
    ppermute x12, waiting for transfers between devices, send(): return lax.ppermute(value, AXES, pairs)  33.2 us
    ppermute x9, starting transfers between devices, shifted(): lax.ppermute(value, axis, [(source, (source + steps) % count) for source...  20.8 us
    ppermute x12, starting transfers between devices, send(): return lax.ppermute(value, AXES, pairs)  19.9 us
    all_to_all x1, blocking collectives, swap_in_plane(): lax.all_to_all(value, AXES, split_axis=0, concat_axis=0, tiled=True, axis...  16.6 us
    pallas_call x1, Pallas kernels, visit_patterns(): pl.pallas_call(pattern_kernel, out_shape=(tile, tall, tile, part, part),...  12.2 us
    ppermute x9, waiting for transfers between devices, shifted(): lax.ppermute(value, axis, [(source, (source + steps) % count) for source...  9.36 us
    unnamed x14, local copies, waits for them, and re-layouts  3.19 us
  transfers between devices with their start and end apart: 21, of which 13 were waited for; matrix products, arithmetic and copies ran while one was open for 0% of the time, Pallas kernels for 4%

profile of v5, /device:TPU:1, one launch (start us, length us, event | category | flops | bytes accessed | tf_op | source)
XLA Modules:
  0.0 123.8 jit_solution(16619105716259835407)
XLA Ops:
  1.4 2.5 %collective-permute-start.1 = (s32[4,2]{1,0:T(4,128)S(1)}, s32[4,2]{1,0:T(4,128)S(1)}, u32[]{:S(2)}, u32[]{:S(2)}) collective-permute-start(s32[4,2]{1,0:T(4,128)S(1)} %copy.22.own.points), channel_id=1, source_target_pairs={{0,16},{16,32},{32,48},{48,64},{64,80},{80,96},{96,112},{112,128},... | collective-permute-start | bytes 104 | tf_op jit(solution)/shard_map/ppermute | solution.py:76
  5.9 4.8 %collective-permute-start = (f32[1,256,256]{2,1,0:T(8,128)S(1)}, f32[1,256,256]{2,1,0:T(8,128)S(1)}, u32[]{:S(2)}, u32[]{:S(2)}) collective-permute-start(f32[1,256,256]{2,1,0:T(8,128)S(1)} %get-tuple-element.19), channel_id=1, source_target_pairs={{0,240},{16,0},{32,16},{48,32},{64,48},{80,64},{96,80},{112,96},{1... | collective-permute-start | bytes 786440 | tf_op jit(solution)/shard_map/ppermute | solution.py:76
  15.4 3.6 %collective-permute-start.2 = (s32[8,2]{1,0:T(8,128)S(1)}, s32[8,2]{1,0:T(8,128)S(1)}, u32[]{:S(2)}, u32[]{:S(2)}) collective-permute-start(s32[8,2]{1,0:T(8,128)S(1)} %pad_add_fusion), channel_id=1, source_target_pairs={{0,1},{1,2},{2,3},{3,4},{4,5},{5,6},{6,7},{7,8},{8,9},{9,10},{10,1... | collective-permute-start | bytes 200 | tf_op jit(solution)/shard_map/ppermute | solution.py:76
  18.9 4.0 %collective-permute-done.3.right_imag = f32[1,256,256]{2,1,0:T(8,128)S(1)} collective-permute-done((f32[1,256,256]{2,1,0:T(8,128)S(1)}, f32[1,256,256]{2,1,0:T(8,128)S(1)}, u32[]{:S(2)}, u32[]{:S(2)}) %collective-permute-start.3) | collective-permute-done | bytes 262176 | tf_op jit(solution)/shard_map/ppermute | solution.py:76
  22.9 4.8 %collective-permute-start.6 = (f32[1,256,256]{2,1,0:T(8,128)S(1)}, f32[1,256,256]{2,1,0:T(8,128)S(1)}, u32[]{:S(2)}, u32[]{:S(2)}) collective-permute-start(f32[1,256,256]{2,1,0:T(8,128)S(1)} %collective-permute-done.3.right_imag), channel_id=1, source_target_pairs={{0,15},{1,0},{2,1},{3,2},{4,3},{5,4},{6,5},{7,6},{8,7},{9,8},{10,9... | collective-permute-start | bytes 786440 | tf_op jit(solution)/shard_map/ppermute | solution.py:76
  27.9 1.9 %cover.1 = (f32[256,256]{1,0:T(8,128)S(1)}, f32[1,6,8,256]{3,2,1,0:T(8,128)S(1)}) custom-call(s32[5]{0:T(128)S(1)} %stack.23.refs_3_.place, s32[16,16]{1,0:T(8,128)S(1)} %copy-done.4, s32[4,2]{1,0:T(4,128)S(1)} %copy.22.own.points, s32[4,2]{1,0:T(4,128)S(1)} %collective-permute-done.1.left, s32[8,2]{1,0:T(8,128)S(1)} %collective-permute-done.2.refs_2_.above, ...), custom_call_target="tpu_custom_call" | custom-call | flops 2000000000 | bytes 4000000 | tf_op jit(solution)/shard_map/cover/pallas_call | solution.py:244
  30.2 4.9 %collective-permute-done.5.corner_real = f32[1,256,256]{2,1,0:T(8,128)S(1)} collective-permute-done((f32[1,256,256]{2,1,0:T(8,128)S(1)}, f32[1,256,256]{2,1,0:T(8,128)S(1)}, u32[]{:S(2)}, u32[]{:S(2)}) %collective-permute-start.5) | collective-permute-done | bytes 262176 | tf_op jit(solution)/shard_map/ppermute | solution.py:76
  35.2 12.2 %patterns.1 = (f32[2,256,256]{2,1,0:T(8,128)S(1)}, f32[2,512,256]{2,1,0:T(8,128)S(1)}, f32[2,256,256]{2,1,0:T(8,128)S(1)}, f32[16,7,8,256]{3,2,1,0:T(8,128)S(1)}, f32[16,7,8,256]{3,2,1,0:T(8,128)S(1)}) custom-call(s32[5]{0:T(128)S(1)} %stack.23.refs_3_.place, s32[16,16]{1,0:T(8,128)S(1)} %copy-done.4, s32[4,2]{1,0:T(4,128)S(1)} %copy.22.own.points, ...), custom_call_target="tpu_custom_call" | custom-call | flops 10000000000 | bytes 10000000 | tf_op jit(solution)/shard_map/patterns/pallas_call | solution.py:437
  47.6 2.4 %collective-permute-done.8.refs_1_ = f32[16,7,8,256]{3,2,1,0:T(8,128)S(1)} collective-permute-done((f32[16,7,8,256]{3,2,1,0:T(8,128)S(1)}, f32[16,7,8,256]{3,2,1,0:T(8,128)S(1)}, u32[]{:S(2)}, u32[]{:S(2)}) %collective-permute-start.8) | collective-permute-done | bytes 917536 | tf_op jit(solution)/shard_map/ppermute | solution.py:71
  50.6 4.9 %collective-permute-start.9 = (f32[4,7,8,256]{3,2,1,0:T(8,128)S(1)}, f32[4,7,8,256]{3,2,1,0:T(8,128)S(1)}, u32[]{:S(2)}, u32[]{:S(2)}) collective-permute-start(f32[4,7,8,256]{3,2,1,0:T(8,128)S(1)} %get-tuple-element.29), channel_id=1, source_target_pairs={{0,4},{1,5},{16,20},{17,21},{32,36},{33,37},{48,52},{49,53},{64,68... | collective-permute-start | bytes 688136 | tf_op jit(solution)/shard_map/ppermute | solution.py:71
  56.1 2.0 %collective-permute-start.11 = (f32[4,7,8,256]{3,2,1,0:T(8,128)S(1)}, f32[4,7,8,256]{3,2,1,0:T(8,128)S(1)}, u32[]{:S(2)}, u32[]{:S(2)}) collective-permute-start(f32[4,7,8,256]{3,2,1,0:T(8,128)S(1)} %get-tuple-element.31), channel_id=1, source_target_pairs={{0,12},{1,13},{16,28},{17,29},{32,44},{33,45},{48,60},{49,61},{64,... | collective-permute-start | bytes 688136 | tf_op jit(solution)/shard_map/ppermute | solution.py:71
  58.1 2.3 %collective-permute-done.9.refs_1_ = f32[4,7,8,256]{3,2,1,0:T(8,128)S(1)} collective-permute-done((f32[4,7,8,256]{3,2,1,0:T(8,128)S(1)}, f32[4,7,8,256]{3,2,1,0:T(8,128)S(1)}, u32[]{:S(2)}, u32[]{:S(2)}) %collective-permute-start.9) | collective-permute-done | bytes 229408 | tf_op jit(solution)/shard_map/ppermute | solution.py:71
  60.4 6.2 %collective-permute-done.10.refs_2_ = f32[4,7,8,256]{3,2,1,0:T(8,128)S(1)} collective-permute-done((f32[4,7,8,256]{3,2,1,0:T(8,128)S(1)}, f32[4,7,8,256]{3,2,1,0:T(8,128)S(1)}, u32[]{:S(2)}, u32[]{:S(2)}) %collective-permute-start.10) | collective-permute-done | bytes 229408 | tf_op jit(solution)/shard_map/ppermute | solution.py:71
  68.7 4.2 %collective-permute-start.13 = (f32[1,7,8,256]{3,2,1,0:T(8,128)S(1)}, f32[1,7,8,256]{3,2,1,0:T(8,128)S(1)}, u32[]{:S(2)}, u32[]{:S(2)}) collective-permute-start(f32[1,7,8,256]{3,2,1,0:T(8,128)S(1)} %get-tuple-element.34), channel_id=1, source_target_pairs={{0,2},{1,3},{16,18},{17,19},{32,34},{33,35},{48,50},{49,51},{64,66... | collective-permute-start | bytes 172040 | tf_op jit(solution)/shard_map/ppermute | solution.py:71
  74.2 4.2 %collective-permute-done.12.refs_1_ = f32[1,7,8,256]{3,2,1,0:T(8,128)S(1)} collective-permute-done((f32[1,7,8,256]{3,2,1,0:T(8,128)S(1)}, f32[1,7,8,256]{3,2,1,0:T(8,128)S(1)}, u32[]{:S(2)}, u32[]{:S(2)}) %collective-permute-start.12) | collective-permute-done | bytes 57376 | tf_op jit(solution)/shard_map/ppermute | solution.py:71
  78.4 5.0 %collective-permute-done.13.refs_2_ = f32[1,7,8,256]{3,2,1,0:T(8,128)S(1)} collective-permute-done((f32[1,7,8,256]{3,2,1,0:T(8,128)S(1)}, f32[1,7,8,256]{3,2,1,0:T(8,128)S(1)}, u32[]{:S(2)}, u32[]{:S(2)}) %collective-permute-start.13) | collective-permute-done | bytes 57376 | tf_op jit(solution)/shard_map/ppermute | solution.py:71
  83.5 2.3 %collective-permute-start.15 = (f32[2,256,256]{2,1,0:T(8,128)S(1)}, f32[2,256,256]{2,1,0:T(8,128)S(1)}, u32[]{:S(2)}, u32[]{:S(2)}) collective-permute-start(f32[2,256,256]{2,1,0:T(8,128)S(1)} %add_corner.1), channel_id=1, source_target_pairs={{0,1},{1,2},{2,3},{3,4},{4,5},{5,6},{6,7},{7,8},{8,9},{9,10},{10,1... | collective-permute-start | bytes 1572872 | tf_op jit(solution)/shard_map/ppermute | solution.py:76
  85.9 3.0 %collective-permute-done.16.refs_1_ = f32[1,7,8,256]{3,2,1,0:T(8,128)S(1)} collective-permute-done((f32[1,7,8,256]{3,2,1,0:T(8,128)S(1)}, f32[1,7,8,256]{3,2,1,0:T(8,128)S(1)}, u32[]{:S(2)}, u32[]{:S(2)}) %collective-permute-start.16) | collective-permute-done | bytes 57376 | tf_op jit(solution)/shard_map/ppermute | solution.py:71
  89.1 2.3 %collective-permute-start.17 = (f32[1,7,8,256]{3,2,1,0:T(8,128)S(1)}, f32[1,7,8,256]{3,2,1,0:T(8,128)S(1)}, u32[]{:S(2)}, u32[]{:S(2)}) collective-permute-start(f32[1,7,8,256]{3,2,1,0:T(8,128)S(1)} %plain_sum.3.refs_0_), channel_id=1, source_target_pairs={{0,32},{1,33},{16,48},{17,49},{32,64},{33,65},{48,80},{49,81},{64,... | collective-permute-start | bytes 172040 | tf_op jit(solution)/shard_map/ppermute | solution.py:71
  91.4 4.3 %collective-permute-done.19.refs_3_ = f32[1,7,8,256]{3,2,1,0:T(8,128)S(1)} collective-permute-done((f32[1,7,8,256]{3,2,1,0:T(8,128)S(1)}, f32[1,7,8,256]{3,2,1,0:T(8,128)S(1)}, u32[]{:S(2)}, u32[]{:S(2)}) %collective-permute-start.19) | collective-permute-done | bytes 57376 | tf_op jit(solution)/shard_map/ppermute | solution.py:71
  97.3 3.1 %collective-permute-done.17.refs_1_ = f32[1,7,8,256]{3,2,1,0:T(8,128)S(1)} collective-permute-done((f32[1,7,8,256]{3,2,1,0:T(8,128)S(1)}, f32[1,7,8,256]{3,2,1,0:T(8,128)S(1)}, u32[]{:S(2)}, u32[]{:S(2)}) %collective-permute-start.17) | collective-permute-done | bytes 57376 | tf_op jit(solution)/shard_map/ppermute | solution.py:71
  100.5 16.6 %all_to_all.5.mine_ref = f32[16,6,8,256]{3,2,1,0:T(8,128)S(1)} all-to-all(f32[16,6,8,256]{3,2,1,0:T(8,128)S(1)} %update_probe.1), channel_id=1, replica_groups={{0,128,2,130,4,132,6,134,8,136,10,138,12,140,14,142},{1,129,3,131,5,133..., dimensions={0} | all-to-all | bytes 1572864 | tf_op jit(solution)/shard_map/all_to_all | solution.py:67
  117.1 2.9 %collective-permute-start.20 = (f32[16,6,8,256]{3,2,1,0:T(8,128)S(1)}, f32[16,6,8,256]{3,2,1,0:T(8,128)S(1)}, u32[]{:S(2)}, u32[]{:S(2)}) collective-permute-start(f32[16,6,8,256]{3,2,1,0:T(8,128)S(1)} %all_to_all.5.mine_ref), channel_id=1, source_target_pairs={{0,1},{1,0},{16,17},{17,16},{32,33},{33,32},{48,49},{49,48},{64,65... | collective-permute-start | bytes 2359304 | tf_op jit(solution)/shard_map/ppermute | solution.py:71
  121.9 1.8 %join_halves.1 = f32[6,32,8,256]{3,2,1,0:T(8,128)} custom-call(s32[5]{0:T(128)S(1)} %stack.23.refs_3_.place, f32[16,6,8,256]{3,2,1,0:T(8,128)S(1)} %all_to_all.5.mine_ref, f32[16,6,8,256]{3,2,1,0:T(8,128)S(1)} %collective-permute-done.20.other_ref), custom_call_target="tpu_custom_call" | custom-call | tf_op jit(solution)/shard_map/join_halves/pallas_call | solution.py:541
  (49 shorter events, 16.8 us)
Async XLA Ops:
  1.4 14.0 %collective-permute-start.1 = (s32[4,2]{1,0:T(4,128)S(1)}, s32[4,2]{1,0:T(4,128)S(1)}, u32[]{:S(2)}, u32[]{:S(2)}) collective-permute-start(s32[4,2]{1,0:T(4,128)S(1)} %copy.22.own.points), channel_id=1, source_target_pairs={{0,16},{16,32},{32,48},{48,64},{64,80},{80,96},{96,112},{112,128},... | collective-permute-start | bytes 104 | tf_op jit(solution)/shard_map/ppermute | solution.py:76
  3.9 26.4 %collective-permute-start.4 = (f32[2,256,256]{2,1,0:T(8,128)}, f32[2,256,256]{2,1,0:T(8,128)S(1)}, u32[]{:S(2)}, u32[]{:S(2)}) collective-permute-start(f32[2,256,256]{2,1,0:T(8,128)} %own_ref.1), channel_id=1, source_target_pairs={{0,15},{1,0},{2,1},{3,2},{4,3},{5,4},{6,5},{7,6},{8,7},{9,8},{10,9... | collective-permute-start | bytes 1572872 | tf_op jit(solution)/shard_map/ppermute | solution.py:76
  5.9 21.8 %collective-permute-start = (f32[1,256,256]{2,1,0:T(8,128)S(1)}, f32[1,256,256]{2,1,0:T(8,128)S(1)}, u32[]{:S(2)}, u32[]{:S(2)}) collective-permute-start(f32[1,256,256]{2,1,0:T(8,128)S(1)} %get-tuple-element.19), channel_id=1, source_target_pairs={{0,240},{16,0},{32,16},{48,32},{64,48},{80,64},{96,80},{112,96},{1... | collective-permute-start | bytes 786440 | tf_op jit(solution)/shard_map/ppermute | solution.py:76
  10.7 12.2 %collective-permute-start.3 = (f32[1,256,256]{2,1,0:T(8,128)S(1)}, f32[1,256,256]{2,1,0:T(8,128)S(1)}, u32[]{:S(2)}, u32[]{:S(2)}) collective-permute-start(f32[1,256,256]{2,1,0:T(8,128)S(1)} %get-tuple-element.20), channel_id=1, source_target_pairs={{0,240},{16,0},{32,16},{48,32},{64,48},{80,64},{96,80},{112,96},{1... | collective-permute-start | bytes 786440 | tf_op jit(solution)/shard_map/ppermute | solution.py:76
  15.3 12.6 %copy-start.2 = (f32[3,2,256,256]{3,2,1,0:T(8,128)S(1)}, f32[3,2,256,256]{3,2,1,0:T(8,128)}, u32[]{:S(2)}) copy-start(f32[3,2,256,256]{3,2,1,0:T(8,128)} %probe.3) | copy-start | bytes 4718596
  15.3 12.6 %copy-start.4 = (s32[16,16]{1,0:T(8,128)S(1)}, s32[16,16]{1,0:T(8,128)}, u32[]{:S(2)}) copy-start(s32[16,16]{1,0:T(8,128)} %counts.3) | copy-start | bytes 3076
  15.4 12.4 %collective-permute-start.2 = (s32[8,2]{1,0:T(8,128)S(1)}, s32[8,2]{1,0:T(8,128)S(1)}, u32[]{:S(2)}, u32[]{:S(2)}) collective-permute-start(s32[8,2]{1,0:T(8,128)S(1)} %pad_add_fusion), channel_id=1, source_target_pairs={{0,1},{1,2},{2,3},{3,4},{4,5},{5,6},{6,7},{7,8},{8,9},{9,10},{10,1... | collective-permute-start | bytes 200 | tf_op jit(solution)/shard_map/ppermute | solution.py:76
  22.9 7.3 %collective-permute-start.6 = (f32[1,256,256]{2,1,0:T(8,128)S(1)}, f32[1,256,256]{2,1,0:T(8,128)S(1)}, u32[]{:S(2)}, u32[]{:S(2)}) collective-permute-start(f32[1,256,256]{2,1,0:T(8,128)S(1)} %collective-permute-done.3.right_imag), channel_id=1, source_target_pairs={{0,15},{1,0},{2,1},{3,2},{4,3},{5,4},{6,5},{7,6},{8,7},{9,8},{10,9... | collective-permute-start | bytes 786440 | tf_op jit(solution)/shard_map/ppermute | solution.py:76
  27.8 7.4 %copy-start.1 = (f32[2,256,256]{2,1,0:T(8,128)S(1)}, f32[2,256,256]{2,1,0:T(8,128)}, u32[]{:S(2)}) copy-start(f32[2,256,256]{2,1,0:T(8,128)} %own_ref.1) | copy-start | bytes 1572868
  27.8 7.4 %collective-permute-start.5 = (f32[1,256,256]{2,1,0:T(8,128)S(1)}, f32[1,256,256]{2,1,0:T(8,128)S(1)}, u32[]{:S(2)}, u32[]{:S(2)}) collective-permute-start(f32[1,256,256]{2,1,0:T(8,128)S(1)} %after.1.right_real), channel_id=1, source_target_pairs={{0,15},{1,0},{2,1},{3,2},{4,3},{5,4},{6,5},{7,6},{8,7},{9,8},{10,9... | collective-permute-start | bytes 786440 | tf_op jit(solution)/shard_map/ppermute | solution.py:76
  47.4 2.6 %collective-permute-start.8 = (f32[16,7,8,256]{3,2,1,0:T(8,128)S(1)}, f32[16,7,8,256]{3,2,1,0:T(8,128)S(1)}, u32[]{:S(2)}, u32[]{:S(2)}) collective-permute-start(f32[16,7,8,256]{3,2,1,0:T(8,128)S(1)} %get-tuple-element.27), channel_id=1, source_target_pairs={{0,1},{1,0},{16,17},{17,16},{32,33},{33,32},{48,49},{49,48},{64,65... | collective-permute-start | bytes 2752520 | tf_op jit(solution)/shard_map/ppermute | solution.py:71
  47.5 36.0 %collective-permute-start.7 = (f32[2,512,256]{2,1,0:T(8,128)S(1)}, f32[2,512,256]{2,1,0:T(8,128)S(1)}, u32[]{:S(2)}, u32[]{:S(2)}) collective-permute-start(f32[2,512,256]{2,1,0:T(8,128)S(1)} %get-tuple-element.24), channel_id=1, source_target_pairs={{0,16},{16,32},{32,48},{48,64},{64,80},{80,96},{96,112},{112,128},... | collective-permute-start | bytes 3145736 | tf_op jit(solution)/shard_map/ppermute | solution.py:76
  50.6 9.8 %collective-permute-start.9 = (f32[4,7,8,256]{3,2,1,0:T(8,128)S(1)}, f32[4,7,8,256]{3,2,1,0:T(8,128)S(1)}, u32[]{:S(2)}, u32[]{:S(2)}) collective-permute-start(f32[4,7,8,256]{3,2,1,0:T(8,128)S(1)} %get-tuple-element.29), channel_id=1, source_target_pairs={{0,4},{1,5},{16,20},{17,21},{32,36},{33,37},{48,52},{49,53},{64,68... | collective-permute-start | bytes 688136 | tf_op jit(solution)/shard_map/ppermute | solution.py:71
  55.5 11.1 %collective-permute-start.10 = (f32[4,7,8,256]{3,2,1,0:T(8,128)S(1)}, f32[4,7,8,256]{3,2,1,0:T(8,128)S(1)}, u32[]{:S(2)}, u32[]{:S(2)}) collective-permute-start(f32[4,7,8,256]{3,2,1,0:T(8,128)S(1)} %get-tuple-element.30), channel_id=1, source_target_pairs={{0,8},{1,9},{16,24},{17,25},{32,40},{33,41},{48,56},{49,57},{64,72... | collective-permute-start | bytes 688136 | tf_op jit(solution)/shard_map/ppermute | solution.py:71
  56.1 10.5 %collective-permute-start.11 = (f32[4,7,8,256]{3,2,1,0:T(8,128)S(1)}, f32[4,7,8,256]{3,2,1,0:T(8,128)S(1)}, u32[]{:S(2)}, u32[]{:S(2)}) collective-permute-start(f32[4,7,8,256]{3,2,1,0:T(8,128)S(1)} %get-tuple-element.31), channel_id=1, source_target_pairs={{0,12},{1,13},{16,28},{17,29},{32,44},{33,45},{48,60},{49,61},{64,... | collective-permute-start | bytes 688136 | tf_op jit(solution)/shard_map/ppermute | solution.py:71
  67.2 11.2 %collective-permute-start.12 = (f32[1,7,8,256]{3,2,1,0:T(8,128)S(1)}, f32[1,7,8,256]{3,2,1,0:T(8,128)S(1)}, u32[]{:S(2)}, u32[]{:S(2)}) collective-permute-start(f32[1,7,8,256]{3,2,1,0:T(8,128)S(1)} %get-tuple-element.33), channel_id=1, source_target_pairs={{0,128},{1,129},{16,144},{17,145},{32,160},{33,161},{48,176},{49,1... | collective-permute-start | bytes 172040 | tf_op jit(solution)/shard_map/ppermute | solution.py:71
  68.7 14.8 %collective-permute-start.13 = (f32[1,7,8,256]{3,2,1,0:T(8,128)S(1)}, f32[1,7,8,256]{3,2,1,0:T(8,128)S(1)}, u32[]{:S(2)}, u32[]{:S(2)}) collective-permute-start(f32[1,7,8,256]{3,2,1,0:T(8,128)S(1)} %get-tuple-element.34), channel_id=1, source_target_pairs={{0,2},{1,3},{16,18},{17,19},{32,34},{33,35},{48,50},{49,51},{64,66... | collective-permute-start | bytes 172040 | tf_op jit(solution)/shard_map/ppermute | solution.py:71
  72.9 10.5 %collective-permute-start.14 = (f32[1,7,8,256]{3,2,1,0:T(8,128)S(1)}, f32[1,7,8,256]{3,2,1,0:T(8,128)S(1)}, u32[]{:S(2)}, u32[]{:S(2)}) collective-permute-start(f32[1,7,8,256]{3,2,1,0:T(8,128)S(1)} %get-tuple-element.35), channel_id=1, source_target_pairs={{0,130},{1,131},{16,146},{17,147},{32,162},{33,163},{48,178},{49,1... | collective-permute-start | bytes 172040 | tf_op jit(solution)/shard_map/ppermute | solution.py:71
  83.5 16.9 %collective-permute-start.15 = (f32[2,256,256]{2,1,0:T(8,128)S(1)}, f32[2,256,256]{2,1,0:T(8,128)S(1)}, u32[]{:S(2)}, u32[]{:S(2)}) collective-permute-start(f32[2,256,256]{2,1,0:T(8,128)S(1)} %add_corner.1), channel_id=1, source_target_pairs={{0,1},{1,2},{2,3},{3,4},{4,5},{5,6},{6,7},{7,8},{8,9},{9,10},{10,1... | collective-permute-start | bytes 1572872 | tf_op jit(solution)/shard_map/ppermute | solution.py:76
  85.9 3.0 %collective-permute-start.16 = (f32[1,7,8,256]{3,2,1,0:T(8,128)S(1)}, f32[1,7,8,256]{3,2,1,0:T(8,128)S(1)}, u32[]{:S(2)}, u32[]{:S(2)}) collective-permute-start(f32[1,7,8,256]{3,2,1,0:T(8,128)S(1)} %plain_sum.2.refs_0_), channel_id=1, source_target_pairs={{0,16},{1,17},{16,0},{17,1},{32,48},{33,49},{48,32},{49,33},{64,80... | collective-permute-start | bytes 172040 | tf_op jit(solution)/shard_map/ppermute | solution.py:71
  88.9 6.8 %collective-permute-start.19 = (f32[1,7,8,256]{3,2,1,0:T(8,128)S(1)}, f32[1,7,8,256]{3,2,1,0:T(8,128)S(1)}, u32[]{:S(2)}, u32[]{:S(2)}) collective-permute-start(f32[1,7,8,256]{3,2,1,0:T(8,128)S(1)} %plain_sum.3.refs_0_), channel_id=1, source_target_pairs={{0,96},{1,97},{16,112},{17,113},{32,0},{33,1},{48,16},{49,17},{64,... | collective-permute-start | bytes 172040 | tf_op jit(solution)/shard_map/ppermute | solution.py:71
  89.0 8.3 %collective-permute-start.18 = (f32[1,7,8,256]{3,2,1,0:T(8,128)S(1)}, f32[1,7,8,256]{3,2,1,0:T(8,128)S(1)}, u32[]{:S(2)}, u32[]{:S(2)}) collective-permute-start(f32[1,7,8,256]{3,2,1,0:T(8,128)S(1)} %plain_sum.3.refs_0_), channel_id=1, source_target_pairs={{0,64},{1,65},{16,80},{17,81},{32,96},{33,97},{48,112},{49,113},{6... | collective-permute-start | bytes 172040 | tf_op jit(solution)/shard_map/ppermute | solution.py:71
  89.1 11.3 %collective-permute-start.17 = (f32[1,7,8,256]{3,2,1,0:T(8,128)S(1)}, f32[1,7,8,256]{3,2,1,0:T(8,128)S(1)}, u32[]{:S(2)}, u32[]{:S(2)}) collective-permute-start(f32[1,7,8,256]{3,2,1,0:T(8,128)S(1)} %plain_sum.3.refs_0_), channel_id=1, source_target_pairs={{0,32},{1,33},{16,48},{17,49},{32,64},{33,65},{48,80},{49,81},{64,... | collective-permute-start | bytes 172040 | tf_op jit(solution)/shard_map/ppermute | solution.py:71
  117.1 4.8 %collective-permute-start.20 = (f32[16,6,8,256]{3,2,1,0:T(8,128)S(1)}, f32[16,6,8,256]{3,2,1,0:T(8,128)S(1)}, u32[]{:S(2)}, u32[]{:S(2)}) collective-permute-start(f32[16,6,8,256]{3,2,1,0:T(8,128)S(1)} %all_to_all.5.mine_ref), channel_id=1, source_target_pairs={{0,1},{1,0},{16,17},{17,16},{32,33},{33,32},{48,49},{49,48},{64,65... | collective-permute-start | bytes 2359304 | tf_op jit(solution)/shard_map/ppermute | solution.py:71
  (4 other events, 10.6 us)
